TPU v7x, 256 devices: a whole 4x4x8 slice. The times are simulated.
256 devices in a mesh: dp: 8 (over x, y_lo), space: 32 (over y_hi, z, core).
Axes of the slice: x: 4, y: 4 (y_hi: 2, y_lo: 2; y = y_hi * 2 + y_lo), z: 8, core: 2. Of those that a mesh axis runs over, the one named last changes fastest.
Arguments:
- volumes: bfloat16 [128, 4, 128, 4, 512], P('dp', None, 'space'), may hold values from -6 to 6
- targets: float32 [128, 4], P('dp'), may hold values from -6 to 6
- counts: int32 [32], replicated, may hold values from 0 to 2, as said below
- w_conv1: bfloat16 [3, 3, 3, 32, 4], replicated, may hold values from -0.625 to 0.625
- w_conv2: bfloat16 [3, 3, 3, 64, 32], replicated, may hold values from -0.21875 to 0.21875
- w_dense1: bfloat16 [2048, 128], replicated, may hold values from -1.5 to 1.5
- w_dense2: bfloat16 [128, 64], replicated, may hold values from -0.5 to 0.5
- w_dense3: bfloat16 [64, 4], replicated, may hold values from -0.75 to 0.75
Outputs:
- loss: float32 [], replicated
- grad_w1: float32 [3, 3, 3, 32, 4], replicated
- grad_w2: float32 [3, 3, 3, 64, 32], replicated
- grad_d1: float32 [2048, 128], replicated
- grad_d2: float32 [128, 64], replicated
- grad_d3: float32 [64, 4], replicated
Inputs may be any that keep to these rules, and one draw needn't show every extreme that they name: The counts sum to 16; a group may hold no sample, and the largest holds exactly 2.
All inputs are finite; a program needn't handle non-finite values.
Results may differ from a plain program's by a relative error of at most 0.018.
Values may be sent and summed in bfloat16 or wider, within the bound.
No kernel may reach another device: no remote copies, remote signals or barrier semaphores. Data moves between devices by JAX's collectives and lax.ppermute only.
A program may use at most 128 MiB of HBM per device.

v0:
```python
import jax
import jax.numpy as jnp
from jax import lax
from jax.sharding import PartitionSpec as P

MOST = 2


def from_behind(shard, axis, by):
    devices = lax.axis_size(axis)
    pairs = [(i, i + by) for i in range(devices) if 0 <= i + by < devices]
    return lax.ppermute(shard, axis, pairs)


def leaky_relu(values):
    return values * (0.65 + 0.35 * jnp.tanh(values))


def slope_of(values):
    tangent = jnp.tanh(values)
    return 0.65 + 0.35 * tangent + 0.35 * values * (1.0 - tangent * tangent)


def conv_down(padded, weight):
    return lax.conv_general_dilated(
        padded,
        weight,
        (2, 2, 2),
        "VALID",
        dimension_numbers=("NCDHW", "DHWOI", "NCDHW"),
        preferred_element_type=jnp.float32,
    )


def kernel_grad(padded, grad_out):
    result = lax.conv_general_dilated(
        padded,
        grad_out,
        (1, 1, 1),
        "VALID",
        rhs_dilation=(2, 2, 2),
        dimension_numbers=("CNDHW", "IODHW", "NCDHW"),
        preferred_element_type=jnp.float32,
    )
    return jnp.transpose(result, (2, 3, 4, 1, 0))


def conv_back(grad_out, weight):
    flipped = weight[::-1, ::-1, ::-1]
    return lax.conv_general_dilated(
        grad_out,
        flipped,
        (1, 1, 1),
        ((2, 2), (2, 2), (2, 2)),
        lhs_dilation=(2, 2, 2),
        dimension_numbers=("NCDHW", "DHWIO", "NCDHW"),
        preferred_element_type=jnp.float32,
    )


def pad_lower(rim, block):
    joined = jnp.concatenate([rim, block], axis=2)
    return jnp.pad(joined, ((0, 0), (0, 0), (0, 0), (1, 0), (1, 0)))


def local(volumes, targets, counts, w_conv1, w_conv2, w_dense1, w_dense2, w_dense3):
    nspace = lax.axis_size("space")
    position = lax.axis_index("space")
    batch, cin, depth, height, width = volumes.shape
    half_x = depth // 2
    quarter_x, quarter_y, quarter_z = (depth // 4, height // 4, width // 4)
    chans_two = w_conv2.shape[3]
    capacity = MOST
    rim_input = from_behind(volumes[:, :, depth - 1 : depth], "space", 1)
    padded_input = pad_lower(rim_input, volumes)
    hidden1 = conv_down(padded_input, w_conv1)
    act1 = leaky_relu(hidden1).astype(jnp.bfloat16)
    rim_act = from_behind(act1[:, :, half_x - 1 : half_x], "space", 1)
    padded_act = pad_lower(rim_act, act1)
    hidden2 = conv_down(padded_act, w_conv2)
    act2 = leaky_relu(hidden2).astype(jnp.bfloat16)
    ends = jnp.cumsum(counts, dtype=jnp.int32)
    starts = ends - counts
    slot_ids = jnp.arange(capacity, dtype=jnp.int32)
    live_slots = (slot_ids[None, :] < counts[:, None]).reshape(-1)
    pick_rows = jnp.clip(starts[:, None] + slot_ids[None, :], 0, batch - 1).reshape(-1)
    zero_value = jnp.zeros((), jnp.bfloat16)
    packed = jnp.where(
        live_slots[:, None, None, None, None], jnp.take(act2, pick_rows, axis=0), zero_value
    )
    packed = packed.reshape(nspace, capacity, chans_two, quarter_x, quarter_y, quarter_z)
    arrived = lax.all_to_all(packed, "space", split_axis=0, concat_axis=0, tiled=True)
    feature_grid = jnp.mean(arrived.astype(jnp.float32), axis=5).astype(jnp.bfloat16)
    feats = jnp.transpose(feature_grid, (1, 2, 0, 3, 4)).reshape(capacity, -1)
    own_count = counts[position]
    own_start = starts[position]
    valid_rows = (slot_ids < own_count).astype(jnp.float32)[:, None]
    group_size = jnp.maximum(own_count, 1).astype(jnp.float32)
    own_targets = jnp.take(targets, jnp.clip(own_start + slot_ids, 0, batch - 1), axis=0)
    dense1 = jnp.dot(feats, w_dense1, preferred_element_type=jnp.float32)
    centred = dense1 - 0.5 * jnp.sum(valid_rows * dense1, axis=0) / group_size
    out1 = leaky_relu(centred).astype(jnp.bfloat16)
    dense2 = jnp.dot(out1, w_dense2, preferred_element_type=jnp.float32)
    out2 = leaky_relu(dense2).astype(jnp.bfloat16)
    pred = jnp.dot(out2, w_dense3, preferred_element_type=jnp.float32)
    diff = valid_rows * (pred - own_targets)
    loss_part = 0.5 * jnp.sum(diff * diff) / batch
    gpred = (diff / batch).astype(jnp.bfloat16)
    grad_d3 = jnp.dot(out2.T, gpred, preferred_element_type=jnp.float32)
    gdense2 = (
        jnp.dot(gpred, w_dense3.T, preferred_element_type=jnp.float32) * slope_of(dense2)
    ).astype(jnp.bfloat16)
    grad_d2 = jnp.dot(out1.T, gdense2, preferred_element_type=jnp.float32)
    gcentred = jnp.dot(gdense2, w_dense2.T, preferred_element_type=jnp.float32) * slope_of(centred)
    gcentred_mean = jnp.sum(valid_rows * gcentred, axis=0) / group_size
    gdense1 = (valid_rows * (gcentred - 0.5 * gcentred_mean)).astype(jnp.bfloat16)
    grad_d1 = jnp.dot(feats.T, gdense1, preferred_element_type=jnp.float32)
    gfeats = jnp.dot(gdense1, w_dense1.T, preferred_element_type=jnp.float32).astype(jnp.bfloat16)
    outgoing = gfeats.reshape(capacity, chans_two, nspace, quarter_x, quarter_y)
    outgoing = jnp.transpose(outgoing, (2, 0, 1, 3, 4))
    returned = lax.all_to_all(outgoing, "space", split_axis=0, concat_axis=0, tiled=True)
    returned = returned.reshape(nspace * capacity, chans_two, quarter_x, quarter_y)
    sample_ids = jnp.arange(batch, dtype=jnp.int32)
    owners = jnp.sum((ends[None, :] <= sample_ids[:, None]).astype(jnp.int32), axis=1)
    flat_rows = owners * capacity + (sample_ids - jnp.take(starts, owners))
    grad_pool = jnp.take(returned, flat_rows, axis=0)
    spread = grad_pool[..., None].astype(jnp.float32) / quarter_z
    ghidden2 = (spread * slope_of(hidden2)).astype(jnp.bfloat16)
    grad_w2 = kernel_grad(padded_act, ghidden2)
    extended = conv_back(ghidden2, w_conv2)
    incoming = from_behind(extended[:, :, 0:1, 1:, 1:].astype(jnp.bfloat16), "space", -1).astype(
        jnp.float32
    )
    gact1 = extended[:, :, 1:, 1:, 1:].at[:, :, half_x - 1 :].add(incoming)
    ghidden1 = (gact1 * slope_of(hidden1)).astype(jnp.bfloat16)
    grad_w1 = kernel_grad(padded_input, ghidden1)
    sum_w1, sum_w2, sum_d1, sum_d2, sum_d3, loss = lax.psum(
        (grad_w1, grad_w2, grad_d1, grad_d2, grad_d3, loss_part), ("dp", "space")
    )
    return (loss, sum_w1, sum_w2, sum_d1, sum_d2, sum_d3)


def solution(mesh):
    placed = (P("dp", None, "space", None, None), P("dp", None), P(), P(), P(), P(), P(), P())
    return jax.shard_map(
        local, mesh=mesh, in_specs=placed, out_specs=(P(), P(), P(), P(), P(), P()), check_vma=False
    )
```

profile of v0, /device:TPU:1, one launch (start us, length us, event | category | flops | bytes accessed | tf_op | source)
XLA Modules:
  0.0 443.8 jit_solution(9873356816846228203)
XLA Ops:
  7.2 1.1 slice.48
  8.5 4.9 %collective-permute-start = (bf16[16,4,1,4,512]{4,0,3,2,1:T(8,128)(2,1)S(1)}, bf16[16,4,1,4,512]{4,0,3,2,1:T(8,128)(2,1)S(1)}, u32[]{:S(2)}, u32[]{:S(2)}) collective-permute-start(bf16[16,4,1,4,512]{4,0,3,2,1:T(8,128)(2,1)S(1)} %copy.75), channel_id=1, source_target_pairs={{0,1},{1,2},{2,3},{3,4},{4,5},{5,6},{6,7},{7,8},{8,9},{9,10},{10,1... | collective-permute-start | bytes 786440 | tf_op jit(solution)/shard_map/ppermute | solution.py:12
  13.4 12.6 %copy.59 = bf16[16,4,4,4,512]{0,1,4,3,2:T(4,128)(2,1)} copy(bf16[16,4,4,4,512]{4,3,2,1,0:T(4,128)(2,1)} %param.10) | data formatting | bytes 2097152 | tf_op args[0]
  26.5 2.5 copy.58
  29.0 15.2 %fusion.1 = f32[16,32,2,2,256]{1,0,4,3,2:T(8,128)} fusion(bf16[3,3,3,32,4]{3,4,2,1,0:T(4,128)(2,1)S(1)} %copy-done.5, bf16[16,4,4,4,512]{0,1,4,3,2:T(4,128)(2,1)} %copy.59, bf16[16,4,1,4,512]{0,1,4,3,2:T(4,128)(2,1)} %copy.58), kind=kOutput, calls=%fused_computation.7 | convolution fusion | flops 96870400 | bytes 3414784 | tf_op jit(solution)/shard_map/conv_general_dilated | solution.py:25
  44.2 6.3 %copy.61 = f32[16,32,2,2,256]{4,1,3,2,0:T(8,128)} copy(f32[16,32,2,2,256]{1,0,4,3,2:T(8,128)} %fusion.1) | data formatting | bytes 4194304 | tf_op jit(solution)/shard_map/conv_general_dilated | solution.py:25
  50.5 2.1 multiply_convert_fusion.1
  52.6 1.9 collective-permute-start.1
  54.6 6.0 %collective-permute-done.1 = bf16[16,32,1,2,256]{4,1,3,2,0:T(8,128)(2,1)S(1)} collective-permute-done((bf16[16,32,1,2,256]{4,1,3,2,0:T(8,128)(2,1)S(1)}, bf16[16,32,1,2,256]{4,1,3,2,0:T(8,128)(2,1)S(1)}, u32[]{:S(2)}, u32[]{:S(2)}) %collective-permute-start.1) | collective-permute-done | bytes 524320 | tf_op jit(solution)/shard_map/ppermute | solution.py:12
  60.8 6.7 %copy.62 = bf16[16,32,3,2,256]{1,0,4,3,2:T(8,128)(2,1)} copy(bf16[16,32,3,2,256]{4,1,3,2,0:T(8,128)(2,1)S(1)} %pad_maximum_fusion.3) | data formatting | bytes 3145728 | tf_op jit(solution)/shard_map/concatenate | solution.py:62
  67.5 6.8 %fusion.23 = f32[16,64,1,1,128]{1,0,4,3,2:T(8,128)S(1)} fusion(bf16[16,32,3,2,256]{1,0,4,3,2:T(8,128)(2,1)} %copy.62, bf16[3,3,3,64,32]{3,4,2,1,0:T(8,128)(2,1)S(1)} %copy-done.2), kind=kOutput, calls=%fused_computation.79 | convolution fusion | flops 150601728 | bytes 2207744 | tf_op jit(solution)/shard_map/conv_general_dilated | solution.py:25
  74.5 0.5 copy.63
  75.0 0.8 gather_fusion
  75.8 1.2 select_select_fusion
  77.0 13.6 %all-to-all-start = ((bf16[32,2,64,1,1,128]{5,2,1,4,3,0:T(8,128)(2,1)}), bf16[32,2,64,1,1,128]{5,2,1,4,3,0:T(8,128)(2,1)S(1)}, u32[]{:S(2)}, u32[]{:S(2)}) async-start(bf16[32,2,64,1,1,128]{5,2,1,4,3,0:T(8,128)(2,1)} %select_select_fusion), calls=%async_computation | async-start | bytes 2097152 | tf_op jit(solution)/shard_map/all_to_all | solution.py:92
  90.5 0.6 dynamic_slice.6
  91.1 0.6 dynamic_slice.7
  92.6 0.7 gather_fusion.2
  93.2 0.7 fusion.9
  93.9 0.6 gather_fusion.1
  94.5 0.6 compare_convert_fusion
  95.1 0.7 compare_and_fusion.2
  95.8 22.4 %all-to-all-done = bf16[32,2,64,1,1,128]{5,2,1,4,3,0:T(8,128)(2,1)S(1)} async-done(((bf16[32,2,64,1,1,128]{5,2,1,4,3,0:T(8,128)(2,1)}), bf16[32,2,64,1,1,128]{5,2,1,4,3,0:T(8,128)(2,1)S(1)}, u32[]{:S(2)}, u32[]{:S(2)}) %all-to-all-start) | async-done | bytes 1048608 | tf_op jit(solution)/shard_map/all_to_all | solution.py:92
  118.3 0.7 convert_reduce_fusion
  119.5 0.7 multiply_reduce_fusion.1
  120.5 1.3 fusion.20
  122.4 0.7 copy.68
  123.1 6.2 %all-to-all-start.1 = ((bf16[32,2,64,1,1]{2,1,4,3,0:T(2,128)(2,1)}), bf16[32,2,64,1,1]{2,1,4,3,0:T(2,128)(2,1)S(1)}, u32[]{:S(2)}, u32[]{:S(2)}) async-start(bf16[32,2,64,1,1]{2,1,4,3,0:T(2,128)(2,1)} %copy.68), calls=%async_computation.1 | async-start | bytes 32768 | tf_op jit(solution)/shard_map/all_to_all | solution.py:121
  130.2 8.4 %all-to-all-done.1 = bf16[32,2,64,1,1]{2,1,4,3,0:T(2,128)(2,1)S(1)} async-done(((bf16[32,2,64,1,1]{2,1,4,3,0:T(2,128)(2,1)}), bf16[32,2,64,1,1]{2,1,4,3,0:T(2,128)(2,1)S(1)}, u32[]{:S(2)}, u32[]{:S(2)}) %all-to-all-start.1) | async-done | bytes 8224 | tf_op jit(solution)/shard_map/all_to_all | solution.py:121
  138.6 0.6 gather_fusion.3
  139.3 10.9 %fusion.22 = f32[16,32,3,3,257]{1,0,4,3,2:T(8,128)S(1)} fusion(bf16[3,3,3,64,32]{3,4,2,1,0:T(8,128)(2,1)S(1)} %copy-done.2, f32[16,64,1,1,128]{1,0,4,3,2:T(8,128)S(1)} %fusion.23, f32[16,64]{1,0:T(8,128)S(1)} %convert_multiply_fusion), kind=kOutput, calls=%fused_computation.78 | convolution fusion | flops 227672064 | bytes 5376000 | tf_op jit(solution)/shard_map/conv_general_dilated | solution.py:50
  150.2 3.9 slice.62
  154.1 2.3 slice.63
  156.4 1.6 slice.66
  158.0 6.2 %copy.76 = f32[16,32,2,2,256]{4,1,3,2,0:T(8,128)} copy(f32[16,32,2,2,256]{1,0,4,3,2:T(8,128)} %slice.62) | data formatting | bytes 4194304
  164.2 2.8 copy.77
  167.0 3.2 copy.71
  170.2 2.9 collective-permute-start.2
  173.1 6.2 %fusion.21 = f32[3,3,3,64,32]{3,4,2,1,0:T(8,128)} fusion(bf16[16,32,3,2,256]{1,0,4,3,2:T(8,128)(2,1)} %copy.62, f32[16,64,1,1,128]{1,0,4,3,2:T(8,128)S(1)} %fusion.23, f32[16,64]{1,0:T(8,128)S(1)} %convert_multiply_fusion), kind=kOutput, calls=%fused_computation.77 | convolution fusion | flops 151781376 | bytes 2322432 | tf_op jit(solution)/shard_map/transpose | solution.py:45
  179.3 1.6 collective-permute-done.2
  180.9 1.1 add_dynamic-update-slice_fusion
  182.0 2.9 multiply_convert_fusion
  184.9 4.8 %copy.73 = bf16[16,32,2,2,256]{1,0,4,3,2:T(8,128)(2,1)} copy(bf16[16,32,2,2,256]{4,1,3,2,0:T(8,128)(2,1)S(1)} %multiply_convert_fusion) | data formatting | bytes 2097152 | tf_op jit(solution)/shard_map/convert_element_type | solution.py:135
  189.6 13.8 %fusion = f32[3,3,3,32,4]{3,4,2,1,0:T(4,128)S(1)} fusion(bf16[16,32,2,2,256]{1,0,4,3,2:T(8,128)(2,1)} %copy.73, bf16[16,4,4,4,512]{0,1,4,3,2:T(4,128)(2,1)} %copy.59, bf16[16,4,1,4,512]{0,1,4,3,2:T(4,128)(2,1)} %copy.58), kind=kOutput, calls=%fused_computation.6 | convolution fusion | flops 96870400 | bytes 2373120 | tf_op jit(solution)/shard_map/transpose | solution.py:45
  203.4 78.7 %all-reduce = (f32[]{:T(128)}, f32[3,3,3,32,4]{3,4,2,1,0:T(4,128)}, f32[128,64]{0,1:T(8,128)}, f32[64,4]{0,1:T(4,128)}) all-reduce(f32[]{:T(128)S(6)} %div.40, f32[3,3,3,32,4]{3,4,2,1,0:T(4,128)S(1)} %fusion, f32[128,64]{0,1:T(8,128)S(1)} %fusion.18, f32[64,4]{0,1:T(4,128)S(1)} %fusion.13), channel_id=1, replica_groups=mesh['dp'=8,'space'=32] {'dp','space'}, use_global_device_ids=true, to_apply=%region_4.5 | all-reduce | flops 11905 | bytes 95240 | tf_op jit(solution)/shard_map/psum | solution.py:137
  282.1 150.8 %all-reduce.4.cloned.1.call-done = (f32[3,3,3,64,32]{3,4,2,1,0:T(8,128)}, f32[2048,128]{1,0:T(8,128)}) async-done(((f32[3,3,3,64,32]{3,4,2,1,0:T(8,128)}, f32[2048,128]{1,0:T(8,128)}), (f32[3,3,3,64,32]{3,4,2,1,0:T(8,128)}, f32[2048,128]{1,0:T(8,128)})) %all-reduce.4.cloned.1.call-update) | async-done | bytes 1269776 | tf_op jit(solution)/shard_map/psum | solution.py:137
  432.9 1.8 copy.81
  434.7 2.3 copy.82
  (54 shorter events, 3.1 us)
Async XLA Ops:
  7.2 112.0 %copy-start = (bf16[2048,128]{1,0:T(8,128)(2,1)S(1)}, bf16[2048,128]{1,0:T(8,128)(2,1)}, u32[]{:S(2)}) copy-start(bf16[2048,128]{1,0:T(8,128)(2,1)} %param.15) | copy-start | bytes 1572868
  8.5 17.5 %copy-start.4 = (s32[32]{0:T(128)S(1)}, s32[32]{0:T(128)}, u32[]{:S(2)}) copy-start(s32[32]{0:T(128)} %param.12) | copy-start | bytes 388
  8.5 18.0 %collective-permute-start = (bf16[16,4,1,4,512]{4,0,3,2,1:T(8,128)(2,1)S(1)}, bf16[16,4,1,4,512]{4,0,3,2,1:T(8,128)(2,1)S(1)}, u32[]{:S(2)}, u32[]{:S(2)}) collective-permute-start(bf16[16,4,1,4,512]{4,0,3,2,1:T(8,128)(2,1)S(1)} %copy.75), channel_id=1, source_target_pairs={{0,1},{1,2},{2,3},{3,4},{4,5},{5,6},{6,7},{7,8},{8,9},{9,10},{10,1... | collective-permute-start | bytes 786440 | tf_op jit(solution)/shard_map/ppermute | solution.py:12
  26.0 3.0 copy-start.5
  52.6 8.0 %collective-permute-start.1 = (bf16[16,32,1,2,256]{4,1,3,2,0:T(8,128)(2,1)S(1)}, bf16[16,32,1,2,256]{4,1,3,2,0:T(8,128)(2,1)S(1)}, u32[]{:S(2)}, u32[]{:S(2)}) collective-permute-start(bf16[16,32,1,2,256]{4,1,3,2,0:T(8,128)(2,1)S(1)} %slice.61), channel_id=1, source_target_pairs={{0,1},{1,2},{2,3},{3,4},{4,5},{5,6},{6,7},{7,8},{8,9},{9,10},{10,1... | collective-permute-start | bytes 1572872 | tf_op jit(solution)/shard_map/ppermute | solution.py:12
  60.8 6.7 %copy-start.2 = (bf16[3,3,3,64,32]{3,4,2,1,0:T(8,128)(2,1)S(1)}, bf16[3,3,3,64,32]{3,4,2,1,0:T(8,128)(2,1)}, u32[]{:S(2)}) copy-start(bf16[3,3,3,64,32]{3,4,2,1,0:T(8,128)(2,1)} %param.14) | copy-start | bytes 331780
  75.7 16.6 %copy-start.3 = (f32[16,4]{0,1:T(4,128)S(1)}, f32[16,4]{0,1:T(4,128)}, u32[]{:S(2)}) copy-start(f32[16,4]{0,1:T(4,128)} %param.11) | copy-start | bytes 772
  77.0 42.4 %copy-start.6 = (bf16[128,64]{0,1:T(8,128)(2,1)S(1)}, bf16[128,64]{0,1:T(8,128)(2,1)}, u32[]{:S(2)}) copy-start(bf16[128,64]{0,1:T(8,128)(2,1)} %param.16) | copy-start | bytes 49156
  77.0 42.6 %copy-start.7 = (bf16[64,4]{0,1:T(4,128)(2,1)S(1)}, bf16[64,4]{0,1:T(4,128)(2,1)}, u32[]{:S(2)}) copy-start(bf16[64,4]{0,1:T(4,128)(2,1)} %param.17) | copy-start | bytes 1540
  77.0 41.3 %all-to-all-start = ((bf16[32,2,64,1,1,128]{5,2,1,4,3,0:T(8,128)(2,1)}), bf16[32,2,64,1,1,128]{5,2,1,4,3,0:T(8,128)(2,1)S(1)}, u32[]{:S(2)}, u32[]{:S(2)}) async-start(bf16[32,2,64,1,1,128]{5,2,1,4,3,0:T(8,128)(2,1)} %select_select_fusion), calls=%async_computation | async-start | bytes 2097152 | tf_op jit(solution)/shard_map/all_to_all | solution.py:92
  123.1 15.5 %all-to-all-start.1 = ((bf16[32,2,64,1,1]{2,1,4,3,0:T(2,128)(2,1)}), bf16[32,2,64,1,1]{2,1,4,3,0:T(2,128)(2,1)S(1)}, u32[]{:S(2)}, u32[]{:S(2)}) async-start(bf16[32,2,64,1,1]{2,1,4,3,0:T(2,128)(2,1)} %copy.68), calls=%async_computation.1 | async-start | bytes 32768 | tf_op jit(solution)/shard_map/all_to_all | solution.py:121
  129.4 303.6 %all-reduce.4.cloned.1.call-start = ((), (), s32[]{:S(2)}) async-start(), calls=%async_computation.2 | async-start | bytes 2981888 | tf_op jit(solution)/shard_map/psum | solution.py:137
  170.2 10.7 %collective-permute-start.2 = (bf16[16,32,1,2,256]{4,1,3,2,0:T(8,128)(2,1)}, bf16[16,32,1,2,256]{4,1,3,2,0:T(8,128)(2,1)S(1)}, u32[]{:S(2)}, u32[]{:S(2)}) collective-permute-start(bf16[16,32,1,2,256]{4,1,3,2,0:T(8,128)(2,1)} %copy.71), channel_id=1, source_target_pairs={{1,0},{2,1},{3,2},{4,3},{5,4},{6,5},{7,6},{8,7},{9,8},{10,9},{11,1... | collective-permute-start | bytes 1572872 | tf_op jit(solution)/shard_map/ppermute | solution.py:12
  189.6 247.3 %copy-start.1 = (bf16[2048,128]{1,0:T(8,128)(2,1)S(1)}, bf16[2048,128]{1,0:T(8,128)(2,1)}, u32[]{:S(2)}) copy-start(bf16[2048,128]{1,0:T(8,128)(2,1)} %param.15) | copy-start | bytes 1572868
Sparse Core Ops, SparseCore 0:
  179.4 253.4 all-reduce.3
where the time goes:
time: 446 us; the launch traced here: 444 us
  waiting for transfers between devices  189 us (42%)
  blocking collectives  78.7 us (18%)
  local copies, waits for them, and re-layouts  63.6 us (14%)
  matrix products  56.1 us (13%)
  starting transfers between devices  29.6 us (7%)
  between operations  15.7 us (4%)
  other arithmetic  11 us (2%)
    psum x1, waiting for transfers between devices, local(): lax.psum((grad_w1, grad_w2, grad_d1, grad_d2, grad_d3, loss_part), ('dp',...  151 us
    psum x1, blocking collectives, local(): lax.psum((grad_w1, grad_w2, grad_d1, grad_d2, grad_d3, loss_part), ('dp',...  78.7 us
    unnamed x23, local copies, waits for them, and re-layouts  26 us
    all_to_all x1, waiting for transfers between devices, local(): lax.all_to_all(packed, 'space', split_axis=0, concat_axis=0, tiled=True)  22.4 us
    conv_general_dilated x2, matrix products, conv_down(): lax.conv_general_dilated(padded, weight, (2, 2, 2), 'VALID', dimension_nu...  22 us
    transpose x2, matrix products, kernel_grad(): return jnp.transpose(result, (2, 3, 4, 1, 0))  19.9 us
    all_to_all x1, starting transfers between devices, local(): lax.all_to_all(packed, 'space', split_axis=0, concat_axis=0, tiled=True)  13.6 us
    conv_general_dilated x1, matrix products, conv_back(): lax.conv_general_dilated(grad_out, flipped, (1, 1, 1), ((2, 2), (2, 2), (...  10.9 us
  transfers between devices with their start and end apart: 6, of which 5 were waited for; matrix products, arithmetic and copies ran while one was open for 10% of the time, Pallas kernels for 0%

commit v1 on v0

v1 whole, which is shorter than its diff:
```python
import functools

import jax
import jax.numpy as jnp
import numpy as np
from jax import lax
from jax.experimental import pallas as pl
from jax.experimental.pallas import tpu as pltpu
from jax.sharding import Mesh
from jax.sharding import PartitionSpec as P

BF = jnp.bfloat16
F32 = jnp.float32
SLABS = ("yh", "z", "core")
PLANE = ("x", "yl", "yh")
S = 16
LANES = 128
WIDE = S * LANES
HALF = 176
CHUNK = 512

NN = (((1,), (0,)), ((), ()))
NT = (((1,), (1,)), ((), ()))
TN = (((0,), (0,)), ((), ()))


def mm(a, b, dims=NN):
    return lax.dot_general(a, b, dims, preferred_element_type=F32)


def mm_exact(a, b):
    return lax.dot_general(
        a, b, NN, preferred_element_type=F32, precision=lax.Precision.HIGHEST
    )


def leaky(v, t):
    return v * (0.65 + 0.35 * t)


def slope(v, t):
    return 0.65 + 0.35 * t + 0.35 * v * (1.0 - t * t)


def split_matrix():
    m = np.zeros((512, 640), np.float32)
    for k, offset in enumerate((-1, 0, 1, 2, 3)):
        for i in range(128):
            if 4 * i + offset >= 0:
                m[4 * i + offset, k * 128 + i] = 1.0
    return m


def band_matrices():
    own = np.zeros((2, 2, 128, 192), np.float32)
    rim = np.zeros((2, 128, 48), np.float32)
    for i in range(2):
        for j in range(2):
            for a in range(3):
                for b in range(3):
                    x, y = 2 * i + a - 1, 2 * j + b - 1
                    if y < 0:
                        continue
                    for e in range(3):
                        for c in range(4):
                            src = ((a * 3 + b) * 3 + e) * 4 + c
                            if x >= 0:
                                own[i, j, src, ((e * 4 + c) * 4 + x) * 4 + y] = 1.0
                            else:
                                rim[j, src, (e * 4 + c) * 4 + y] = 1.0
    return own, rim


def lane_ids(shape):
    return lax.broadcasted_iota(jnp.int32, shape, len(shape) - 1)


def shift_up(x):
    parts = []
    for k in range(x.shape[1] // LANES):
        p = pltpu.roll(x[:, k * LANES : (k + 1) * LANES], 1, 1)
        parts.append(jnp.where(lane_ids(p.shape) == 0, 0.0, p))
    return jnp.concatenate(parts, axis=1)


def shift_down(x):
    parts = []
    for k in range(x.shape[1] // LANES):
        p = pltpu.roll(x[:, k * LANES : (k + 1) * LANES], LANES - 1, 1)
        parts.append(jnp.where(lane_ids(p.shape) == LANES - 1, 0.0, p))
    return jnp.concatenate(parts, axis=1)


def store_plane(h, s, cols, a1_ref, slope_ref):
    t = jnp.tanh(h)
    act = leaky(h, t)
    slope_ref[s, :, cols] = slope(h, t).astype(BF)
    if s == 0:
        a1_ref[64:128, cols] = act.astype(BF)
    else:
        a1_ref[128:192, cols] = act.astype(BF)
        a1_ref[0:64, cols] = shift_up(act).astype(BF)


def first_kernel(v_ref, split_ref, w1_ref, own_ref, w2_ref, x4_ref, a1_ref, slope_ref, send_ref):
    w = jnp.concatenate(
        [mm(w1_ref[...], own_ref[1, j]).astype(BF) for j in range(2)], axis=0
    )
    for q in range(4):
        d = mm(v_ref[q * 256 : (q + 1) * 256, :], split_ref[...])
        for k in range(5):
            for n in range(4):
                x4_ref[k * 64 : (k + 1) * 64, (4 * q + n) * LANES : (4 * q + n + 1) * LANES] = d[
                    n * 64 : (n + 1) * 64, k * LANES : (k + 1) * LANES
                ].astype(BF)
    for q in range(4):
        cols = slice(q * CHUNK, (q + 1) * CHUNK)
        for s in range(2):
            h = mm(w, x4_ref[s * 128 : s * 128 + 192, cols])
            store_plane(h, s, cols, a1_ref, slope_ref)
        send_ref[:, cols] = mm(w2_ref[0], a1_ref[:, cols]).astype(BF)


def second_kernel(
    halo_ref, split_ref, w1_ref, own_ref, rim_ref, w2_ref, x4_ref, a1b_ref, part_ref,
    xh_ref, a1_ref, slope_ref, slope2_ref, pay_ref, fown_ref,
):
    w = jnp.concatenate(
        [mm(w1_ref[...], own_ref[0, j]).astype(BF) for j in range(2)], axis=0
    )
    wh = jnp.concatenate([mm(w1_ref[...], rim_ref[j]).astype(BF) for j in range(2)], axis=0)
    d = mm(halo_ref[...], split_ref[...])
    for k in range(5):
        for n in range(S):
            xh_ref[k * 16 : (k + 1) * 16, n * LANES : (n + 1) * LANES] = d[
                n * 16 : (n + 1) * 16, k * LANES : (k + 1) * LANES
            ].astype(BF)
    total = jnp.zeros((S, 64), F32)
    for q in range(4):
        cols = slice(q * CHUNK, (q + 1) * CHUNK)
        for s in range(2):
            h = mm(w, x4_ref[s * 128 : s * 128 + 192, cols]) + mm(
                wh, xh_ref[s * 32 : s * 32 + 48, cols]
            )
            store_plane(h, s, cols, a1_ref, slope_ref)
        h2 = mm(w2_ref[1], a1_ref[:, cols]) + mm(w2_ref[2], a1b_ref[:, cols])
        h2 = h2 + part_ref[:, cols].astype(F32)
        t = jnp.tanh(h2)
        act2 = leaky(h2, t).astype(BF)
        slope2_ref[:, cols] = slope(h2, t).astype(BF)
        rows = lax.broadcasted_iota(jnp.int32, (S, CHUNK), 0)
        owner = lax.shift_right_logical(lane_ids((S, CHUNK)), 7) + 4 * q
        pick = jnp.where(rows == owner, 1.0, 0.0).astype(BF)
        total = total + mm(pick, act2, NT)
    feats = total * (1.0 / 128.0)
    pay_ref[...] = jnp.concatenate([feats[0:8], feats[8:16]], axis=1).astype(BF)
    fown_ref[...] = jnp.concatenate([feats, jnp.zeros((S, 64), F32)], axis=1).astype(BF)


def tail_kernel(
    g_ref, fown_ref, w1_ref, w1own_ref, w2_ref, w3_ref, same_ref, target_ref, pay_ref, gf_ref
):
    low = lane_ids((8, LANES)) < 64
    pairs = []
    for p in range(16):
        ga, gb = g_ref[2 * p].astype(F32), g_ref[2 * p + 1].astype(F32)
        lo = jnp.where(low, ga, pltpu.roll(gb, 64, 1))
        hi = jnp.where(low, pltpu.roll(ga, 64, 1), gb)
        pairs.append(jnp.concatenate([lo, hi], axis=0).astype(BF))
    feats = jnp.concatenate(pairs, axis=1)
    same = same_ref[...]
    dense1 = mm(feats, w1_ref[...])
    centred = dense1 - 0.5 * mm_exact(same, dense1)
    t1 = jnp.tanh(centred)
    out1 = leaky(centred, t1).astype(BF)
    dense2 = mm(out1, w2_ref[...])
    t2 = jnp.tanh(dense2)
    out2 = leaky(dense2, t2).astype(BF)
    diff = mm(out2, w3_ref[...]) - target_ref[...]
    loss = jnp.sum(jnp.sum(diff * diff, axis=1, keepdims=True), axis=0, keepdims=True) / 32.0
    gpred = (diff / 16.0).astype(BF)
    gdense2 = (mm(gpred, w3_ref[...], NT) * slope(dense2, t2)).astype(BF)
    gcentred = mm(gdense2, w2_ref[...], NT) * slope(centred, t1)
    gdense1 = (gcentred - 0.5 * mm_exact(same, gcentred)).astype(BF)
    gf_ref[...] = mm(w1own_ref[...], gdense1, NT)
    lanes = lane_ids((S, LANES))
    top = lax.broadcasted_iota(jnp.int32, (S, LANES), 0) == 0
    high = loss.astype(BF).astype(F32)
    mid = (loss - high).astype(BF).astype(F32)
    rest = loss - high - mid
    last = fown_ref[...].astype(F32) + gpred.astype(F32)
    for k, piece in enumerate((high, mid, rest)):
        last = last + jnp.where(jnp.logical_and(top, lanes == 68 + k), piece, 0.0)
    pay_ref[0:16] = out1
    pay_ref[16:32] = gdense1
    pay_ref[32:48] = (out2.astype(F32) + pltpu.roll(gdense2.astype(F32), 64, 1)).astype(BF)
    pay_ref[48:64] = last.astype(BF)


def back_kernel(
    core_ref, gf_ref, slope2_ref, next2_ref, block_ref, s1a_ref, s1b_ref, a1a_ref, a1b_ref,
    x4_ref, xh_ref, own_ref, rim_ref, keep_ref, send_ref, g_ref, h_ref, w_ref,
):
    gf = gf_ref[...].astype(BF).astype(F32) * (1.0 / 128.0)
    for q in range(4):
        cols = slice(q * CHUNK, (q + 1) * CHUNK)
        spread = jnp.concatenate(
            [
                jnp.broadcast_to(gf[:, 4 * q + n : 4 * q + n + 1], (128, LANES))
                for n in range(4)
            ],
            axis=1,
        )
        go = spread[0:64] * slope2_ref[:, cols].astype(F32)
        gn = spread[64:128] * next2_ref[:, cols].astype(F32)
        g_ref[0:64, cols] = go.astype(BF)
        g_ref[64:128, cols] = gn.astype(BF)
        g_ref[128:192, cols] = shift_down(go).astype(BF)
        g_ref[192:256, cols] = shift_down(gn).astype(BF)
        gact = mm(block_ref[...], g_ref[:, cols])
        for s in range(2):
            for i, ref in enumerate((s1a_ref, s1b_ref)):
                r = (2 * s + i) * 64
                h_ref[s, i * 64 : (i + 1) * 64, cols] = (
                    gact[r : r + 64] * ref[s, :, cols].astype(F32)
                ).astype(BF)
    go, gn = g_ref[0:64, :], g_ref[64:128, :]
    a1 = mm(go, a1a_ref[...], NT)
    a2 = mm(go, a1b_ref[...], NT)
    a0 = mm(gn, a1b_ref[...], NT)
    w_ref[0:64] = a1[:, :128]
    w_ref[64:128] = a2[:, :128]
    w_ref[128:192] = a0[:, :128]
    w_ref[192:256] = jnp.concatenate([a1[:, 128:192], a2[:, 128:192]], axis=1)
    w_ref[256:320] = jnp.concatenate([a0[:, 128:192], jnp.zeros((64, 64), F32)], axis=1)
    r = mm(h_ref[0], x4_ref[0:192, :], NT) + mm(h_ref[1], x4_ref[128:320, :], NT)
    rh = mm(h_ref[0, 0:64], xh_ref[0:48, :], NT) + mm(h_ref[1, 0:64], xh_ref[32:80, :], NT)
    total = jnp.zeros((32, LANES), F32)
    for i in range(2):
        for j in range(2):
            part = r[(2 * i + j) * 32 : (2 * i + j + 1) * 32]
            for _ in range(2):
                piece = part.astype(BF)
                total = total + mm(piece, own_ref[i, j], NT)
                part = part - piece.astype(F32)
    for j in range(2):
        part = rh[j * 32 : (j + 1) * 32]
        for _ in range(2):
            piece = part.astype(BF)
            total = total + mm(piece, rim_ref[j], NT)
            part = part - piece.astype(F32)
    w_ref[320:352] = total
    first = core_ref[0] == 0

    @pl.when(first)
    def _():
        keep_ref[...] = w_ref[0:HALF].astype(BF)
        send_ref[...] = w_ref[HALF : 2 * HALF].astype(BF)

    @pl.when(jnp.logical_not(first))
    def _():
        keep_ref[...] = w_ref[HALF : 2 * HALF].astype(BF)
        send_ref[...] = w_ref[0:HALF].astype(BF)


def plane_kernel(in_ref, out_ref, d2_ref, d3_ref, loss_ref):
    total = in_ref[0, 0:HALF].astype(F32)
    for p in range(1, 16):
        total = total + in_ref[p, 0:HALF].astype(F32)
    out_ref[0:HALF] = total.astype(BF)

    def stack(k, yh):
        at = HALF + 16 * k
        return jnp.concatenate([in_ref[2 * p + yh, at : at + 16] for p in range(8)], axis=0)

    out1, gdense1, mixed = stack(0, 0), stack(1, 0), stack(2, 0)
    last = [stack(3, yh) for yh in range(2)]
    for yh in range(2):
        d1 = mm(last[yh], gdense1, TN)
        out_ref[HALF + 64 * yh : HALF + 64 * (yh + 1)] = d1[0:64].astype(BF)
    d2 = mm(out1, mixed, TN)
    d2_ref[...] = pltpu.roll(d2, 64, 1)[:, 0:64]
    d3 = mm(mixed, last[0], TN)
    d3_ref[...] = pltpu.roll(d3, 64, 1)[0:64, 0:4]
    lanes = lane_ids((128, LANES))
    rows = lax.broadcasted_iota(jnp.int32, (128, LANES), 0)
    held = jnp.logical_and(
        jnp.logical_and(lanes >= 68, lanes < 71), jnp.bitwise_and(rows, 15) == 0
    )
    values = jnp.where(held, last[0].astype(F32), 0.0)
    loss_ref[...] = jnp.sum(jnp.sum(values, axis=1, keepdims=True), axis=0, keepdims=True)


def depth_kernel(in_ref, out_ref):
    total = in_ref[0, 0:HALF].astype(F32)
    for p in range(1, 8):
        total = total + in_ref[p, 0:HALF].astype(F32)
    out_ref[0:HALF] = total.astype(BF)
    for p in range(8):
        out_ref[HALF + 128 * p : HALF + 128 * (p + 1)] = in_ref[p, HALF : HALF + 128]


def last_kernel(core_ref, mine_ref, other_ref, gw1_ref, gw2_ref, gd1_ref, w_ref):
    first = core_ref[0] == 0

    @pl.when(first)
    def _():
        w_ref[0:HALF] = mine_ref[0:HALF].astype(F32)
        w_ref[HALF : 2 * HALF] = other_ref[0:HALF].astype(F32)

    @pl.when(jnp.logical_not(first))
    def _():
        w_ref[0:HALF] = other_ref[0:HALF].astype(F32)
        w_ref[HALF : 2 * HALF] = mine_ref[0:HALF].astype(F32)

    for z in range(8):
        for yh in range(2):
            at = HALF + 128 * z + 64 * yh
            a = mine_ref[at : at + 64].astype(F32)
            b = other_ref[at : at + 64].astype(F32)
            slab = yh * 16 + z * 2
            gd1_ref[pl.ds(slab, 64, stride=32), :] = jnp.where(first, a, b)
            gd1_ref[pl.ds(slab + 1, 64, stride=32), :] = jnp.where(first, b, a)
    place = {1: 0, 2: 1, 0: 2}
    for a in range(3):
        for e in range(3):
            gw2_ref[a, 0, e] = jnp.zeros((64, 32), F32)
            for b in range(1, 3):
                if e < 2:
                    chunk, off = place[a], e * 64 + (b - 1) * 32
                else:
                    chunk = 4 if a == 0 else 3
                    off = (64 if a == 2 else 0) + (b - 1) * 32
                block = w_ref[chunk * 64 : (chunk + 1) * 64]
                if off:
                    block = pltpu.roll(block, LANES - off, 1)
                gw2_ref[a, b, e] = block[:, 0:32]
    block = w_ref[320:352]
    for a in range(3):
        for b in range(3):
            for e in range(3):
                off = ((a * 3 + b) * 3 + e) * 4
                moved = pltpu.roll(block, LANES - off, 1) if off else block
                gw1_ref[a, b, e] = moved[:, 0:4]


def call(kernel, outs, args, scratch=(), flops=0, scalars=0):
    vm = pl.BlockSpec(memory_space=pltpu.VMEM)
    sm = pl.BlockSpec(memory_space=pltpu.SMEM)
    size = sum(int(np.prod(s)) * jnp.dtype(d).itemsize for s, d in outs)
    return pl.pallas_call(
        kernel,
        out_shape=[jax.ShapeDtypeStruct(s, d) for s, d in outs],
        in_specs=[sm] * scalars + [vm] * (len(args) - scalars),
        out_specs=[vm] * len(outs),
        scratch_shapes=list(scratch),
        compiler_params=pltpu.CompilerParams(vmem_limit_bytes=40 * 1024 * 1024),
        cost_estimate=pl.CostEstimate(flops=flops, bytes_accessed=size, transcendentals=0),
    )(*args)


def local(volumes, targets, counts, w_conv1, w_conv2, w_dense1, w_dense2, w_dense3):
    core = lax.axis_index("core")
    position = lax.axis_index(SLABS)
    slabs = 32
    forward = [(i, i + 1) for i in range(slabs - 1)]
    backward = [(i + 1, i) for i in range(slabs - 1)]
    swap = [(0, 1), (1, 0)]

    rim = volumes[:, :, 3].reshape(256, 512)
    halo = lax.ppermute(rim, SLABS, forward)
    split = jnp.asarray(split_matrix(), BF)
    own_np, rim_np = band_matrices()
    own, rimsel = jnp.asarray(own_np, BF), jnp.asarray(rim_np, BF)
    w1 = jnp.pad(jnp.transpose(w_conv1, (3, 0, 1, 2, 4)).reshape(32, 108), ((0, 0), (0, 20)))
    w2 = jnp.transpose(w_conv2[:, 1:], (0, 3, 2, 1, 4)).reshape(3, 64, 192)

    x4, a1b, s1b, send = call(
        first_kernel,
        [((320, WIDE), BF), ((192, WIDE), BF), ((2, 64, WIDE), BF), ((64, WIDE), BF)],
        (volumes.reshape(1024, 512), split, w1, own, w2),
        flops=10**9,
    )
    part = lax.ppermute(send, SLABS, forward)
    xh, a1a, s1a, slope2, pay, fown = call(
        second_kernel,
        [
            ((80, WIDE), BF), ((192, WIDE), BF), ((2, 64, WIDE), BF), ((64, WIDE), BF),
            ((8, LANES), BF), ((S, LANES), BF),
        ],
        (halo, split, w1, own, rimsel, w2, x4, a1b, part),
        flops=10**9,
    )
    next2 = lax.ppermute(slope2, SLABS, backward)
    spread = jnp.broadcast_to(pay[None], (slabs, 8, LANES))
    gathered = lax.all_to_all(spread, SLABS, 0, 0, tiled=True)

    ends = jnp.cumsum(counts, dtype=jnp.int32)
    ids = jnp.arange(S, dtype=jnp.int32)
    owners = jnp.sum((ends[None, :] <= ids[:, None]).astype(jnp.int32), axis=1)
    alike = (owners[:, None] == owners[None, :]).astype(F32)
    same = alike / jnp.sum(alike, axis=1, keepdims=True)
    wd1 = jnp.transpose(w_dense1.reshape(64, slabs, 128), (1, 0, 2)).reshape(2048, 128)
    wd1own = lax.dynamic_slice(jnp.pad(wd1, ((0, 64), (0, 0))), (position * 64, 0), (128, 128))
    wd2 = jnp.pad(w_dense2, ((0, 0), (0, 64)))
    wd3 = jnp.pad(w_dense3, ((0, 64), (64, 60)))
    goal = jnp.pad(targets, ((0, 0), (64, 60)))
    tail, gf = call(
        tail_kernel,
        [((64, LANES), BF), ((128, S), F32)],
        (gathered, fown, wd1, wd1own, wd2, wd3, same, goal),
        flops=10**8,
    )

    w2t = jnp.transpose(w_conv2[:, 1:], (0, 2, 1, 4, 3)).reshape(3, 3, 64, 64)
    zero = jnp.zeros((64, 64), BF)
    block = jnp.concatenate(
        [
            jnp.concatenate(row, axis=1)
            for row in (
                (w2t[1, 1], zero, zero, zero),
                (w2t[2, 1], w2t[0, 1], zero, zero),
                (w2t[1, 2], zero, w2t[1, 0], zero),
                (w2t[2, 2], w2t[0, 2], w2t[2, 0], w2t[0, 0]),
            )
        ],
        axis=0,
    )
    which = core.astype(jnp.int32).reshape(1)
    keep, give = call(
        back_kernel,
        [((HALF, LANES), BF), ((HALF, LANES), BF)],
        (which, gf, slope2, next2, block, s1a, s1b, a1a, a1b, x4, xh, own, rimsel),
        scratch=[
            pltpu.VMEM((256, WIDE), BF), pltpu.VMEM((2, 128, WIDE), BF),
            pltpu.VMEM((2 * HALF, LANES), F32),
        ],
        flops=10**9,
        scalars=1,
    )
    taken = lax.ppermute(give, "core", swap)
    both = (keep.astype(F32) + taken.astype(F32)).astype(BF)
    rows = HALF + 64
    mixed = jnp.broadcast_to(jnp.concatenate([both, tail], axis=0)[None], (16, rows, LANES))
    planes = lax.all_to_all(mixed, PLANE, 0, 0, tiled=True)
    summed, d2, d3, loss = call(
        plane_kernel,
        [((HALF + 128, LANES), BF), ((128, 64), F32), ((64, 4), F32), ((1, 1), F32)],
        (planes,),
        flops=10**8,
    )
    deep = lax.all_to_all(
        jnp.broadcast_to(summed[None], (8, HALF + 128, LANES)), "z", 0, 0, tiled=True
    )
    (mine,) = call(depth_kernel, [((HALF + 1024, LANES), BF)], (deep,), flops=10**7)
    other = lax.ppermute(mine, "core", swap)
    gw1, gw2, gd1 = call(
        last_kernel,
        [((3, 3, 3, 32, 4), F32), ((3, 3, 3, 64, 32), F32), ((2048, 128), F32)],
        (which, mine, other),
        scratch=[pltpu.VMEM((2 * HALF, LANES), F32)],
        flops=10**7,
        scalars=1,
    )
    return loss.reshape(()), gw1, gw2, gd1, d2, d3


def solution(mesh):
    fine = Mesh(mesh.devices.reshape(4, 2, 2, 8, 2), ("x", "yl", "yh", "z", "core"))
    dp = ("x", "yl")
    placed = (P(dp, None, SLABS, None, None), P(dp, None), P(), P(), P(), P(), P(), P())
    return jax.shard_map(
        local, mesh=fine, in_specs=placed, out_specs=(P(), P(), P(), P(), P(), P()), check_vma=False
    )
```

time: 446 us -> 126 us (0.28)
  waiting for transfers between devices: 189 us -> 7.14 us
  matrix products: 56.1 us -> 0 us
  blocking collectives: 78.7 us -> 39.9 us
  local copies, waits for them, and re-layouts: 63.6 us -> 31.8 us
  Pallas kernels: 0 us -> 15.6 us
  between operations: 15.7 us -> 0.82 us
  other arithmetic: 11 us -> 3.56 us
    psum x1 -> x0, waiting for transfers between devices: 151 us -> none  [local(): lax.psum((grad_w1, grad_w2, grad_d1, grad_d2, grad_d3, loss_part), ('dp',...]
    psum x1 -> x0, blocking collectives: 78.7 us -> none  [local(): lax.psum((grad_w1, grad_w2, grad_d1, grad_d2, grad_d3, loss_part), ('dp',...]
    all_to_all x0 -> x2, blocking collectives: none -> 39.9 us  [the longest x1 20.1 us: local(): lax.all_to_all(jnp.broadcast_to(summed[None], (8, HALF + 128, LANES)), 'z...]
    conv_general_dilated x3 -> x0, matrix products: 32.9 us -> none  [the longest x2 22 us: conv_down(): lax.conv_general_dilated(padded, weight, (2, 2, 2), 'VALID', dimension_nu...]
    all_to_all x2 -> x1, waiting for transfers between devices: 30.8 us -> 6.25 us  [local(): gathered = lax.all_to_all(spread, SLABS, 0, 0, tiled=True)]
    transpose x2 -> x0, matrix products: 19.9 us -> none  [kernel_grad(): return jnp.transpose(result, (2, 3, 4, 1, 0))]
    pallas_call x0 -> x7, Pallas kernels: none -> 15.6 us  [call(): pl.pallas_call(kernel, out_shape=[jax.ShapeDtypeStruct(s, d) for s, d in...]
    unnamed x23 -> x57, local copies, waits for them, and re-layouts: 26 us -> 17.4 us
  transfers between devices with their start and end apart: 6 -> 6, of which waited for: 5 -> 2; matrix products, arithmetic and copies ran while one was open for 10% -> 12% of each run, Pallas kernels for 0% -> 2%
where the time goes in v1:
time: 126 us; the launch traced here: 125 us
  blocking collectives  39.9 us (32%)
  local copies, waits for them, and re-layouts  31.8 us (25%)
  starting transfers between devices  25.9 us (21%)
  Pallas kernels  15.6 us (12%)
  waiting for transfers between devices  7.14 us (6%)
  other arithmetic  3.56 us (3%)
    all_to_all x1, blocking collectives, local(): lax.all_to_all(jnp.broadcast_to(summed[None], (8, HALF + 128, LANES)), 'z...  20.1 us
    all_to_all x1, blocking collectives, local(): planes = lax.all_to_all(mixed, PLANE, 0, 0, tiled=True)  19.8 us
    unnamed x57, local copies, waits for them, and re-layouts  17.4 us
    pallas_call x7, Pallas kernels, call(): pl.pallas_call(kernel, out_shape=[jax.ShapeDtypeStruct(s, d) for s, d in...  15.6 us
    all_to_all x1, starting transfers between devices, local(): gathered = lax.all_to_all(spread, SLABS, 0, 0, tiled=True)  11.5 us
    all_to_all x1, waiting for transfers between devices, local(): gathered = lax.all_to_all(spread, SLABS, 0, 0, tiled=True)  6.25 us
    ppermute x1, starting transfers between devices, local(): part = lax.ppermute(send, SLABS, forward)  4.93 us
    ppermute x1, starting transfers between devices, local(): next2 = lax.ppermute(slope2, SLABS, backward)  3.22 us
  transfers between devices with their start and end apart: 6, of which 2 were waited for; matrix products, arithmetic and copies ran while one was open for 12% of the time, Pallas kernels for 2%

profile of v1, /device:TPU:1, one launch (start us, length us, event | category | flops | bytes accessed | tf_op | source)
XLA Modules:
  0.0 124.7 jit_solution(15876645453314365486)
XLA Ops:
  0.6 1.7 %slice_bitcast_fusion = (bf16[3,3,2,32,64]{4,3,1,2,0:T(8,128)(2,1)}, bf16[3,64,3,2,32]{1,4,2,3,0:T(8,128)(2,1)S(1)}) fusion(bf16[3,3,3,64,32]{3,4,2,1,0:T(8,128)(2,1)} %param.15), kind=kLoop, calls=%fused_computation.6 | loop fusion | bytes 221184 | tf_op jit(solution)/shard_map/transpose | solution.py:415
  2.4 0.8 copy.46.w2_ref
  3.1 0.8 reshape.67
  4.0 1.1 reshape.69.v_ref
  5.1 1.2 copy-done.1
  6.3 0.9 copy-done.9
  7.2 3.1 %shard_map.154 = (bf16[320,2048]{1,0:T(8,128)(2,1)S(1)}, bf16[192,2048]{1,0:T(8,128)(2,1)S(1)}, bf16[2,64,2048]{2,1,0:T(8,128)(2,1)S(1)}, bf16[64,2048]{1,0:T(8,128)(2,1)}) custom-call(bf16[1024,512]{1,0:T(8,128)(2,1)S(1)} %copy-done.1, bf16[512,640]{1,0:T(8,128)(2,1)S(1)} %copy-done.4, bf16[32,128]{1,0:T(8,128)(2,1)S(1)} %pad.21.w1_ref, ...), custom_call_target="tpu_custom_call" | custom-call | flops 1000000000 | bytes 2883584 | tf_op jit(solution)/shard_map/pallas_call | solution.py:351
  10.4 4.9 %collective-permute-start.1 = (bf16[64,2048]{1,0:T(8,128)(2,1)}, bf16[64,2048]{1,0:T(8,128)(2,1)}, u32[]{:S(2)}, u32[]{:S(2)}) collective-permute-start(bf16[64,2048]{1,0:T(8,128)(2,1)} %get-tuple-element.29), channel_id=1, source_target_pairs={{0,1},{1,2},{2,3},{3,4},{4,5},{5,6},{6,7},{7,8},{8,9},{9,10},{10,1... | collective-permute-start | bytes 786440 | tf_op jit(solution)/shard_map/ppermute | solution.py:384
  15.3 1.8 %slice.34 = bf16[16,4,1,4,512]{4,3,2,1,0:T(4,128)(2,1)} slice(bf16[16,4,4,4,512]{4,3,2,1,0:T(4,128)(2,1)} %param.11), slice={[0:16], [0:4], [3:4], [0:4], [0:512]} | slice | bytes 524288 | tf_op jit(solution)/shard_map/slice | solution.py:370
  17.1 1.7 %reshape_squeeze.3 = bf16[256,512]{1,0:T(8,128)(2,1)} reshape(bf16[16,4,1,4,512]{4,3,2,1,0:T(4,128)(2,1)} %slice.34) | data formatting | bytes 524288 | tf_op jit(solution)/shard_map/reshape;squeeze | solution.py:370
  18.8 1.9 %collective-permute-start = (bf16[256,512]{1,0:T(8,128)(2,1)}, bf16[256,512]{1,0:T(8,128)(2,1)}, u32[]{:S(2)}, u32[]{:S(2)}) collective-permute-start(bf16[256,512]{1,0:T(8,128)(2,1)} %reshape_squeeze.3), channel_id=1, source_target_pairs={{0,1},{1,2},{2,3},{3,4},{4,5},{5,6},{6,7},{7,8},{8,9},{9,10},{10,1... | collective-permute-start | bytes 786440 | tf_op jit(solution)/shard_map/ppermute | solution.py:371
  20.7 0.7 copy.50
  21.4 1.4 %reduce-window.8 = s32[32,1]{1,0:T(8,128)} reduce-window(s32[32,1]{1,0:T(8,128)} %copy.50, s32[]{:T(128)} %constant.36.clone.1), window={size=32x1 pad=31_0x0_0}, to_apply=%region_0.1 | reduce-window | flops 992 | bytes 260 | tf_op jit(solution)/shard_map/reduce-window.3
  22.8 0.8 reduce
  23.9 0.9 copy.52
  25.5 0.9 copy-done.10
  26.4 0.8 copy-done.13
  27.2 3.8 %shard_map.155 = (bf16[80,2048]{1,0:T(8,128)(2,1)S(1)}, bf16[192,2048]{1,0:T(8,128)(2,1)S(1)}, bf16[2,64,2048]{2,1,0:T(8,128)(2,1)S(1)}, bf16[64,2048]{1,0:T(8,1...) custom-call(bf16[256,512]{1,0:T(8,128)(2,1)} %collective-permute-done.halo_ref, ...), custom_call_target="tpu_custom_call" | custom-call | flops 1000000000 | bytes 1906688 | tf_op jit(solution)/shard_map/pallas_call | solution.py:351
  31.1 0.9 copy-done.2
  32.0 0.8 copy-done.7
  32.8 0.7 copy-done.11
  34.1 3.2 %collective-permute-start.2 = (bf16[64,2048]{1,0:T(8,128)(2,1)}, bf16[64,2048]{1,0:T(8,128)(2,1)}, u32[]{:S(2)}, u32[]{:S(2)}) collective-permute-start(bf16[64,2048]{1,0:T(8,128)(2,1)} %get-tuple-element.33.slope2_ref), channel_id=1, source_target_pairs={{1,0},{2,1},{3,2},{4,3},{5,4},{6,5},{7,6},{8,7},{9,8},{10,9},{11,1... | collective-permute-start | bytes 786440 | tf_op jit(solution)/shard_map/ppermute | solution.py:394
  37.4 1.3 %copy.47 = bf16[64,32,128]{2,0,1:T(8,128)(2,1)S(1)} copy(bf16[64,32,128]{2,1,0:T(8,128)(2,1)} %bitcast.38) | data formatting | bytes 1048576 | tf_op jit(solution)/shard_map/reshape | solution.py:403
  39.4 11.5 %all-to-all-start = ((bf16[32,8,128]{2,1,0:T(8,128)(2,1)}), bf16[32,8,128]{2,1,0:T(8,128)(2,1)}, u32[]{:S(2)}, u32[]{:S(2)}) async-start(bf16[32,8,128]{2,1,0:T(8,128)(2,1)} %broadcast_in_dim.8), calls=%async_computation | async-start | bytes 131072 | tf_op jit(solution)/shard_map/all_to_all | solution.py:396
  50.9 0.7 pad_dynamic-slice_fusion.w1own_ref
  52.4 0.7 pad.24.w3_ref
  53.3 1.0 fusion.3.block_ref
  54.3 6.3 %all-to-all-done.g_ref = bf16[32,8,128]{2,1,0:T(8,128)(2,1)} async-done(((bf16[32,8,128]{2,1,0:T(8,128)(2,1)}), bf16[32,8,128]{2,1,0:T(8,128)(2,1)}, u32[]{:S(2)}, u32[]{:S(2)}) %all-to-all-start) | async-done | bytes 65568 | tf_op jit(solution)/shard_map/all_to_all | solution.py:396
  60.5 0.8 copy-done.15
  61.3 0.8 copy-done.16
  62.1 0.8 copy-done.17
  62.8 0.7 copy-done.19
  63.5 1.9 %shard_map.156 = (bf16[64,128]{1,0:T(8,128)(2,1)S(1)}, f32[128,16]{1,0:T(8,128)S(1)}) custom-call(bf16[32,8,128]{2,1,0:T(8,128)(2,1)} %all-to-all-done.g_ref, bf16[16,128]{1,0:T(8,128)(2,1)S(1)} %copy-done.19, bf16[2048,128]{1,0:T(8,128)(2,1)S(1)} %bitcast.35, bf16[128,128]{1,0:T(8,128)(2,1)S(1)} %copy-done.15, bf16[128,128]{1,0:T(8,128)(2,1)S(1)} %copy-done.16, ...), custom_call_target="tpu_custom_call" | custom-call | flops 100000000 | bytes 24576 | tf_op jit(solution)/shard_map/pallas_call | solution.py:351
  65.5 1.1 copy-done.3
  66.6 1.0 copy-done.8
  67.7 1.0 copy-done.12
  68.6 0.8 copy-done.14
  69.5 3.6 %shard_map.157 = (bf16[176,128]{1,0:T(8,128)(2,1)S(1)}, bf16[176,128]{1,0:T(8,128)(2,1)S(1)}) custom-call(s32[1]{0:T(128)} %bitcast.core_ref, f32[128,16]{1,0:T(8,128)S(1)} %get-tuple-element.32.gf_ref, bf16[64,2048]{1,0:T(8,128)(2,1)} %get-tuple-element.33.slope2_ref, bf16[64,2048]{1,0:T(8,128)(2,1)} %collective-permute-done.2.next2_ref, ...), custom_call_target="tpu_custom_call" | custom-call | flops 1000000000 | bytes 90112 | tf_op jit(solution)/shard_map/pallas_call | solution.py:351
  73.1 1.3 %collective-permute-start.3 = (bf16[176,128]{1,0:T(8,128)(2,1)S(1)}, bf16[176,128]{1,0:T(8,128)(2,1)S(1)}, u32[]{:S(2)}, u32[]{:S(2)}) collective-permute-start(bf16[176,128]{1,0:T(8,128)(2,1)S(1)} %get-tuple-element.39), channel_id=1, source_target_pairs={{0,1},{1,0},{2,3},{3,2},{4,5},{5,4},{6,7},{7,6},{8,9},{9,8},{10,11... | collective-permute-start | bytes 135176 | tf_op jit(solution)/shard_map/ppermute | solution.py:441
  74.5 0.9 collective-permute-done.3
  75.5 19.8 %all_to_all.15.in_ref = bf16[16,240,128]{2,1,0:T(8,128)(2,1)S(1)} all-to-all(bf16[16,240,128]{2,1,0:T(8,128)(2,1)S(1)} %broadcast_in_dim.10), channel_id=1, replica_groups=mesh['x'=4,'yl'=2,'yh'=2,'z'=8,'core'=2] {'x','yl','yh'}, dimensions={0} | all-to-all | bytes 1966080 | tf_op jit(solution)/shard_map/all_to_all | solution.py:445
  95.3 0.7 shard_map.158
  96.1 20.1 %all_to_all.16.in_ref = bf16[8,304,128]{2,1,0:T(8,128)(2,1)S(1)} all-to-all(bf16[8,304,128]{2,1,0:T(8,128)(2,1)S(1)} %broadcast_in_dim.11), channel_id=1, replica_groups=mesh['x'=4,'yl'=2,'yh'=2,'z'=8,'core'=2] {'z'}, dimensions={0} | all-to-all | bytes 1245184 | tf_op jit(solution)/shard_map/all_to_all | solution.py:452
  116.3 3.0 %collective-permute-start.4 = (bf16[1200,128]{1,0:T(8,128)(2,1)S(1)}, bf16[1200,128]{1,0:T(8,128)(2,1)S(1)}, u32[]{:S(2)}, u32[]{:S(2)}) collective-permute-start(bf16[1200,128]{1,0:T(8,128)(2,1)S(1)} %shard_map.159.mine_ref), channel_id=1, source_target_pairs={{0,1},{1,0},{2,3},{3,2},{4,5},{5,4},{6,7},{7,6},{8,9},{9,8},{10,11... | collective-permute-start | bytes 921608 | tf_op jit(solution)/shard_map/ppermute | solution.py:456
  119.2 0.7 copy.55
  120.6 2.3 %shard_map.160 = (f32[3,3,3,32,4]{4,3,2,1,0:T(8,128)S(1)}, f32[3,3,3,64,32]{4,3,2,1,0:T(8,128)S(1)}, f32[2048,128]{1,0:T(8,128)}) custom-call(s32[1]{0:T(128)} %bitcast.core_ref, bf16[1200,128]{1,0:T(8,128)(2,1)S(1)} %shard_map.159.mine_ref, bf16[1200,128]{1,0:T(8,128)(2,1)S(1)} %collective-permute-done.4.other_ref), custom_call_target="tpu_custom_call" | custom-call | flops 10000000 | bytes 1283584 | tf_op jit(solution)/shard_map/pallas_call | solution.py:351
  122.8 1.1 copy.54
  123.9 0.8 copy.53
  (60 shorter events, 4.4 us)
Async XLA Ops:
  0.6 3.3 %copy-start.20 = (bf16[16,4,4,4,512]{4,3,2,1,0:T(4,128)(2,1)S(1)}, bf16[16,4,4,4,512]{4,3,2,1,0:T(4,128)(2,1)}, u32[]{:S(2)}) copy-start(bf16[16,4,4,4,512]{4,3,2,1,0:T(4,128)(2,1)} %param.11) | copy-start | bytes 3145732
  2.3 2.8 %copy-start = (bf16[2,2,128,192]{3,2,1,0:T(8,128)(2,1)S(1)}, bf16[2,2,128,192]{3,2,1,0:T(8,128)(2,1)}, u32[]{:S(2)}) copy-start(bf16[2,2,128,192]{3,2,1,0:T(8,128)(2,1)} %constant.40.clone.own_ref) | copy-start | bytes 589828
  2.3 2.8 %copy-start.4 = (bf16[512,640]{1,0:T(8,128)(2,1)S(1)}, bf16[512,640]{1,0:T(8,128)(2,1)}, u32[]{:S(2)}) copy-start(bf16[512,640]{1,0:T(8,128)(2,1)} %constant.39.clone.split_ref) | copy-start | bytes 1966084
  5.1 1.2 copy-start.1
  6.3 0.9 copy-start.9
  7.2 13.5 %copy-start.24 = (s32[32]{0:T(128)S(1)}, s32[32]{0:T(128)}, u32[]{:S(2)}) copy-start(s32[32]{0:T(128)} %param.13) | copy-start | bytes 388
  10.4 20.7 %copy-start.5 = (bf16[2,64,2048]{2,1,0:T(8,128)(2,1)}, bf16[2,64,2048]{2,1,0:T(8,128)(2,1)S(1)}, u32[]{:S(2)}) copy-start(bf16[2,64,2048]{2,1,0:T(8,128)(2,1)S(1)} %get-tuple-element.35.s1b_ref) | copy-start | bytes 1572868
  10.4 15.1 %collective-permute-start.1 = (bf16[64,2048]{1,0:T(8,128)(2,1)}, bf16[64,2048]{1,0:T(8,128)(2,1)}, u32[]{:S(2)}, u32[]{:S(2)}) collective-permute-start(bf16[64,2048]{1,0:T(8,128)(2,1)} %get-tuple-element.29), channel_id=1, source_target_pairs={{0,1},{1,2},{2,3},{3,4},{4,5},{5,6},{6,7},{7,8},{8,9},{9,10},{10,1... | collective-permute-start | bytes 786440 | tf_op jit(solution)/shard_map/ppermute | solution.py:384
  18.8 6.7 %collective-permute-start = (bf16[256,512]{1,0:T(8,128)(2,1)}, bf16[256,512]{1,0:T(8,128)(2,1)}, u32[]{:S(2)}, u32[]{:S(2)}) collective-permute-start(bf16[256,512]{1,0:T(8,128)(2,1)} %reshape_squeeze.3), channel_id=1, source_target_pairs={{0,1},{1,2},{2,3},{3,4},{4,5},{5,6},{6,7},{7,8},{8,9},{9,10},{10,1... | collective-permute-start | bytes 786440 | tf_op jit(solution)/shard_map/ppermute | solution.py:371
  25.5 0.9 copy-start.10
  26.4 0.8 copy-start.13
  31.1 0.9 copy-start.2
  32.0 0.8 copy-start.7
  32.8 0.7 copy-start.11
  33.5 0.6 copy-start.18
  34.1 17.5 %copy-start.21 = (bf16[128,64]{0,1:T(8,128)(2,1)S(1)}, bf16[128,64]{0,1:T(8,128)(2,1)}, u32[]{:S(2)}) copy-start(bf16[128,64]{0,1:T(8,128)(2,1)} %param.17) | copy-start | bytes 49156
  34.1 18.2 %copy-start.23 = (bf16[64,4]{0,1:T(4,128)(2,1)S(1)}, bf16[64,4]{0,1:T(4,128)(2,1)}, u32[]{:S(2)}) copy-start(bf16[64,4]{0,1:T(4,128)(2,1)} %param.18) | copy-start | bytes 1540
  34.1 19.0 %copy-start.22 = (f32[16,4]{0,1:T(4,128)S(1)}, f32[16,4]{0,1:T(4,128)}, u32[]{:S(2)}) copy-start(f32[16,4]{0,1:T(4,128)} %param.12) | copy-start | bytes 772
  34.1 31.3 %collective-permute-start.2 = (bf16[64,2048]{1,0:T(8,128)(2,1)}, bf16[64,2048]{1,0:T(8,128)(2,1)}, u32[]{:S(2)}, u32[]{:S(2)}) collective-permute-start(bf16[64,2048]{1,0:T(8,128)(2,1)} %get-tuple-element.33.slope2_ref), channel_id=1, source_target_pairs={{1,0},{2,1},{3,2},{4,3},{5,4},{6,5},{7,6},{8,7},{9,8},{10,9},{11,1... | collective-permute-start | bytes 786440 | tf_op jit(solution)/shard_map/ppermute | solution.py:394
  37.4 28.1 %copy-start.6 = (bf16[2,64,2048]{2,1,0:T(8,128)(2,1)S(1)}, bf16[2,64,2048]{2,1,0:T(8,128)(2,1)}, u32[]{:S(2)}) copy-start(bf16[2,64,2048]{2,1,0:T(8,128)(2,1)} %copy-done.5) | copy-start | bytes 1572868
  39.4 21.2 %all-to-all-start = ((bf16[32,8,128]{2,1,0:T(8,128)(2,1)}), bf16[32,8,128]{2,1,0:T(8,128)(2,1)}, u32[]{:S(2)}, u32[]{:S(2)}) async-start(bf16[32,8,128]{2,1,0:T(8,128)(2,1)} %broadcast_in_dim.8), calls=%async_computation | async-start | bytes 131072 | tf_op jit(solution)/shard_map/all_to_all | solution.py:396
  60.5 0.8 copy-start.15
  61.3 0.8 copy-start.16
  62.1 0.8 copy-start.17
  62.8 0.7 copy-start.19
  65.5 1.1 copy-start.3
  66.6 1.0 copy-start.8
  67.7 1.0 copy-start.12
  68.6 0.8 copy-start.14
  73.1 2.2 %collective-permute-start.3 = (bf16[176,128]{1,0:T(8,128)(2,1)S(1)}, bf16[176,128]{1,0:T(8,128)(2,1)S(1)}, u32[]{:S(2)}, u32[]{:S(2)}) collective-permute-start(bf16[176,128]{1,0:T(8,128)(2,1)S(1)} %get-tuple-element.39), channel_id=1, source_target_pairs={{0,1},{1,0},{2,3},{3,2},{4,5},{5,4},{6,7},{7,6},{8,9},{9,8},{10,11... | collective-permute-start | bytes 135176 | tf_op jit(solution)/shard_map/ppermute | solution.py:441
  116.3 4.3 %collective-permute-start.4 = (bf16[1200,128]{1,0:T(8,128)(2,1)S(1)}, bf16[1200,128]{1,0:T(8,128)(2,1)S(1)}, u32[]{:S(2)}, u32[]{:S(2)}) collective-permute-start(bf16[1200,128]{1,0:T(8,128)(2,1)S(1)} %shard_map.159.mine_ref), channel_id=1, source_target_pairs={{0,1},{1,0},{2,3},{3,2},{4,5},{5,4},{6,7},{7,6},{8,9},{9,8},{10,11... | collective-permute-start | bytes 921608 | tf_op jit(solution)/shard_map/ppermute | solution.py:456

commit v2 on v1

v2 whole, which is shorter than its diff:
```python
import functools

import jax
import jax.numpy as jnp
import numpy as np
from jax import lax
from jax.experimental import pallas as pl
from jax.experimental.pallas import tpu as pltpu
from jax.sharding import Mesh
from jax.sharding import PartitionSpec as P

BF = jnp.bfloat16
F32 = jnp.float32
SLABS = ("yh", "z", "core")
DP = ("x", "yl")
COLUMN = ("yh", "z")
S = 16
LANES = 128
WIDE = S * LANES
CHUNK = 512
PART = 24
HALF = 8 * PART
BIG = 60 * 1024 * 1024
SMALL = 16 * 1024 * 1024

NN = (((1,), (0,)), ((), ()))
NT = (((1,), (1,)), ((), ()))
TN = (((0,), (0,)), ((), ()))


def mm(a, b, dims=NN):
    return lax.dot_general(a, b, dims, preferred_element_type=F32)


def mm_exact(a, b):
    return lax.dot_general(
        a, b, NN, preferred_element_type=F32, precision=lax.Precision.HIGHEST
    )


def leaky(v, t):
    return v * (0.65 + 0.35 * t)


def slope(v, t):
    return 0.65 + 0.35 * t + 0.35 * v * (1.0 - t * t)


@functools.cache
def split_matrix():
    m = np.zeros((512, 640), np.float32)
    for k, offset in enumerate((-1, 0, 1, 2, 3)):
        for i in range(128):
            if 4 * i + offset >= 0:
                m[4 * i + offset, k * 128 + i] = 1.0
    return m


@functools.cache
def band_matrices():
    own = np.zeros((2, 2, 108, 192), np.float32)
    rim = np.zeros((2, 108, 48), np.float32)
    own_back = np.zeros((2, 2, 128, 192), np.float32)
    rim_back = np.zeros((2, 128, 48), np.float32)
    for i in range(2):
        for j in range(2):
            for a in range(3):
                for b in range(3):
                    x, y = 2 * i + a - 1, 2 * j + b - 1
                    if y < 0:
                        continue
                    for e in range(3):
                        for c in range(4):
                            tap = (a * 3 + b) * 3 + e
                            if x >= 0:
                                col = ((e * 4 + c) * 4 + x) * 4 + y
                                own[i, j, tap * 4 + c, col] = 1.0
                                own_back[i, j, c * 32 + tap, col] = 1.0
                            else:
                                col = (e * 4 + c) * 4 + y
                                rim[j, tap * 4 + c, col] = 1.0
                                rim_back[j, c * 32 + tap, col] = 1.0
    return own, rim, own_back, rim_back


def lane_ids(shape):
    return lax.broadcasted_iota(jnp.int32, shape, len(shape) - 1)


def shift_up(x):
    parts = []
    for k in range(x.shape[1] // LANES):
        p = pltpu.roll(x[:, k * LANES : (k + 1) * LANES], 1, 1)
        parts.append(jnp.where(lane_ids(p.shape) == 0, 0.0, p))
    return jnp.concatenate(parts, axis=1)


def shift_down(x):
    parts = []
    for k in range(x.shape[1] // LANES):
        p = pltpu.roll(x[:, k * LANES : (k + 1) * LANES], LANES - 1, 1)
        parts.append(jnp.where(lane_ids(p.shape) == LANES - 1, 0.0, p))
    return jnp.concatenate(parts, axis=1)


class Feed:
    def __init__(self, sources, buffers, sems):
        self.copies = [
            pltpu.make_async_copy(s, b, sems.at[k])
            for k, (s, b) in enumerate(zip(sources, buffers, strict=True))
        ]
        self.buffers, self.done = buffers, set()
        for copy in self.copies:
            copy.start()

    def __getitem__(self, k):
        if k not in self.done:
            self.copies[k].wait()
            self.done.add(k)
        return self.buffers[k]


def call(kernel, outs, args, scalars=(), scratch=(), vmem=BIG, flops=10**8):
    args = [a if isinstance(a, tuple) else (a, 1) for a in args]
    n_in, n_sc, n_out = len(args), len(scalars), len(outs)
    pieces = [(k, p, a.shape[0] // n) for k, (a, n) in enumerate(args) for p in range(n)]
    early = [k for k, o in enumerate(outs) if o[2]]

    def body(*refs):
        scalar_refs, refs = refs[:n_sc], refs[n_sc:]
        ins, refs = refs[:n_in], refs[n_in:]
        out_refs, refs = refs[:n_out], refs[n_out:]
        buffers, refs = refs[:n_in], refs[n_in:]
        held, refs = refs[: len(early)], refs[len(early) :]
        in_sems, out_sems, extra = refs[0], refs[1], refs[2:]

        def cut(ref, k, p, size):
            return ref if args[k][1] == 1 else ref.at[pl.ds(p * size, size)]

        feed = Feed(
            [cut(ins[k], k, p, s) for k, p, s in pieces],
            [cut(buffers[k], k, p, s) for k, p, s in pieces],
            in_sems,
        )
        local_outs = list(out_refs)
        for n, k in enumerate(early):
            local_outs[k] = held[n]
        sent = []

        def send(k):
            n = early.index(k)
            copy = pltpu.make_async_copy(held[n], out_refs[k], out_sems.at[n])
            copy.start()
            sent.append(copy)

        kernel(scalar_refs, feed, local_outs, send, *extra)
        for copy in sent:
            copy.wait()

    size = sum(int(np.prod(o[0])) * jnp.dtype(o[1]).itemsize for o in outs)
    return pl.pallas_call(
        body,
        out_shape=[jax.ShapeDtypeStruct(o[0], o[1]) for o in outs],
        in_specs=[pl.BlockSpec(memory_space=pltpu.SMEM)] * n_sc
        + [pl.BlockSpec(memory_space=pl.ANY)] * n_in,
        out_specs=[
            pl.BlockSpec(memory_space=pl.ANY if o[2] else pltpu.VMEM) for o in outs
        ],
        scratch_shapes=[pltpu.VMEM(a.shape, a.dtype) for a, _ in args]
        + [pltpu.VMEM(outs[k][0], outs[k][1]) for k in early]
        + [pltpu.SemaphoreType.DMA((len(pieces),)), pltpu.SemaphoreType.DMA((max(len(early), 1),))]
        + list(scratch),
        compiler_params=pltpu.CompilerParams(vmem_limit_bytes=vmem),
        cost_estimate=pl.CostEstimate(flops=flops, bytes_accessed=size, transcendentals=0),
    )(*scalars, *[a for a, _ in args])


def store_plane(h, s, cols, a1_ref, slope_ref):
    t = jnp.tanh(h)
    act = leaky(h, t)
    slope_ref[s, :, cols] = slope(h, t).astype(BF)
    if s == 0:
        a1_ref[64:128, cols] = act.astype(BF)
    else:
        a1_ref[128:192, cols] = act.astype(BF)
        a1_ref[0:64, cols] = shift_up(act).astype(BF)


def taps_of(w2_ref, a):
    return jnp.concatenate([w2_ref[a, b, e] for e in range(3) for b in (1, 2)], axis=0)


def first_kernel(scalars, feed, outs, send):
    x4_ref, a1_ref, slope_ref, send_ref = outs
    split, w1, own = feed[4], feed[5], feed[6]
    taps = w1[...].reshape(108, 32)
    w = jnp.concatenate([mm(taps, own[1, j], TN).astype(BF) for j in range(2)], axis=0)
    for q in range(4):
        v = feed[q]
        rows = jnp.concatenate([v[n].reshape(64, 512) for n in range(4)], axis=0)
        d = mm(rows, split[...])
        for k in range(5):
            for n in range(4):
                x4_ref[k * 64 : (k + 1) * 64, (4 * q + n) * LANES : (4 * q + n + 1) * LANES] = d[
                    n * 64 : (n + 1) * 64, k * LANES : (k + 1) * LANES
                ].astype(BF)
    send(0)
    w2 = taps_of(feed[7], 0)
    for q in range(4):
        cols = slice(q * CHUNK, (q + 1) * CHUNK)
        for s in range(2):
            h = mm(w, x4_ref[s * 128 : s * 128 + 192, cols])
            store_plane(h, s, cols, a1_ref, slope_ref)
        send_ref[:, cols] = mm(w2, a1_ref[:, cols], TN).astype(BF)
    send(1)
    send(2)


def second_kernel(scalars, feed, outs, send, wide_ref):
    xh_ref, a1_ref, slope_ref, part_ref, wd1_ref, block_ref = outs
    halo, split, w1, own, rim, w2 = (feed[k] for k in range(6))
    taps = w1[...].reshape(108, 32)
    w = jnp.concatenate([mm(taps, own[0, j], TN).astype(BF) for j in range(2)], axis=0)
    wh = jnp.concatenate([mm(taps, rim[j], TN).astype(BF) for j in range(2)], axis=0)
    rows = jnp.concatenate([halo[n].reshape(16, 512) for n in range(S)], axis=0)
    d = mm(rows, split[...])
    for k in range(5):
        for n in range(S):
            xh_ref[k * 16 : (k + 1) * 16, n * LANES : (n + 1) * LANES] = d[
                n * 16 : (n + 1) * 16, k * LANES : (k + 1) * LANES
            ].astype(BF)
    send(0)
    w2a, w2b = taps_of(w2, 1), taps_of(w2, 2)
    x4, a1b = feed[6], feed[7]
    for q in range(4):
        cols = slice(q * CHUNK, (q + 1) * CHUNK)
        for s in range(2):
            h = mm(w, x4[s * 128 : s * 128 + 192, cols]) + mm(
                wh, xh_ref[s * 32 : s * 32 + 48, cols]
            )
            store_plane(h, s, cols, a1_ref, slope_ref)
        part_ref[:, cols] = mm(w2a, a1_ref[:, cols], TN) + mm(w2b, a1b[:, cols], TN)
    for k in (1, 2, 3):
        send(k)
    wide_ref[...] = feed[8][...].astype(F32)
    for x in range(32):
        wd1_ref[x * 64 : (x + 1) * 64] = wide_ref[pl.ds(x, 64, stride=32), :].astype(BF)
    wd1_ref[2048:2112] = jnp.zeros((64, LANES), BF)
    send(4)

    def tap(a, e):
        return jnp.concatenate([w2[a, 1, e], w2[a, 2, e]], axis=0)

    zero = jnp.zeros((64, 64), BF)
    for k, row in enumerate(
        (
            (tap(1, 1), zero, zero, zero),
            (tap(2, 1), tap(0, 1), zero, zero),
            (tap(1, 2), zero, tap(1, 0), zero),
            (tap(2, 2), tap(0, 2), tap(2, 0), tap(0, 0)),
        )
    ):
        block_ref[k * 64 : (k + 1) * 64] = jnp.concatenate(row, axis=1)
    send(5)


def third_kernel(scalars, feed, outs, send):
    slope2_ref, pay_ref, fown_ref = outs
    part, got = feed[0], feed[1]
    total = jnp.zeros((S, 64), F32)
    for q in range(4):
        cols = slice(q * CHUNK, (q + 1) * CHUNK)
        h2 = part[:, cols] + got[:, cols].astype(F32)
        t = jnp.tanh(h2)
        act2 = leaky(h2, t).astype(BF)
        slope2_ref[:, cols] = slope(h2, t).astype(BF)
        rows = lax.broadcasted_iota(jnp.int32, (S, CHUNK), 0)
        owner = lax.shift_right_logical(lane_ids((S, CHUNK)), 7) + 4 * q
        pick = jnp.where(rows == owner, 1.0, 0.0).astype(BF)
        total = total + mm(pick, act2, NT)
    feats = total * (1.0 / 128.0)
    pay = jnp.concatenate([feats[0:8], feats[8:16]], axis=1).astype(BF)
    for x in range(32):
        pay_ref[x] = pay
    fown_ref[...] = jnp.concatenate([feats, jnp.zeros((S, 64), F32)], axis=1).astype(BF)


def tail(scalars, feed, padded_ref):
    counts, position = scalars[0], scalars[1]
    ends = []
    for k in range(32):
        ends.append(counts[k] + (ends[-1] if k else 0))
    by_row = lax.broadcasted_iota(jnp.int32, (S, S), 0)
    by_col = lax.broadcasted_iota(jnp.int32, (S, S), 1)
    row_owner = jnp.zeros((S, S), jnp.int32)
    col_owner = jnp.zeros((S, S), jnp.int32)
    for end in ends:
        row_owner = row_owner + jnp.where(by_row >= end, 1, 0)
        col_owner = col_owner + jnp.where(by_col >= end, 1, 0)
    alike = jnp.where(row_owner == col_owner, 1.0, 0.0)
    same = alike / jnp.sum(alike, axis=1, keepdims=True)

    w2 = jnp.concatenate([feed[3][...], jnp.zeros((64, LANES), BF)], axis=0)
    padded_ref[...] = jnp.zeros((LANES, LANES), F32)
    padded_ref[64:68, 0:64] = feed[4][...].astype(F32)
    w3 = padded_ref[...].astype(BF)
    padded_ref[...] = jnp.zeros((LANES, LANES), F32)
    padded_ref[64:68, 0:S] = feed[5][...]
    goal = jnp.transpose(padded_ref[...], (1, 0))[0:S]

    low = lane_ids((8, LANES)) < 64
    g, pairs = feed[0], []
    for p in range(16):
        ga, gb = g[2 * p].astype(F32), g[2 * p + 1].astype(F32)
        lo = jnp.where(low, ga, pltpu.roll(gb, 64, 1))
        hi = jnp.where(low, pltpu.roll(ga, 64, 1), gb)
        pairs.append(jnp.concatenate([lo, hi], axis=0).astype(BF))
    feats = jnp.concatenate(pairs, axis=1)
    wd1 = feed[2]
    dense1 = mm(feats, wd1[0:2048])
    centred = dense1 - 0.5 * mm_exact(same, dense1)
    t1 = jnp.tanh(centred)
    out1 = leaky(centred, t1).astype(BF)
    dense2 = mm(out1, w2, NT)
    t2 = jnp.tanh(dense2)
    out2 = leaky(dense2, t2).astype(BF)
    diff = mm(out2, w3, NT) - goal
    loss = jnp.sum(jnp.sum(diff * diff, axis=1, keepdims=True), axis=0, keepdims=True) / 32.0
    gpred = (diff / 16.0).astype(BF)
    gdense2 = (mm(gpred, w3) * slope(dense2, t2)).astype(BF)
    gcentred = mm(gdense2, w2) * slope(centred, t1)
    gdense1 = (gcentred - 0.5 * mm_exact(same, gcentred)).astype(BF)
    at = pl.multiple_of(position[0] * 64, 64)
    gfeats = mm(wd1[pl.ds(at, LANES), :], gdense1, NT)
    return out1, out2, gpred, gdense2, gdense1, gfeats, loss


def split_loss(loss):
    high = loss.astype(BF).astype(F32)
    mid = (loss - high).astype(BF).astype(F32)
    return high, mid, loss - high - mid


def back_kernel(scalars, feed, outs, send, padded_ref, g_ref, h_ref, w_ref):
    keep_ref, give_ref, own_ref = outs
    core = scalars[2]
    out1, out2, gpred, gdense2, gdense1, gfeats, loss = tail(scalars, feed, padded_ref)
    gf = gfeats.astype(BF).astype(F32) * (1.0 / 128.0)
    slope2, next2, block = feed[6], feed[7], feed[8]
    s1 = (feed[9], feed[10])
    for q in range(4):
        cols = slice(q * CHUNK, (q + 1) * CHUNK)
        spread = jnp.concatenate(
            [
                jnp.broadcast_to(gf[:, 4 * q + n : 4 * q + n + 1], (128, LANES))
                for n in range(4)
            ],
            axis=1,
        )
        go = spread[0:64] * slope2[:, cols].astype(F32)
        gn = spread[64:128] * next2[:, cols].astype(F32)
        g_ref[0:64, cols] = go.astype(BF)
        g_ref[64:128, cols] = gn.astype(BF)
        g_ref[128:192, cols] = shift_down(go).astype(BF)
        g_ref[192:256, cols] = shift_down(gn).astype(BF)
        gact = mm(block[...], g_ref[:, cols])
        for s in range(2):
            for i in range(2):
                r = (2 * s + i) * 64
                h_ref[s, i * 64 : (i + 1) * 64, cols] = (
                    gact[r : r + 64] * s1[i][s, :, cols].astype(F32)
                ).astype(BF)
    a1a, a1b = feed[11], feed[12]
    w_ref[0:192] = mm(a1b[...], g_ref[0:128, :], NT)
    a1 = mm(a1a[...], g_ref[0:64, :], NT)
    w_ref[192:288] = jnp.concatenate([a1[0:96], a1[96:192]], axis=1)
    x4, xh = feed[13], feed[14]
    r = mm(x4[0:192, :], h_ref[0], NT) + mm(x4[128:320, :], h_ref[1], NT)
    rh = mm(xh[0:48, :], h_ref[0], NT) + mm(xh[32:80, :], h_ref[1], NT)
    own, rim = feed[15], feed[16]
    r_high, rh_high = r.astype(BF), rh.astype(BF)
    r_low, rh_low = (r - r_high.astype(F32)).astype(BF), (rh - rh_high.astype(F32)).astype(BF)
    group = lax.shift_right_logical(lane_ids((LANES, LANES)), 5)
    taps = jnp.zeros((LANES, LANES), F32)
    for i in range(2):
        for j in range(2):
            part = mm(own[i, j], r_high) + mm(own[i, j], r_low)
            if i == 0:
                part = part + mm(rim[j], rh_high) + mm(rim[j], rh_low)
            taps = jnp.where(group == 2 * i + j, part, taps)
    taps = taps + pltpu.roll(taps, 64, 1)
    taps = taps + pltpu.roll(taps, 32, 1)
    packed = taps[0:32]
    for c in range(1, 4):
        packed = jnp.where(group[0:32] == c, taps[c * 32 : (c + 1) * 32], packed)
    w_ref[288:320] = packed
    w_ref[320:384] = jnp.zeros((64, LANES), F32)
    first = core[0] == 0

    @pl.when(first)
    def _():
        keep_ref[...] = w_ref[0:HALF].astype(BF)
        give_ref[...] = w_ref[HALF : 2 * HALF].astype(BF)

    @pl.when(jnp.logical_not(first))
    def _():
        keep_ref[...] = w_ref[HALF : 2 * HALF].astype(BF)
        give_ref[...] = w_ref[0:HALF].astype(BF)

    own_ref[0:64] = mm(feed[1][...], gdense1, TN)[0:64].astype(BF)
    own_ref[64:128] = mm(gdense2, out1, TN)[0:64].astype(BF)
    d3 = mm(gpred, out2, TN)[64:72]
    lanes = lane_ids((8, LANES))
    top = lax.broadcasted_iota(jnp.int32, (8, LANES), 0) == 0
    for k, piece in enumerate(split_loss(loss)):
        d3 = jnp.where(jnp.logical_and(top, lanes == 64 + k), piece, d3)
    own_ref[128:136] = d3.astype(BF)
    own_ref[136:144] = jnp.zeros((8, LANES), BF)


def spread_kernel(scalars, feed, outs, send):
    (out_ref,) = outs
    keep, own, taken = feed[0], feed[1], feed[2]
    both = keep[...].astype(F32) + taken[...].astype(F32)
    mine = own[...].astype(F32)
    for k in range(8):
        out_ref[k] = jnp.concatenate(
            [
                both[k * PART : (k + 1) * PART],
                mine[128:136],
                mine[k * 8 : (k + 1) * 8],
                mine[64 + k * 8 : 72 + k * 8],
            ],
            axis=0,
        ).astype(BF)


def group_kernel(scalars, feed, outs, send):
    out_ref, d2_ref, d3_ref, loss_ref = outs
    got = feed[0]
    total = got[0].astype(F32)
    for k in range(1, 8):
        total = total + got[k].astype(F32)
    pay = jnp.concatenate([total[0:PART], total[32:40]], axis=0).astype(BF)
    for k in range(16):
        out_ref[k] = pay
    d2_ref[...] = total[40:48]
    small = total[PART:32]
    d3_ref[...] = small[0:4, 0:64]
    lanes = lane_ids((8, LANES))
    rows = lax.broadcasted_iota(jnp.int32, (8, LANES), 0)
    held = jnp.logical_and(jnp.logical_and(lanes >= 64, lanes < 67), rows == 0)
    values = jnp.where(held, small, 0.0)
    loss_ref[...] = jnp.sum(jnp.sum(values, axis=1, keepdims=True), axis=0, keepdims=True)


def column_kernel(scalars, feed, outs, send):
    (out_ref,) = outs
    got, d2 = feed[0], feed[1]
    blocks = [got[k].astype(F32) for k in range(16)]
    total = blocks[0][0:PART]
    for b in blocks[1:]:
        total = total + b[0:PART]
    pay = jnp.concatenate([total, d2[...]] + [b[PART:32] for b in blocks], axis=0).astype(BF)
    for k in range(8):
        out_ref[k] = pay


def last_kernel(scalars, feed, outs, send, w_ref, t_ref):
    gw1_ref, gw2_ref, gd1_ref, gd2_ref = outs
    mine, other = feed[0], feed[1]
    first = scalars[0][0] == 0
    for k in range(8):
        a, b = mine[k].astype(F32), other[k].astype(F32)
        low, high = jnp.where(first, a, b), jnp.where(first, b, a)
        w_ref[k * PART : (k + 1) * PART] = low[0:PART]
        w_ref[HALF + k * PART : HALF + (k + 1) * PART] = high[0:PART]
        gd2_ref[k * 8 : (k + 1) * 8] = a[PART:32]
        for slab in range(16):
            at = 32 + 8 * slab
            row = k * 256 + 2 * slab
            gd1_ref[pl.ds(row, 8, stride=32), :] = low[at : at + 8]
            gd1_ref[pl.ds(row + 1, 8, stride=32), :] = high[at : at + 8]
    send(2)
    for a in range(3):
        for e in range(3):
            gw2_ref[a, 0, e] = jnp.zeros((32, 64), F32)
            for b in (1, 2):
                at = e * 64 + (b - 1) * 32
                right = a == 0
                if a == 1:
                    right = at >= 96
                    at = 192 + at % 96
                block = w_ref[at : at + 32]
                if right:
                    block = pltpu.roll(block, 64, 1)
                gw2_ref[a, b, e] = block[:, 0:64]
    packed = w_ref[288:320]
    for c in range(4):
        t_ref[c * 32 : (c + 1) * 32] = pltpu.roll(packed, (LANES - 32 * c) % LANES, 1)
    for a in range(3):
        for b in range(3):
            for e in range(3):
                tap = (a * 3 + b) * 3 + e
                gw1_ref[a, b, e] = t_ref[pl.ds(tap, 4, stride=32), :][:, 0:32]


def local(volumes, targets, counts, w_conv1, w_conv2, w_dense1, w_dense2, w_dense3):
    core = lax.axis_index("core").astype(jnp.int32).reshape(1)
    position = lax.axis_index(SLABS).astype(jnp.int32).reshape(1)
    forward = [(i, i + 1) for i in range(31)]
    backward = [(i + 1, i) for i in range(31)]
    swap = [(0, 1), (1, 0)]
    split = jnp.asarray(split_matrix(), BF)
    own, rim, own_back, rim_back = (jnp.asarray(m, BF) for m in band_matrices())
    w1 = jnp.swapaxes(w_conv1, 3, 4).reshape(27, 4, 32)
    w2 = jnp.swapaxes(w_conv2, 3, 4)

    halo = lax.ppermute(volumes[:, :, 3], SLABS, forward)
    x4, a1b, s1b, away = call(
        first_kernel,
        [
            ((320, WIDE), BF, True), ((192, WIDE), BF, True), ((2, 64, WIDE), BF, True),
            ((64, WIDE), BF, False),
        ],
        ((volumes, 4), split, w1, own, w2),
        flops=10**9,
    )
    got = lax.ppermute(away, SLABS, forward)
    xh, a1a, s1a, part, wd1, block = call(
        second_kernel,
        [
            ((80, WIDE), BF, True), ((192, WIDE), BF, True), ((2, 64, WIDE), BF, True),
            ((64, WIDE), F32, True), ((2112, LANES), BF, True), ((256, 256), BF, True),
        ],
        (halo, split, w1, own, rim, w2, x4, a1b, w_dense1),
        scratch=[pltpu.VMEM((2048, LANES), F32)],
        flops=2 * 10**9,
    )
    slope2, pay, fown = call(
        third_kernel,
        [((64, WIDE), BF, False), ((32, 8, LANES), BF, False), ((S, LANES), BF, False)],
        (part, got),
    )
    gathered = lax.all_to_all(pay, SLABS, 0, 0, tiled=True)
    next2 = lax.ppermute(slope2, SLABS, backward)
    keep, give, mine = call(
        back_kernel,
        [((HALF, LANES), BF, False), ((HALF, LANES), BF, False), ((144, LANES), BF, False)],
        (
            gathered, fown, wd1, w_dense2.T, w_dense3.T, targets.T, slope2, next2, block,
            s1a, s1b, a1a, a1b, x4, xh, own_back, rim_back,
        ),
        scalars=(counts, position, core),
        scratch=[
            pltpu.VMEM((LANES, LANES), F32), pltpu.VMEM((256, WIDE), BF),
            pltpu.VMEM((2, 128, WIDE), BF), pltpu.VMEM((2 * HALF, LANES), F32),
        ],
        flops=2 * 10**9,
    )
    taken = lax.ppermute(give, "core", swap)
    (scattered,) = call(
        spread_kernel, [((8, 48, LANES), BF, False)], (keep, mine, taken), vmem=SMALL
    )
    over_dp = lax.all_to_all(scattered, DP, 0, 0, tiled=True)
    to_column, d2, d3, loss = call(
        group_kernel,
        [((16, 32, LANES), BF, False), ((8, LANES), F32, False), ((4, 64), F32, False), ((1, 1), F32, False)],
        (over_dp,),
        vmem=SMALL,
    )
    over_column = lax.all_to_all(to_column, COLUMN, 0, 0, tiled=True)
    (back,) = call(
        column_kernel, [((8, 160, LANES), BF, False)], (over_column, d2), vmem=SMALL
    )
    summed = lax.all_to_all(back, DP, 0, 0, tiled=True)
    other = lax.ppermute(summed, "core", swap)
    gw1, gw2, gd1, gd2 = call(
        last_kernel,
        [
            ((3, 3, 3, 4, 32), F32, False), ((3, 3, 3, 32, 64), F32, False),
            ((2048, LANES), F32, True), ((64, LANES), F32, False),
        ],
        (summed, other),
        scalars=(core,),
        scratch=[pltpu.VMEM((2 * HALF, LANES), F32), pltpu.VMEM((LANES, LANES), F32)],
        vmem=SMALL,
    )
    return (
        loss.reshape(()), jnp.swapaxes(gw1, 3, 4), jnp.swapaxes(gw2, 3, 4), gd1, gd2.T, d3.T,
    )


def solution(mesh):
    fine = Mesh(mesh.devices.reshape(4, 2, 2, 8, 2), ("x", "yl", "yh", "z", "core"))
    placed = (P(DP, None, SLABS, None, None), P(DP, None), P(), P(), P(), P(), P(), P())
    return jax.shard_map(
        local, mesh=fine, in_specs=placed, out_specs=(P(), P(), P(), P(), P(), P()), check_vma=False
    )
```

time: 126 us -> 99.3 us (0.79)
  local copies, waits for them, and re-layouts: 31.8 us -> 4.74 us
  blocking collectives: 39.9 us -> 29.7 us
  Pallas kernels: 15.6 us -> 24.5 us
  waiting for transfers between devices: 7.14 us -> 11.9 us
  other arithmetic: 3.56 us -> 0 us
    unnamed x57 -> x12, local copies, waits for them, and re-layouts: 17.4 us -> 3.69 us
    all_to_all x2 -> x3, blocking collectives: 39.9 us -> 29.7 us  [the longest x1 11.5 us: local(): over_column = lax.all_to_all(to_column, COLUMN, 0, 0, tiled=True)]
    pallas_call x7 -> x8, Pallas kernels: 15.6 us -> 24.5 us  [call(): pl.pallas_call(body, out_shape=[jax.ShapeDtypeStruct(o[0], o[1]) for o in...]
    reshape x5 -> x0, local copies, waits for them, and re-layouts: 4.03 us -> none  [the longest x1 1.31 us: local(): w_dense1.reshape(64, slabs, 128)]
    all_to_all x1, waiting for transfers between devices: 6.25 us -> 9.57 us  [local(): gathered = lax.all_to_all(pay, SLABS, 0, 0, tiled=True)]
    transpose x3 -> x0, local copies, waits for them, and re-layouts: 2.64 us -> none  [the longest x2 2.63 us: local(): w2t = jnp.transpose(w_conv2[:, 1:], (0, 2, 1, 4, 3)).reshape(3, 3, 64, 64)]
    another operation x2 -> x0, local copies, waits for them, and re-layouts: 2.41 us -> none  [the longest x1 1.72 us: local(): rim = volumes[:, :, 3].reshape(256, 512)]
    another operation x2 -> x0, other arithmetic: 2.19 us -> none
  transfers between devices with their start and end apart: 6 -> 6, of which waited for: 2 -> 3; matrix products, arithmetic and copies ran while one was open for 12% -> 0% of each run, Pallas kernels for 2% -> 12%
where the time goes in v2:
time: 99.3 us; the launch traced here: 98.7 us
  blocking collectives  29.7 us (30%)
  starting transfers between devices  27 us (27%)
  Pallas kernels  24.5 us (25%)
  waiting for transfers between devices  11.9 us (12%)
  local copies, waits for them, and re-layouts  4.74 us (5%)
    pallas_call x8, Pallas kernels, call(): pl.pallas_call(body, out_shape=[jax.ShapeDtypeStruct(o[0], o[1]) for o in...  24.5 us
    all_to_all x1, starting transfers between devices, local(): gathered = lax.all_to_all(pay, SLABS, 0, 0, tiled=True)  12.2 us
    all_to_all x1, blocking collectives, local(): over_column = lax.all_to_all(to_column, COLUMN, 0, 0, tiled=True)  11.5 us
    all_to_all x1, waiting for transfers between devices, local(): gathered = lax.all_to_all(pay, SLABS, 0, 0, tiled=True)  9.57 us
    all_to_all x1, blocking collectives, local(): over_dp = lax.all_to_all(scattered, DP, 0, 0, tiled=True)  9.17 us
    all_to_all x1, blocking collectives, local(): summed = lax.all_to_all(back, DP, 0, 0, tiled=True)  9.03 us
    ppermute x1, starting transfers between devices, local(): halo = lax.ppermute(volumes[:, :, 3], SLABS, forward)  4.94 us
    ppermute x1, starting transfers between devices, local(): other = lax.ppermute(summed, 'core', swap)  4.23 us
  transfers between devices with their start and end apart: 6, of which 3 were waited for; matrix products, arithmetic and copies ran while one was open for 0% of the time, Pallas kernels for 12%

profile of v2, /device:TPU:1, one launch (start us, length us, event | category | flops | bytes accessed | tf_op | source)
XLA Modules:
  0.0 98.7 jit_solution(524761340063415456)
XLA Ops:
  0.6 1.1 %slice_bitcast_fusion = bf16[16,4,4,512]{3,2,1,0:T(4,128)(2,1)S(1)} fusion(bf16[16,4,4,4,512]{4,3,2,1,0:T(4,128)(2,1)} %refs_0_.2), kind=kLoop, calls=%fused_computation | loop fusion | bytes 524288 | tf_op jit(solution)/shard_map/squeeze | solution.py:519
  1.7 4.9 %collective-permute-start = (bf16[16,4,4,512]{3,2,1,0:T(4,128)(2,1)S(1)}, bf16[16,4,4,512]{3,2,1,0:T(4,128)(2,1)S(1)}, u32[]{:S(2)}, u32[]{:S(2)}) collective-permute-start(bf16[16,4,4,512]{3,2,1,0:T(4,128)(2,1)S(1)} %slice_bitcast_fusion), channel_id=1, source_target_pairs={{0,1},{1,2},{2,3},{3,4},{4,5},{5,6},{6,7},{7,8},{8,9},{9,10},{10,1... | collective-permute-start | bytes 786440 | tf_op jit(solution)/shard_map/ppermute | solution.py:519
  6.6 6.4 %shard_map.172 = (bf16[320,2048]{1,0:T(8,128)(2,1)}, bf16[192,2048]{1,0:T(8,128)(2,1)}, bf16[2,64,2048]{2,1,0:T(8,128)(2,1)}, bf16[64,2048]{1,0:T(8,128)(2,1)}) custom-call(bf16[16,4,4,4,512]{4,3,2,1,0:T(4,128)(2,1)} %refs_0_.2, bf16[512,640]{1,0:T(8,128)(2,1)} %constant.26.clone.refs_1_, bf16[27,4,32]{2,1,0:T(4,128)(2,1)} %bitcast.23, ...), custom_call_target="tpu_custom_call" | custom-call | flops 1000000000 | bytes 2883584 | tf_op jit(solution)/shard_map/pallas_call | solution.py:161
  13.0 1.9 %collective-permute-start.1 = (bf16[64,2048]{1,0:T(8,128)(2,1)}, bf16[64,2048]{1,0:T(8,128)(2,1)S(1)}, u32[]{:S(2)}, u32[]{:S(2)}) collective-permute-start(bf16[64,2048]{1,0:T(8,128)(2,1)} %get-tuple-element.33), channel_id=1, source_target_pairs={{0,1},{1,2},{2,3},{3,4},{4,5},{5,6},{6,7},{7,8},{8,9},{9,10},{10,1... | collective-permute-start | bytes 786440 | tf_op jit(solution)/shard_map/ppermute | solution.py:529
  15.0 0.0 collective-permute-done.refs_0_
  15.0 0.0 copy-start.5
  15.0 0.7 copy-done.5
  15.7 5.2 %shard_map.173 = (bf16[80,2048]{1,0:T(8,128)(2,1)}, bf16[192,2048]{1,0:T(8,128)(2,1)}, bf16[2,64,2048]{2,1,0:T(8,128)(2,1)}, f32[64,2048]{1,0:T(8,128)}, bf16[21...) custom-call(bf16[16,4,4,512]{3,2,1,0:T(4,128)(2,1)} %copy-done.5, bf16[512,640]{1,0:T(8,128)(2,1)} %constant.26.clone.refs_1_, ...), custom_call_target="tpu_custom_call" | custom-call | flops 2000000000 | bytes 2834432 | tf_op jit(solution)/shard_map/pallas_call | solution.py:161
  20.9 0.0 collective-permute-done.1.refs_1_
  20.9 0.0 copy-start.2
  20.9 0.7 copy-done.2
  21.6 2.2 %shard_map.174 = (bf16[64,2048]{1,0:T(8,128)(2,1)}, bf16[32,8,128]{2,1,0:T(8,128)(2,1)}, bf16[16,128]{1,0:T(8,128)(2,1)}) custom-call(f32[64,2048]{1,0:T(8,128)} %get-tuple-element.32.refs_0_, bf16[64,2048]{1,0:T(8,128)(2,1)} %copy-done.2), custom_call_target="tpu_custom_call" | custom-call | flops 100000000 | bytes 331776 | tf_op jit(solution)/shard_map/pallas_call | solution.py:161
  23.8 2.4 %collective-permute-start.2 = (bf16[64,2048]{1,0:T(8,128)(2,1)}, bf16[64,2048]{1,0:T(8,128)(2,1)S(1)}, u32[]{:S(2)}, u32[]{:S(2)}) collective-permute-start(bf16[64,2048]{1,0:T(8,128)(2,1)} %get-tuple-element.37.refs_9_), channel_id=1, source_target_pairs={{1,0},{2,1},{3,2},{4,3},{5,4},{6,5},{7,6},{8,7},{9,8},{10,9},{11,1... | collective-permute-start | bytes 786440 | tf_op jit(solution)/shard_map/ppermute | solution.py:546
  26.2 12.2 %all-to-all-start = ((bf16[32,8,128]{2,1,0:T(8,128)(2,1)}), bf16[32,8,128]{2,1,0:T(8,128)(2,1)S(1)}, u32[]{:S(2)}, u32[]{:S(2)}) async-start(bf16[32,8,128]{2,1,0:T(8,128)(2,1)} %get-tuple-element.34), calls=%async_computation | async-start | bytes 131072 | tf_op jit(solution)/shard_map/all_to_all | solution.py:545
  38.4 9.6 %all-to-all-done.refs_3_ = bf16[32,8,128]{2,1,0:T(8,128)(2,1)S(1)} async-done(((bf16[32,8,128]{2,1,0:T(8,128)(2,1)}), bf16[32,8,128]{2,1,0:T(8,128)(2,1)S(1)}, u32[]{:S(2)}, u32[]{:S(2)}) %all-to-all-start) | async-done | bytes 65568 | tf_op jit(solution)/shard_map/all_to_all | solution.py:545
  48.0 0.0 copy-start.3
  48.0 0.0 collective-permute-done.2.refs_10_
  48.0 0.0 copy-start.4
  48.0 0.6 copy-done.3
  48.6 0.1 copy-done.4
  48.7 7.0 %shard_map.175 = (bf16[192,128]{1,0:T(8,128)(2,1)}, bf16[192,128]{1,0:T(8,128)(2,1)}, bf16[144,128]{1,0:T(8,128)(2,1)}) custom-call(s32[32]{0:T(128)} %refs_0_.3, s32[1]{0:T(128)} %bitcast.refs_1_, s32[1]{0:T(128)} %bitcast.1.refs_2_.refs_0_, bf16[32,8,128]{2,1,0:T(8,128)(2,1)} %copy-done.3, bf16[16,128]{1,0:T(8,128)(2,1)} %get-tuple-element.35.refs_4_, ...), custom_call_target="tpu_custom_call" | custom-call | flops 2000000000 | bytes 135168 | tf_op jit(solution)/shard_map/pallas_call | solution.py:161
  55.7 1.3 %collective-permute-start.3 = (bf16[192,128]{1,0:T(8,128)(2,1)}, bf16[192,128]{1,0:T(8,128)(2,1)S(1)}, u32[]{:S(2)}, u32[]{:S(2)}) collective-permute-start(bf16[192,128]{1,0:T(8,128)(2,1)} %get-tuple-element.45), channel_id=1, source_target_pairs={{0,1},{1,0},{2,3},{3,2},{4,5},{5,4},{6,7},{7,6},{8,9},{9,8},{10,11... | collective-permute-start | bytes 147464 | tf_op jit(solution)/shard_map/ppermute | solution.py:561
  57.1 1.1 %collective-permute-done.3.refs_2_ = bf16[192,128]{1,0:T(8,128)(2,1)S(1)} collective-permute-done((bf16[192,128]{1,0:T(8,128)(2,1)}, bf16[192,128]{1,0:T(8,128)(2,1)S(1)}, u32[]{:S(2)}, u32[]{:S(2)}) %collective-permute-start.3) | collective-permute-done | bytes 49184 | tf_op jit(solution)/shard_map/ppermute | solution.py:561
  58.2 0.0 copy-start
  58.2 0.8 copy-done
  59.0 0.0 copy-start.1
  59.0 0.8 copy-done.1
  59.7 0.2 shard_map.176
  59.9 9.2 %all_to_all.20.refs_0_ = bf16[8,48,128]{2,1,0:T(8,128)(2,1)S(1)} all-to-all(bf16[8,48,128]{2,1,0:T(8,128)(2,1)S(1)} %shard_map.176), channel_id=1, replica_groups=mesh['x'=4,'yl'=2,'yh'=2,'z'=8,'core'=2] {'x','yl'}, dimensions={0} | all-to-all | bytes 196608 | tf_op jit(solution)/shard_map/all_to_all | solution.py:565
  69.1 0.7 shard_map.177
  69.8 11.5 %all_to_all.21.refs_0_ = bf16[16,32,128]{2,1,0:T(8,128)(2,1)S(1)} all-to-all(bf16[16,32,128]{2,1,0:T(8,128)(2,1)S(1)} %get-tuple-element.47), channel_id=1, replica_groups=mesh['x'=4,'yl'=2,'yh'=2,'z'=8,'core'=2] {'yh','z'}, dimensions={0} | all-to-all | bytes 262144 | tf_op jit(solution)/shard_map/all_to_all | solution.py:572
  81.4 0.2 shard_map.178
  81.6 9.0 %all_to_all.22.refs_1_ = bf16[8,160,128]{2,1,0:T(8,128)(2,1)S(1)} all-to-all(bf16[8,160,128]{2,1,0:T(8,128)(2,1)S(1)} %shard_map.178), channel_id=1, replica_groups=mesh['x'=4,'yl'=2,'yh'=2,'z'=8,'core'=2] {'x','yl'}, dimensions={0} | all-to-all | bytes 655360 | tf_op jit(solution)/shard_map/all_to_all | solution.py:576
  90.6 4.2 %collective-permute-start.4 = (bf16[8,160,128]{2,1,0:T(8,128)(2,1)S(1)}, bf16[8,160,128]{2,1,0:T(8,128)(2,1)S(1)}, u32[]{:S(2)}, u32[]{:S(2)}) collective-permute-start(bf16[8,160,128]{2,1,0:T(8,128)(2,1)S(1)} %all_to_all.22.refs_1_), channel_id=1, source_target_pairs={{0,1},{1,0},{2,3},{3,2},{4,5},{5,4},{6,7},{7,6},{8,9},{9,8},{10,11... | collective-permute-start | bytes 983048 | tf_op jit(solution)/shard_map/ppermute | solution.py:577
  94.8 1.3 %collective-permute-done.4.refs_2_ = bf16[8,160,128]{2,1,0:T(8,128)(2,1)S(1)} collective-permute-done((bf16[8,160,128]{2,1,0:T(8,128)(2,1)S(1)}, bf16[8,160,128]{2,1,0:T(8,128)(2,1)S(1)}, u32[]{:S(2)}, u32[]{:S(2)}) %collective-permute-start.4) | collective-permute-done | bytes 327712 | tf_op jit(solution)/shard_map/ppermute | solution.py:577
  96.1 2.6 %shard_map.179 = (f32[3,3,3,4,32]{4,3,2,1,0:T(4,128)}, f32[3,3,3,32,64]{4,3,2,1,0:T(8,128)}, f32[2048,128]{1,0:T(8,128)}, f32[64,128]{1,0:T(8,128)}) custom-call(s32[1]{0:T(128)} %bitcast.1.refs_2_.refs_0_, bf16[8,160,128]{2,1,0:T(8,128)(2,1)S(1)} %all_to_all.22.refs_1_, bf16[8,160,128]{2,1,0:T(8,128)(2,1)S(1)} %collective-permute-done.4.refs_2_), custom_call_target="tpu_custom_call" | custom-call | flops 100000000 | bytes 1316352 | tf_op jit(solution)/shard_map/pallas_call | solution.py:161
Async XLA Ops:
  1.7 13.3 %collective-permute-start = (bf16[16,4,4,512]{3,2,1,0:T(4,128)(2,1)S(1)}, bf16[16,4,4,512]{3,2,1,0:T(4,128)(2,1)S(1)}, u32[]{:S(2)}, u32[]{:S(2)}) collective-permute-start(bf16[16,4,4,512]{3,2,1,0:T(4,128)(2,1)S(1)} %slice_bitcast_fusion), channel_id=1, source_target_pairs={{0,1},{1,2},{2,3},{3,4},{4,5},{5,6},{6,7},{7,8},{8,9},{9,10},{10,1... | collective-permute-start | bytes 786440 | tf_op jit(solution)/shard_map/ppermute | solution.py:519
  13.0 7.9 %collective-permute-start.1 = (bf16[64,2048]{1,0:T(8,128)(2,1)}, bf16[64,2048]{1,0:T(8,128)(2,1)S(1)}, u32[]{:S(2)}, u32[]{:S(2)}) collective-permute-start(bf16[64,2048]{1,0:T(8,128)(2,1)} %get-tuple-element.33), channel_id=1, source_target_pairs={{0,1},{1,2},{2,3},{3,4},{4,5},{5,6},{6,7},{7,8},{8,9},{9,10},{10,1... | collective-permute-start | bytes 786440 | tf_op jit(solution)/shard_map/ppermute | solution.py:529
  15.0 0.7 copy-start.5
  20.9 0.7 copy-start.2
  23.8 24.2 %collective-permute-start.2 = (bf16[64,2048]{1,0:T(8,128)(2,1)}, bf16[64,2048]{1,0:T(8,128)(2,1)S(1)}, u32[]{:S(2)}, u32[]{:S(2)}) collective-permute-start(bf16[64,2048]{1,0:T(8,128)(2,1)} %get-tuple-element.37.refs_9_), channel_id=1, source_target_pairs={{1,0},{2,1},{3,2},{4,3},{5,4},{6,5},{7,6},{8,7},{9,8},{10,9},{11,1... | collective-permute-start | bytes 786440 | tf_op jit(solution)/shard_map/ppermute | solution.py:546
  26.2 21.8 %all-to-all-start = ((bf16[32,8,128]{2,1,0:T(8,128)(2,1)}), bf16[32,8,128]{2,1,0:T(8,128)(2,1)S(1)}, u32[]{:S(2)}, u32[]{:S(2)}) async-start(bf16[32,8,128]{2,1,0:T(8,128)(2,1)} %get-tuple-element.34), calls=%async_computation | async-start | bytes 131072 | tf_op jit(solution)/shard_map/all_to_all | solution.py:545
  48.0 0.6 copy-start.3
  48.0 0.7 copy-start.4
  55.7 2.4 %collective-permute-start.3 = (bf16[192,128]{1,0:T(8,128)(2,1)}, bf16[192,128]{1,0:T(8,128)(2,1)S(1)}, u32[]{:S(2)}, u32[]{:S(2)}) collective-permute-start(bf16[192,128]{1,0:T(8,128)(2,1)} %get-tuple-element.45), channel_id=1, source_target_pairs={{0,1},{1,0},{2,3},{3,2},{4,5},{5,4},{6,7},{7,6},{8,9},{9,8},{10,11... | collective-permute-start | bytes 147464 | tf_op jit(solution)/shard_map/ppermute | solution.py:561
  58.2 0.8 copy-start
  59.0 0.8 copy-start.1
  90.6 5.5 %collective-permute-start.4 = (bf16[8,160,128]{2,1,0:T(8,128)(2,1)S(1)}, bf16[8,160,128]{2,1,0:T(8,128)(2,1)S(1)}, u32[]{:S(2)}, u32[]{:S(2)}) collective-permute-start(bf16[8,160,128]{2,1,0:T(8,128)(2,1)S(1)} %all_to_all.22.refs_1_), channel_id=1, source_target_pairs={{0,1},{1,0},{2,3},{3,2},{4,5},{5,4},{6,7},{7,6},{8,9},{9,8},{10,11... | collective-permute-start | bytes 983048 | tf_op jit(solution)/shard_map/ppermute | solution.py:577

commit v3 on v2

v3 whole, which is shorter than its diff:
```python
import functools

import jax
import jax.numpy as jnp
import numpy as np
from jax import lax
from jax.experimental import pallas as pl
from jax.experimental.pallas import tpu as pltpu
from jax.sharding import Mesh
from jax.sharding import PartitionSpec as P

BF = jnp.bfloat16
F32 = jnp.float32
SLABS = ("yh", "z", "core")
DP = ("x", "yl")
COLUMN = ("yh", "z")
S = 16
LANES = 128
WIDE = S * LANES
CHUNK = 512
PART = 24
SMALL = 16 * 1024 * 1024

NN = (((1,), (0,)), ((), ()))
NT = (((1,), (1,)), ((), ()))
TN = (((0,), (0,)), ((), ()))


def mm(a, b, dims=NN):
    return lax.dot_general(a, b, dims, preferred_element_type=F32)


def mm_exact(a, b):
    return lax.dot_general(
        a, b, NN, preferred_element_type=F32, precision=lax.Precision.HIGHEST
    )


def leaky(v, t):
    return v * (0.65 + 0.35 * t)


def slope(v, t):
    return 0.65 + 0.35 * t + 0.35 * v * (1.0 - t * t)


@functools.cache
def split_matrix():
    m = np.zeros((512, 640), np.float32)
    for k, offset in enumerate((-1, 0, 1, 2, 3)):
        for i in range(128):
            if 4 * i + offset >= 0:
                m[4 * i + offset, k * 128 + i] = 1.0
    return m


@functools.cache
def band_matrices():
    own = np.zeros((2, 2, 108, 192), np.float32)
    rim = np.zeros((2, 108, 48), np.float32)
    for i in range(2):
        for j in range(2):
            for a in range(3):
                for b in range(3):
                    x, y = 2 * i + a - 1, 2 * j + b - 1
                    if y < 0:
                        continue
                    for e in range(3):
                        for c in range(4):
                            src = ((a * 3 + b) * 3 + e) * 4 + c
                            if x >= 0:
                                own[i, j, src, ((e * 4 + c) * 4 + x) * 4 + y] = 1.0
                            else:
                                rim[j, src, (e * 4 + c) * 4 + y] = 1.0
    return own, rim


def lane_ids(shape):
    return lax.broadcasted_iota(jnp.int32, shape, len(shape) - 1)


def shift_up(x):
    parts = []
    for k in range(x.shape[1] // LANES):
        p = pltpu.roll(x[:, k * LANES : (k + 1) * LANES], 1, 1)
        parts.append(jnp.where(lane_ids(p.shape) == 0, 0.0, p))
    return jnp.concatenate(parts, axis=1)


def shift_down(x):
    parts = []
    for k in range(x.shape[1] // LANES):
        p = pltpu.roll(x[:, k * LANES : (k + 1) * LANES], LANES - 1, 1)
        parts.append(jnp.where(lane_ids(p.shape) == LANES - 1, 0.0, p))
    return jnp.concatenate(parts, axis=1)


def call(kernel, outs, args, scalars=(), scratch=(), vmem=SMALL, flops=10**8):
    size = sum(int(np.prod(s)) * jnp.dtype(d).itemsize for s, d in outs)
    return pl.pallas_call(
        kernel,
        out_shape=[jax.ShapeDtypeStruct(s, d) for s, d in outs],
        in_specs=[pl.BlockSpec(memory_space=pltpu.SMEM)] * len(scalars)
        + [pl.BlockSpec(memory_space=pltpu.VMEM)] * len(args),
        out_specs=[pl.BlockSpec(memory_space=pltpu.VMEM)] * len(outs),
        scratch_shapes=list(scratch),
        compiler_params=pltpu.CompilerParams(vmem_limit_bytes=vmem),
        cost_estimate=pl.CostEstimate(flops=flops, bytes_accessed=size, transcendentals=0),
    )(*scalars, *args)


def parts(ref, *heights):
    out, at = [], 0
    for h in heights:
        out.append(ref.at[at : at + h])
        at += h
    return out


def bands(taps, ref, *index):
    return jnp.concatenate([mm(taps, ref[(*index, j)], TN).astype(BF) for j in range(2)], axis=0)


def split_here():
    z = lax.broadcasted_iota(jnp.int32, (512, LANES), 0)
    m = lax.broadcasted_iota(jnp.int32, (512, LANES), 1)
    return jnp.concatenate(
        [jnp.where(z - 4 * m == k - 1, 1.0, 0.0).astype(BF) for k in range(5)], axis=1
    )


def band_here(i, j):
    row = lax.broadcasted_iota(jnp.int32, (108, 1), 0)
    tap = lax.shift_right_logical(row, 2)
    third = lax.shift_right_logical(tap * 43, 7)
    a = lax.shift_right_logical(third * 43, 7)
    e, b = tap - 3 * third, third - 3 * a
    row_key = (e * 4 + jnp.bitwise_and(row, 3)) * 64 + a * 8 + b
    col = lax.broadcasted_iota(jnp.int32, (1, 192), 1)
    x = jnp.bitwise_and(lax.shift_right_logical(col, 2), 3) - 2 * i + 1
    y = jnp.bitwise_and(col, 3) - 2 * j + 1
    col_key = lax.shift_right_logical(col, 4) * 64 + x * 8 + y
    return jnp.where(row_key == col_key, 1.0, 0.0).astype(BF)


def store_plane(h, s, cols, a1_ref, slope_ref):
    t = jnp.tanh(h)
    act = leaky(h, t)
    slope_ref[s * 64 : (s + 1) * 64, cols] = slope(h, t).astype(BF)
    if s == 0:
        a1_ref[64:128, cols] = act.astype(BF)
    else:
        a1_ref[128:192, cols] = act.astype(BF)
        a1_ref[0:64, cols] = shift_up(act).astype(BF)


def taps_of(w2_ref, a):
    return jnp.concatenate([w2_ref[a, b, e] for e in range(3) for b in (1, 2)], axis=0)


def bands(taps, ref, *index):
    return jnp.concatenate([mm(taps, ref[(*index, j)], TN).astype(BF) for j in range(2)], axis=0)


OWN = (320, 192)
NEAR = (80, 192, 128)


def separate(rows, split, out_ref, height, first, many):
    d = mm(rows, split[...])
    for k in range(5):
        for n in range(many):
            at = (first + n) * LANES
            out_ref[k * height : (k + 1) * height, at : at + LANES] = d[
                n * height : (n + 1) * height, k * LANES : (k + 1) * LANES
            ].astype(BF)


def first_kernel(v, w1, w2, out_ref, slope_ref, away_ref):
    x4_ref, a1_ref = parts(out_ref, *OWN)
    split = split_here()
    w = bands(w1[...].reshape(108, 32), {(j,): band_here(1, j) for j in range(2)})
    w2a = taps_of(w2, 0)
    for q in range(4):
        rows = jnp.concatenate([v[4 * q + n].reshape(64, 512) for n in range(4)], axis=0)
        separate(rows, split, x4_ref, 64, 4 * q, 4)
        cols = slice(q * CHUNK, (q + 1) * CHUNK)
        for s in range(2):
            h = mm(w, x4_ref[s * 128 : s * 128 + 192, cols])
            store_plane(h, s, cols, a1_ref, slope_ref)
        away_ref[:, cols] = mm(w2a, a1_ref[:, cols], TN).astype(BF)


def second_kernel(
    halo, split, w1, own, rim, w2, first_ref, wd1, out_ref, part_ref, wd1_ref, block_ref, wide_ref
):
    x4, a1c = parts(first_ref, *OWN)
    xh_ref, a1_ref, slope_ref = parts(out_ref, *NEAR)
    taps = w1[...].reshape(108, 32)
    w, wh = bands(taps, own, 0), bands(taps, rim)
    rows = jnp.concatenate([halo[n].reshape(16, 512) for n in range(S)], axis=0)
    separate(rows, split, xh_ref, 16, 0, S)
    taps_b, taps_c = taps_of(w2, 1), taps_of(w2, 2)
    for q in range(4):
        cols = slice(q * CHUNK, (q + 1) * CHUNK)
        for s in range(2):
            h = mm(w, x4[s * 128 : s * 128 + 192, cols]) + mm(
                wh, xh_ref[s * 32 : s * 32 + 48, cols]
            )
            store_plane(h, s, cols, a1_ref, slope_ref)
        part_ref[:, cols] = mm(taps_b, a1_ref[:, cols], TN) + mm(taps_c, a1c[:, cols], TN)

    def tap(a, e):
        return jnp.concatenate([w2[a, 1, e], w2[a, 2, e]], axis=0)

    zero = jnp.zeros((64, 64), BF)
    for k, row in enumerate(
        (
            (tap(1, 1), zero, zero, zero),
            (tap(2, 1), tap(0, 1), zero, zero),
            (tap(1, 2), zero, tap(1, 0), zero),
            (tap(2, 2), tap(0, 2), tap(2, 0), tap(0, 0)),
        )
    ):
        block_ref[k * 64 : (k + 1) * 64] = jnp.concatenate(row, axis=1)
    wide_ref[...] = wd1[...].astype(F32)
    for x in range(32):
        wd1_ref[x * 64 : (x + 1) * 64] = wide_ref[pl.ds(x, 64, stride=32), :].astype(BF)


def third_kernel(part, got, slope2_ref, pay_ref, fown_ref):
    total = jnp.zeros((S, 64), F32)
    for q in range(4):
        cols = slice(q * CHUNK, (q + 1) * CHUNK)
        h2 = part[:, cols] + got[:, cols].astype(F32)
        t = jnp.tanh(h2)
        act2 = leaky(h2, t).astype(BF)
        slope2_ref[:, cols] = slope(h2, t).astype(BF)
        rows = lax.broadcasted_iota(jnp.int32, (S, CHUNK), 0)
        owner = lax.shift_right_logical(lane_ids((S, CHUNK)), 7) + 4 * q
        pick = jnp.where(rows == owner, 1.0, 0.0).astype(BF)
        total = total + mm(pick, act2, NT)
    feats = total * (1.0 / 128.0)
    pay = jnp.concatenate([feats[0:8], feats[8:16]], axis=1).astype(BF)
    for x in range(32):
        pay_ref[x] = pay
    fown_ref[...] = jnp.concatenate([feats, jnp.zeros((S, 64), F32)], axis=1).astype(BF)


def split_loss(loss):
    high = loss.astype(BF).astype(F32)
    mid = (loss - high).astype(BF).astype(F32)
    return high, mid, loss - high - mid


def tail_kernel(
    counts, position, g, wd1, wd2, wd3, targets, fown, gf_ref, mix_ref, small_ref, padded_ref
):
    ends = []
    for k in range(32):
        ends.append(counts[k] + (ends[-1] if k else 0))
    by_row = lax.broadcasted_iota(jnp.int32, (S, S), 0)
    by_col = lax.broadcasted_iota(jnp.int32, (S, S), 1)
    row_owner = jnp.zeros((S, S), jnp.int32)
    col_owner = jnp.zeros((S, S), jnp.int32)
    for end in ends:
        row_owner = row_owner + jnp.where(by_row >= end, 1, 0)
        col_owner = col_owner + jnp.where(by_col >= end, 1, 0)
    alike = jnp.where(row_owner == col_owner, 1.0, 0.0)
    same = alike / jnp.sum(alike, axis=1, keepdims=True)

    low = lane_ids((8, LANES)) < 64
    pairs = []
    for p in range(16):
        ga, gb = g[2 * p].astype(F32), g[2 * p + 1].astype(F32)
        lo = jnp.where(low, ga, pltpu.roll(gb, 64, 1))
        hi = jnp.where(low, pltpu.roll(ga, 64, 1), gb)
        pairs.append(jnp.concatenate([lo, hi], axis=0).astype(BF))
    feats = jnp.concatenate(pairs, axis=1)
    dense1 = mm(feats, wd1[...])
    centred = dense1 - 0.5 * mm_exact(same, dense1)
    t1 = jnp.tanh(centred)
    out1 = leaky(centred, t1).astype(BF)

    w2 = jnp.concatenate([wd2[...], jnp.zeros((64, LANES), BF)], axis=0)
    padded_ref[...] = jnp.zeros((LANES, LANES), F32)
    padded_ref[64:68, 0:64] = wd3[...].astype(F32)
    w3 = padded_ref[...].astype(BF)
    padded_ref[...] = jnp.zeros((LANES, LANES), F32)
    padded_ref[64:68, 0:S] = targets[...]
    goal = jnp.transpose(padded_ref[...], (1, 0))[0:S]

    dense2 = mm(out1, w2, NT)
    t2 = jnp.tanh(dense2)
    out2 = leaky(dense2, t2).astype(BF)
    diff = mm(out2, w3, NT) - goal
    loss = jnp.sum(jnp.sum(diff * diff, axis=1, keepdims=True), axis=0, keepdims=True) / 32.0
    gpred = (diff / 16.0).astype(BF)
    gdense2 = (mm(gpred, w3) * slope(dense2, t2)).astype(BF)
    gcentred = mm(gdense2, w2) * slope(centred, t1)
    gdense1 = (gcentred - 0.5 * mm_exact(same, gcentred)).astype(BF)
    here = position[0]
    after = jnp.minimum(here + 1, 31)
    for k, slab in enumerate((here, after)):
        rows = wd1[pl.ds(pl.multiple_of(slab * 64, 64), 64), :]
        gf_ref[k * 64 : (k + 1) * 64] = mm(rows, gdense1, NT)

    d1 = mm(fown[...], gdense1, TN)
    d2 = mm(gdense2, out1, TN)
    d3 = mm(gpred, out2, TN)[64:72]
    lanes = lane_ids((8, LANES))
    top = lax.broadcasted_iota(jnp.int32, (8, LANES), 0) == 0
    for k, piece in enumerate(split_loss(loss)):
        d3 = jnp.where(jnp.logical_and(top, lanes == 64 + k), piece, d3)
    small_ref[...] = d3
    for p in range(16):
        mix_ref[p * 8 : p * 8 + 4] = d1[p * 4 : p * 4 + 4]
        mix_ref[p * 8 + 4 : p * 8 + 8] = d2[p * 4 : p * 4 + 4]


def tap_sums(r_ref, rh_ref):
    group = lax.shift_right_logical(lane_ids((12, LANES)), 5)
    sums = [jnp.zeros((12, LANES), F32) for _ in range(9)]

    def add(rows, places):
        for g, a, b in places:
            if 0 <= a < 3 and 0 <= b < 3:
                sums[a * 3 + b] = sums[a * 3 + b] + jnp.where(group == g, rows, 0.0)

    for y in range(4):
        for x in range(4):
            add(
                r_ref[pl.ds(x * 4 + y, 12, stride=16), :],
                [(2 * i + j, x - 2 * i + 1, y - 2 * j + 1) for i in range(2) for j in range(2)],
            )
        add(rh_ref[pl.ds(y, 12, stride=4), :], [(j, 0, y - 2 * j + 1) for j in range(2)])
    out = []
    for total in sums:
        total = total + pltpu.roll(total, 64, 1)
        out.append(total + pltpu.roll(total, 32, 1))
    return out


def back_kernel(
    gf_ref, mix, small, first_ref, s1c, block, slope2, next2, near, out_ref,
    g_ref, h_ref, w_ref, r_ref, rh_ref,
):
    x4, a1c = parts(first_ref, *OWN)
    gf = gf_ref[...].astype(BF).astype(F32) * (1.0 / 128.0)
    for q in range(4):
        cols = slice(q * CHUNK, (q + 1) * CHUNK)
        spread = jnp.concatenate(
            [jnp.broadcast_to(gf[:, 4 * q + n : 4 * q + n + 1], (128, LANES)) for n in range(4)],
            axis=1,
        )
        go = spread[0:64] * slope2[:, cols].astype(F32)
        gn = spread[64:128] * next2[:, cols].astype(F32)
        g_ref[0:64, cols] = go.astype(BF)
        g_ref[64:128, cols] = gn.astype(BF)
        g_ref[128:192, cols] = shift_down(go).astype(BF)
        g_ref[192:256, cols] = shift_down(gn).astype(BF)
        gact = mm(block[...], g_ref[:, cols])
        s1b = parts(near, *NEAR)[2]
        for s in range(2):
            for i, s1 in enumerate((s1b, s1c)):
                r = (2 * s + i) * 64
                h_ref[s, i * 64 : (i + 1) * 64, cols] = (
                    gact[r : r + 64] * s1[s * 64 : (s + 1) * 64, cols].astype(F32)
                ).astype(BF)
    xh, a1b, _ = parts(near, *NEAR)
    w_ref[0:192] = mm(a1c[...], g_ref[0:128, :], NT)
    a1 = mm(a1b[...], g_ref[0:64, :], NT)
    w_ref[192:288] = jnp.concatenate([a1[0:96], a1[96:192]], axis=1)
    r_ref[...] = mm(x4[0:192, :], h_ref[0], NT) + mm(x4[128:320, :], h_ref[1], NT)
    rh_ref[...] = mm(xh[0:48, :], h_ref[0], NT) + mm(xh[32:80, :], h_ref[1], NT)
    sums = tap_sums(r_ref, rh_ref)
    group = lax.shift_right_logical(lane_ids((12, LANES)), 5)
    w_ref[288:384] = jnp.zeros((96, LANES), F32)
    for k in range(3):
        packed = sums[4 * k]
        for n in range(1, 4):
            if 4 * k + n < 9:
                packed = jnp.where(group == n, sums[4 * k + n], packed)
        w_ref[288 + 16 * k : 300 + 16 * k] = packed
    zero = jnp.zeros((8, LANES), F32)
    for p in range(16):
        out_ref[p] = jnp.concatenate(
            [w_ref[p * PART : (p + 1) * PART], small[...], mix[p * 8 : (p + 1) * 8], zero], axis=0
        ).astype(BF)


def low_half(a, b):
    rows = lax.broadcasted_iota(jnp.int32, (8, LANES), 0)
    return jnp.where(rows < 4, a, pltpu.roll(b, 4, 0))


def high_half(a, b):
    rows = lax.broadcasted_iota(jnp.int32, (8, LANES), 0)
    return jnp.where(rows < 4, pltpu.roll(a, 4, 0), b)


def group_kernel(got, out_ref, d2_ref, d3_ref, loss_ref):
    even, odd = got[0].astype(F32), got[1].astype(F32)
    for k in range(1, 8):
        even, odd = even + got[2 * k].astype(F32), odd + got[2 * k + 1].astype(F32)
    total = even[0:PART] + odd[0:PART]
    d1 = low_half(even[32:40], odd[32:40])
    pay = jnp.concatenate([total, d1], axis=0).astype(BF)
    for k in range(16):
        out_ref[k] = pay
    d2_ref[...] = pltpu.roll(even[32:40], 4, 0)
    small = even[PART:32]
    d3_ref[...] = small[0:4, 0:64]
    lanes = lane_ids((8, LANES))
    rows = lax.broadcasted_iota(jnp.int32, (8, LANES), 0)
    held = jnp.logical_and(jnp.logical_and(lanes >= 64, lanes < 67), rows == 0)
    values = jnp.where(held, small, 0.0)
    loss_ref[...] = jnp.sum(jnp.sum(values, axis=1, keepdims=True), axis=0, keepdims=True)


def column_kernel(got, d2, out_ref):
    blocks = [got[k].astype(F32) for k in range(16)]
    total = blocks[0][0:PART]
    for b in blocks[1:]:
        total = total + b[0:PART]
    pay = jnp.concatenate([total, d2[...]] + [b[PART:32] for b in blocks], axis=0).astype(BF)
    for k in range(8):
        out_ref[k] = pay


def last_kernel(core, mine, other, gw1_ref, gw2_ref, gd1_ref, gd2_ref, w_ref):
    first = core[0] == 0
    for k in range(8):
        a, b = mine[k].astype(F32), other[k].astype(F32)
        low, high = jnp.where(first, a, b), jnp.where(first, b, a)
        w_ref[2 * k * PART : (2 * k + 1) * PART] = low[0:PART]
        w_ref[(2 * k + 1) * PART : (2 * k + 2) * PART] = high[0:PART]
        gd2_ref[k * 8 : (k + 1) * 8] = low_half(low[PART:32], high[PART:32])
        for q in range(16):
            at = 32 + 8 * q
            lo, hi = low[at : at + 8], high[at : at + 8]
            gd1_ref[pl.ds(k * 256 + 2 * q, 8, stride=32), :] = low_half(lo, hi)
            gd1_ref[pl.ds(k * 256 + 2 * q + 1, 8, stride=32), :] = high_half(lo, hi)
    for a in range(3):
        for e in range(3):
            gw2_ref[a, 0, e] = jnp.zeros((32, 64), F32)
            for b in (1, 2):
                at = e * 64 + (b - 1) * 32
                right = a == 0
                if a == 1:
                    right = at >= 96
                    at = 192 + at % 96
                block = w_ref[at : at + 32]
                if right:
                    block = pltpu.roll(block, 64, 1)
                gw2_ref[a, b, e] = block[:, 0:64]
    for a in range(3):
        for b in range(3):
            k, n = divmod(a * 3 + b, 4)
            packed = w_ref[288 + 16 * k : 304 + 16 * k]
            if n:
                packed = pltpu.roll(packed, LANES - 32 * n, 1)
            for e in range(3):
                gw1_ref[a, b, e] = packed[4 * e : 4 * e + 4, 0:32]


def local(volumes, targets, counts, w_conv1, w_conv2, w_dense1, w_dense2, w_dense3):
    core = lax.axis_index("core").astype(jnp.int32).reshape(1)
    position = lax.axis_index(SLABS).astype(jnp.int32).reshape(1)
    forward = [(i, i + 1) for i in range(31)]
    backward = [(i + 1, i) for i in range(31)]
    swap = [(0, 1), (1, 0)]
    split = jnp.asarray(split_matrix(), BF)
    own, rim = (jnp.asarray(m, BF) for m in band_matrices())
    w1 = jnp.swapaxes(w_conv1, 3, 4).reshape(27, 4, 32)
    w2 = jnp.swapaxes(w_conv2, 3, 4)

    halo = lax.ppermute(volumes[:, :, 3], SLABS, forward)
    held_own, held_slope, away = call(
        first_kernel,
        [((sum(OWN), WIDE), BF), ((128, WIDE), BF), ((64, WIDE), BF)],
        (volumes, w1, w2),
        flops=10**9,
    )
    got = lax.ppermute(away, SLABS, forward)
    held_near, part, wd1, block = call(
        second_kernel,
        [
            ((sum(NEAR), WIDE), BF), ((64, WIDE), F32), ((2048, LANES), BF),
            ((256, 256), BF),
        ],
        (
            halo, split, w1, own, rim, w2, held_own, w_dense1,
        ),
        scratch=[pltpu.VMEM((2048, LANES), F32)],
        flops=2 * 10**9,
    )
    slope2, pay, fown = call(
        third_kernel,
        [((64, WIDE), BF), ((32, 8, LANES), BF), ((S, LANES), BF)],
        (part, got),
        flops=10**8,
    )
    gathered = lax.all_to_all(pay, SLABS, 0, 0, tiled=True)
    next2 = lax.ppermute(slope2, SLABS, backward)
    gf, mix, small = call(
        tail_kernel,
        [((LANES, S), F32), ((LANES, LANES), F32), ((8, LANES), F32)],
        (gathered, wd1, w_dense2.T, w_dense3.T, targets.T, fown),
        scalars=(counts, position),
        scratch=[pltpu.VMEM((LANES, LANES), F32)],
        flops=2000000000,
    )
    (scattered,) = call(
        back_kernel,
        [((16, 48, LANES), BF)],
        (gf, mix, small, held_own, held_slope, block, slope2, next2, held_near),
        scratch=[
            pltpu.VMEM((256, WIDE), BF), pltpu.VMEM((2, 128, WIDE), BF),
            pltpu.VMEM((16 * PART, LANES), F32), pltpu.VMEM((192, LANES), F32),
            pltpu.VMEM((48, LANES), F32),
        ],
        flops=2 * 10**9,
    )
    over_group = lax.all_to_all(scattered, (*DP, "core"), 0, 0, tiled=True)
    to_column, d2, d3, loss = call(
        group_kernel,
        [((16, 32, LANES), BF), ((8, LANES), F32), ((4, 64), F32), ((1, 1), F32)],
        (over_group,),
    )
    over_column = lax.all_to_all(to_column, COLUMN, 0, 0, tiled=True)
    (back,) = call(
        column_kernel, [((8, 160, LANES), BF)], (over_column, d2)
    )
    summed = lax.all_to_all(back, DP, 0, 0, tiled=True)
    other = lax.ppermute(summed, "core", swap)
    gw1, gw2, gd1, gd2 = call(
        last_kernel,
        [
            ((3, 3, 3, 4, 32), F32), ((3, 3, 3, 32, 64), F32),
            ((2048, LANES), F32), ((64, LANES), F32),
        ],
        (summed, other),
        scalars=(core,),
        scratch=[pltpu.VMEM((16 * PART, LANES), F32)],
    )
    return (
        loss.reshape(()), jnp.swapaxes(gw1, 3, 4), jnp.swapaxes(gw2, 3, 4), gd1, gd2.T, d3.T,
    )


def solution(mesh):
    fine = Mesh(mesh.devices.reshape(4, 2, 2, 8, 2), ("x", "yl", "yh", "z", "core"))
    placed = (P(DP, None, SLABS, None, None), P(DP, None), P(), P(), P(), P(), P(), P())
    return jax.shard_map(
        local, mesh=fine, in_specs=placed, out_specs=(P(), P(), P(), P(), P(), P()), check_vma=False
    )
```

time: 99.3 us -> 87.8 us (0.88)
  Pallas kernels: 24.5 us -> 12.6 us
  blocking collectives: 29.7 us -> 33.8 us
  waiting for transfers between devices: 11.9 us -> 8.68 us
  starting transfers between devices: 27 us -> 25 us
  local copies, waits for them, and re-layouts: 4.74 us -> 6.31 us
    pallas_call x8, Pallas kernels: 24.5 us -> 12.6 us  [call(): pl.pallas_call(kernel, out_shape=[jax.ShapeDtypeStruct(s, d) for s, d in...]
    all_to_all x1, blocking collectives: 9.17 us -> 12.3 us  [local(): over_group = lax.all_to_all(scattered, (*DP, 'core'), 0, 0, tiled=True)]
    all_to_all x1, waiting for transfers between devices: 9.57 us -> 7.42 us  [local(): gathered = lax.all_to_all(pay, SLABS, 0, 0, tiled=True)]
    unnamed x12 -> x34, local copies, waits for them, and re-layouts: 3.69 us -> 5.2 us
    ppermute x1 -> x0, starting transfers between devices: 1.34 us -> none  [local(): taken = lax.ppermute(give, 'core', swap)]
    all_to_all x1, blocking collectives: 11.5 us -> 12.6 us  [local(): over_column = lax.all_to_all(to_column, COLUMN, 0, 0, tiled=True)]
    ppermute x1 -> x0, waiting for transfers between devices: 1.09 us -> none  [local(): taken = lax.ppermute(give, 'core', swap)]
    ppermute x1, starting transfers between devices: 4.23 us -> 3.14 us  [local(): other = lax.ppermute(summed, 'core', swap)]
  transfers between devices with their start and end apart: 6 -> 5, of which waited for: 3 -> 2; matrix products, arithmetic and copies ran while one was open for 0% -> 0% of each run, Pallas kernels for 12% -> 8%
where the time goes in v3:
time: 87.8 us; the launch traced here: 87.3 us
  blocking collectives  33.8 us (38%)
  starting transfers between devices  25 us (28%)
  Pallas kernels  12.6 us (14%)
  waiting for transfers between devices  8.68 us (10%)
  local copies, waits for them, and re-layouts  6.31 us (7%)
  between operations  0.88 us (1%)
    all_to_all x1, starting transfers between devices, local(): gathered = lax.all_to_all(pay, SLABS, 0, 0, tiled=True)  12.9 us
    pallas_call x8, Pallas kernels, call(): pl.pallas_call(kernel, out_shape=[jax.ShapeDtypeStruct(s, d) for s, d in...  12.6 us
    all_to_all x1, blocking collectives, local(): over_column = lax.all_to_all(to_column, COLUMN, 0, 0, tiled=True)  12.6 us
    all_to_all x1, blocking collectives, local(): over_group = lax.all_to_all(scattered, (*DP, 'core'), 0, 0, tiled=True)  12.3 us
    all_to_all x1, blocking collectives, local(): summed = lax.all_to_all(back, DP, 0, 0, tiled=True)  8.89 us
    all_to_all x1, waiting for transfers between devices, local(): gathered = lax.all_to_all(pay, SLABS, 0, 0, tiled=True)  7.42 us
    unnamed x34, local copies, waits for them, and re-layouts  5.2 us
    ppermute x1, starting transfers between devices, local(): halo = lax.ppermute(volumes[:, :, 3], SLABS, forward)  4.94 us
  transfers between devices with their start and end apart: 5, of which 2 were waited for; matrix products, arithmetic and copies ran while one was open for 0% of the time, Pallas kernels for 8%

profile of v3, /device:TPU:1, one launch (start us, length us, event | category | flops | bytes accessed | tf_op | source)
XLA Modules:
  0.0 87.3 jit_solution(12298566986168136183)
XLA Ops:
  0.6 0.0 copy-start.1
  0.6 1.1 %slice_bitcast_fusion = bf16[16,4,4,512]{3,2,1,0:T(4,128)(2,1)S(1)} fusion(bf16[16,4,4,4,512]{4,3,2,1,0:T(4,128)(2,1)} %v.1), kind=kLoop, calls=%fused_computation | loop fusion | bytes 524288 | tf_op jit(solution)/shard_map/squeeze | solution.py:478
  1.8 4.9 %collective-permute-start = (bf16[16,4,4,512]{3,2,1,0:T(4,128)(2,1)S(1)}, bf16[16,4,4,512]{3,2,1,0:T(4,128)(2,1)S(1)}, u32[]{:S(2)}, u32[]{:S(2)}) collective-permute-start(bf16[16,4,4,512]{3,2,1,0:T(4,128)(2,1)S(1)} %slice_bitcast_fusion), channel_id=1, source_target_pairs={{0,1},{1,2},{2,3},{3,4},{4,5},{5,6},{6,7},{7,8},{8,9},{9,10},{10,1... | collective-permute-start | bytes 786440 | tf_op jit(solution)/shard_map/ppermute | solution.py:478
  6.7 0.0 copy-start
  6.7 1.2 %copy-done = bf16[16,4,4,4,512]{4,3,2,1,0:T(4,128)(2,1)S(1)} copy-done((bf16[16,4,4,4,512]{4,3,2,1,0:T(4,128)(2,1)S(1)}, bf16[16,4,4,4,512]{4,3,2,1,0:T(4,128)(2,1)}, u32[]{:S(2)}) %copy-start) | copy-done | bytes 1048600
  7.9 0.0 copy-start.2
  7.9 0.9 %copy-done.2 = bf16[3,3,3,64,32]{3,4,2,1,0:T(8,128)(2,1)S(1)} copy-done((bf16[3,3,3,64,32]{3,4,2,1,0:T(8,128)(2,1)S(1)}, bf16[3,3,3,64,32]{3,4,2,1,0:T(8,128)(2,1)}, u32[]{:S(2)}) %copy-start.2) | copy-done | bytes 110616
  8.9 0.7 copy-done.4
  9.6 0.0 copy-start.12
  9.6 2.8 %shard_map.154 = (bf16[512,2048]{1,0:T(8,128)(2,1)S(1)}, bf16[128,2048]{1,0:T(8,128)(2,1)S(1)}, bf16[64,2048]{1,0:T(8,128)(2,1)S(1)}) custom-call(bf16[16,4,4,4,512]{4,3,2,1,0:T(4,128)(2,1)S(1)} %copy-done, bf16[27,4,32]{2,1,0:T(4,128)(2,1)S(1)} %bitcast.20, bf16[3,3,3,32,64]{4,3,2,1,0:T(8,128)(2,1)S(1)} %bitcast.18), custom_call_target="tpu_custom_call" | custom-call | flops 1000000000 | bytes 2883584 | tf_op jit(solution)/shard_map/pallas_call | solution.py:100
  12.5 1.9 %collective-permute-start.1 = (bf16[64,2048]{1,0:T(8,128)(2,1)S(1)}, bf16[64,2048]{1,0:T(8,128)(2,1)S(1)}, u32[]{:S(2)}, u32[]{:S(2)}) collective-permute-start(bf16[64,2048]{1,0:T(8,128)(2,1)S(1)} %get-tuple-element.29), channel_id=1, source_target_pairs={{0,1},{1,2},{2,3},{3,4},{4,5},{5,6},{6,7},{7,8},{8,9},{9,10},{10,1... | collective-permute-start | bytes 786440 | tf_op jit(solution)/shard_map/ppermute | solution.py:485
  14.4 0.0 collective-permute-done.halo
  14.4 0.0 copy-done.1
  14.4 0.0 copy-done.3
  14.4 0.0 copy-done.5
  14.5 0.0 copy-done.10
  14.5 0.0 copy-done.11
  14.5 0.0 copy-done.12
  14.5 0.0 copy-start.6
  14.5 0.0 copy-start.7
  14.5 0.0 copy-start.8
  14.5 0.0 copy-start.9
  14.5 2.5 %shard_map.155 = (bf16[400,2048]{1,0:T(8,128)(2,1)S(1)}, f32[64,2048]{1,0:T(8,128)S(1)}, bf16[2048,128]{1,0:T(8,128)(2,1)S(1)}, bf16[256,256]{1,0:T(8,128)(2,1)S(1)}) custom-call(bf16[16,4,4,512]{3,2,1,0:T(4,128)(2,1)S(1)} %collective-permute-done.halo, bf16[512,640]{1,0:T(8,128)(2,1)S(1)} %copy-done.10, bf16[27,4,32]{2,1,0:T(4,128)(2,1)S(1)} %bitcast.21, ...), custom_call_target="tpu_custom_call" | custom-call | flops 2000000000 | bytes 2818048 | tf_op jit(solution)/shard_map/pallas_call | solution.py:100
  17.0 0.0 copy-start.13
  17.0 1.2 %copy-done.13 = bf16[400,2048]{1,0:T(8,128)(2,1)} copy-done((bf16[400,2048]{1,0:T(8,128)(2,1)}, bf16[400,2048]{1,0:T(8,128)(2,1)S(1)}, u32[]{:S(2)}) %copy-start.13) | copy-done | bytes 1638424
  18.2 0.0 collective-permute-done.1.got
  18.3 1.0 %shard_map.156 = (bf16[64,2048]{1,0:T(8,128)(2,1)S(1)}, bf16[32,8,128]{2,1,0:T(8,128)(2,1)}, bf16[16,128]{1,0:T(8,128)(2,1)S(1)}) custom-call(f32[64,2048]{1,0:T(8,128)S(1)} %get-tuple-element.28.part, bf16[64,2048]{1,0:T(8,128)(2,1)S(1)} %collective-permute-done.1.got), custom_call_target="tpu_custom_call" | custom-call | flops 100000000 | bytes 331776 | tf_op jit(solution)/shard_map/pallas_call | solution.py:100
  19.3 0.0 copy-done.15
  19.3 12.9 %all-to-all-start = ((bf16[32,8,128]{2,1,0:T(8,128)(2,1)}), bf16[32,8,128]{2,1,0:T(8,128)(2,1)S(1)}, u32[]{:S(2)}, u32[]{:S(2)}) async-start(bf16[32,8,128]{2,1,0:T(8,128)(2,1)} %get-tuple-element.30), calls=%async_computation | async-start | bytes 131072 | tf_op jit(solution)/shard_map/all_to_all | solution.py:504
  32.2 2.1 %collective-permute-start.2 = (bf16[64,2048]{1,0:T(8,128)(2,1)S(1)}, bf16[64,2048]{1,0:T(8,128)(2,1)S(1)}, u32[]{:S(2)}, u32[]{:S(2)}) collective-permute-start(bf16[64,2048]{1,0:T(8,128)(2,1)S(1)} %get-tuple-element.38.slope2), channel_id=1, source_target_pairs={{1,0},{2,1},{3,2},{4,3},{5,4},{6,5},{7,6},{8,7},{9,8},{10,9},{11,1... | collective-permute-start | bytes 786440 | tf_op jit(solution)/shard_map/ppermute | solution.py:505
  34.3 7.4 %all-to-all-done.g = bf16[32,8,128]{2,1,0:T(8,128)(2,1)S(1)} async-done(((bf16[32,8,128]{2,1,0:T(8,128)(2,1)}), bf16[32,8,128]{2,1,0:T(8,128)(2,1)S(1)}, u32[]{:S(2)}, u32[]{:S(2)}) %all-to-all-start) | async-done | bytes 65568 | tf_op jit(solution)/shard_map/all_to_all | solution.py:504
  41.7 0.0 copy-done.6
  41.8 0.0 copy-done.7
  41.8 0.0 copy-done.8
  41.8 0.0 copy-done.9
  41.8 0.0 copy-start.16
  41.8 1.0 %copy-done.16 = bf16[2048,128]{1,0:T(8,128)(2,1)S(1)} copy-done((bf16[2048,128]{1,0:T(8,128)(2,1)S(1)}, bf16[2048,128]{1,0:T(8,128)(2,1)}, u32[]{:S(2)}) %copy-start.16) | copy-done | bytes 524312
  42.8 1.7 %shard_map.157 = (f32[128,16]{1,0:T(8,128)S(1)}, f32[128,128]{1,0:T(8,128)S(1)}, f32[8,128]{1,0:T(8,128)S(1)}) custom-call(s32[32]{0:T(128)S(1)} %copy-done.9, s32[1]{0:T(128)} %bitcast.position, bf16[32,8,128]{2,1,0:T(8,128)(2,1)S(1)} %all-to-all-done.g, bf16[2048,128]{1,0:T(8,128)(2,1)S(1)} %copy-done.16, bf16[64,128]{1,0:T(8,128)(2,1)S(1)} %bitcast.22, ...), custom_call_target="tpu_custom_call" | custom-call | flops 2000000000 | bytes 77824 | tf_op jit(solution)/shard_map/pallas_call | solution.py:100
  44.5 0.0 collective-permute-done.2.next2
  44.5 0.0 copy-done.14
  44.5 2.2 %shard_map.158 = bf16[16,48,128]{2,1,0:T(8,128)(2,1)S(1)} custom-call(f32[128,16]{1,0:T(8,128)S(1)} %get-tuple-element.33.gf_ref, f32[128,128]{1,0:T(8,128)S(1)} %get-tuple-element.34.mix, f32[8,128]{1,0:T(8,128)S(1)} %get-tuple-element.35.small, bf16[512,2048]{1,0:T(8,128)(2,1)S(1)} %get-tuple-element.27.first_ref, ...), custom_call_target="tpu_custom_call" | custom-call | flops 2000000000 | bytes 196608 | tf_op jit(solution)/shard_map/pallas_call | solution.py:100
  46.8 12.3 %all_to_all.20.got = bf16[16,48,128]{2,1,0:T(8,128)(2,1)S(1)} all-to-all(bf16[16,48,128]{2,1,0:T(8,128)(2,1)S(1)} %shard_map.158), channel_id=1, replica_groups=mesh['x'=4,'yl'=2,'yh'=2,'z'=8,'core'=2] {'x','yl','core'}, dimensions={0} | all-to-all | bytes 393216 | tf_op jit(solution)/shard_map/all_to_all | solution.py:525
  59.0 0.6 shard_map.159
  59.6 12.6 %all_to_all.21.got = bf16[16,32,128]{2,1,0:T(8,128)(2,1)S(1)} all-to-all(bf16[16,32,128]{2,1,0:T(8,128)(2,1)S(1)} %get-tuple-element.41), channel_id=1, replica_groups=mesh['x'=4,'yl'=2,'yh'=2,'z'=8,'core'=2] {'yh','z'}, dimensions={0} | all-to-all | bytes 262144 | tf_op jit(solution)/shard_map/all_to_all | solution.py:531
  72.3 8.9 %all_to_all.22.mine = bf16[8,160,128]{2,1,0:T(8,128)(2,1)S(1)} all-to-all(bf16[8,160,128]{2,1,0:T(8,128)(2,1)S(1)} %shard_map.160), channel_id=1, replica_groups=mesh['x'=4,'yl'=2,'yh'=2,'z'=8,'core'=2] {'x','yl'}, dimensions={0} | all-to-all | bytes 655360 | tf_op jit(solution)/shard_map/all_to_all | solution.py:535
  81.2 3.1 %collective-permute-start.3 = (bf16[8,160,128]{2,1,0:T(8,128)(2,1)S(1)}, bf16[8,160,128]{2,1,0:T(8,128)(2,1)S(1)}, u32[]{:S(2)}, u32[]{:S(2)}) collective-permute-start(bf16[8,160,128]{2,1,0:T(8,128)(2,1)S(1)} %all_to_all.22.mine), channel_id=1, source_target_pairs={{0,1},{1,0},{2,3},{3,2},{4,5},{5,4},{6,7},{7,6},{8,9},{9,8},{10,11... | collective-permute-start | bytes 983048 | tf_op jit(solution)/shard_map/ppermute | solution.py:536
  84.3 1.3 %collective-permute-done.3.other = bf16[8,160,128]{2,1,0:T(8,128)(2,1)S(1)} collective-permute-done((bf16[8,160,128]{2,1,0:T(8,128)(2,1)S(1)}, bf16[8,160,128]{2,1,0:T(8,128)(2,1)S(1)}, u32[]{:S(2)}, u32[]{:S(2)}) %collective-permute-start.3) | collective-permute-done | bytes 327712 | tf_op jit(solution)/shard_map/ppermute | solution.py:536
  85.6 1.7 %shard_map.161 = (f32[3,3,3,4,32]{4,3,2,1,0:T(4,128)}, f32[3,3,3,32,64]{4,3,2,1,0:T(8,128)}, f32[2048,128]{1,0:T(8,128)}, f32[64,128]{1,0:T(8,128)}) custom-call(s32[1]{0:T(128)} %bitcast.10.core, bf16[8,160,128]{2,1,0:T(8,128)(2,1)S(1)} %all_to_all.22.mine, bf16[8,160,128]{2,1,0:T(8,128)(2,1)S(1)} %collective-permute-done.3.other), custom_call_target="tpu_custom_call" | custom-call | flops 100000000 | bytes 1316352 | tf_op jit(solution)/shard_map/pallas_call | solution.py:100
  (8 shorter events, 0.1 us)
Async XLA Ops:
  0.6 13.8 %copy-start.1 = (bf16[2048,128]{1,0:T(8,128)(2,1)S(1)}, bf16[2048,128]{1,0:T(8,128)(2,1)}, u32[]{:S(2)}) copy-start(bf16[2048,128]{1,0:T(8,128)(2,1)} %wd1.1) | copy-start | bytes 1572868
  1.8 12.7 %collective-permute-start = (bf16[16,4,4,512]{3,2,1,0:T(4,128)(2,1)S(1)}, bf16[16,4,4,512]{3,2,1,0:T(4,128)(2,1)S(1)}, u32[]{:S(2)}, u32[]{:S(2)}) collective-permute-start(bf16[16,4,4,512]{3,2,1,0:T(4,128)(2,1)S(1)} %slice_bitcast_fusion), channel_id=1, source_target_pairs={{0,1},{1,2},{2,3},{3,4},{4,5},{5,6},{6,7},{7,8},{8,9},{9,10},{10,1... | collective-permute-start | bytes 786440 | tf_op jit(solution)/shard_map/ppermute | solution.py:478
  6.7 1.2 %copy-start = (bf16[16,4,4,4,512]{4,3,2,1,0:T(4,128)(2,1)S(1)}, bf16[16,4,4,4,512]{4,3,2,1,0:T(4,128)(2,1)}, u32[]{:S(2)}) copy-start(bf16[16,4,4,4,512]{4,3,2,1,0:T(4,128)(2,1)} %v.1) | copy-start | bytes 3145732
  7.9 0.9 %copy-start.2 = (bf16[3,3,3,64,32]{3,4,2,1,0:T(8,128)(2,1)S(1)}, bf16[3,3,3,64,32]{3,4,2,1,0:T(8,128)(2,1)}, u32[]{:S(2)}) copy-start(bf16[3,3,3,64,32]{3,4,2,1,0:T(8,128)(2,1)} %param.15) | copy-start | bytes 331780
  8.9 0.7 copy-start.4
  9.6 4.8 %copy-start.3 = (bf16[3,3,3,64,32]{3,4,2,1,0:T(8,128)(2,1)S(1)}, bf16[3,3,3,64,32]{3,4,2,1,0:T(8,128)(2,1)}, u32[]{:S(2)}) copy-start(bf16[3,3,3,64,32]{3,4,2,1,0:T(8,128)(2,1)} %param.15) | copy-start | bytes 331780
  9.6 4.8 %copy-start.5 = (bf16[3,3,3,32,4]{3,4,2,1,0:T(4,128)(2,1)S(1)}, bf16[3,3,3,32,4]{3,4,2,1,0:T(4,128)(2,1)}, u32[]{:S(2)}) copy-start(bf16[3,3,3,32,4]{3,4,2,1,0:T(4,128)(2,1)} %param.14) | copy-start | bytes 20740
  9.6 4.8 %copy-start.10 = (bf16[512,640]{1,0:T(8,128)(2,1)S(1)}, bf16[512,640]{1,0:T(8,128)(2,1)}, u32[]{:S(2)}) copy-start(bf16[512,640]{1,0:T(8,128)(2,1)} %constant.22.clone.split) | copy-start | bytes 1966084
  9.6 4.8 %copy-start.11 = (bf16[2,2,108,192]{3,2,1,0:T(8,128)(2,1)S(1)}, bf16[2,2,108,192]{3,2,1,0:T(8,128)(2,1)}, u32[]{:S(2)}) copy-start(bf16[2,2,108,192]{3,2,1,0:T(8,128)(2,1)} %constant.23.clone.own) | copy-start | bytes 497668
  9.6 4.9 %copy-start.12 = (bf16[2,108,48]{2,1,0:T(8,128)(2,1)S(1)}, bf16[2,108,48]{2,1,0:T(8,128)(2,1)}, u32[]{:S(2)}) copy-start(bf16[2,108,48]{2,1,0:T(8,128)(2,1)} %constant.24.clone.rim) | copy-start | bytes 62212
  12.5 5.8 %collective-permute-start.1 = (bf16[64,2048]{1,0:T(8,128)(2,1)S(1)}, bf16[64,2048]{1,0:T(8,128)(2,1)S(1)}, u32[]{:S(2)}, u32[]{:S(2)}) collective-permute-start(bf16[64,2048]{1,0:T(8,128)(2,1)S(1)} %get-tuple-element.29), channel_id=1, source_target_pairs={{0,1},{1,2},{2,3},{3,4},{4,5},{5,6},{6,7},{7,8},{8,9},{9,10},{10,1... | collective-permute-start | bytes 786440 | tf_op jit(solution)/shard_map/ppermute | solution.py:485
  14.5 27.3 %copy-start.6 = (bf16[128,64]{0,1:T(8,128)(2,1)S(1)}, bf16[128,64]{0,1:T(8,128)(2,1)}, u32[]{:S(2)}) copy-start(bf16[128,64]{0,1:T(8,128)(2,1)} %param.17) | copy-start | bytes 49156
  14.5 27.3 %copy-start.7 = (f32[16,4]{0,1:T(4,128)S(1)}, f32[16,4]{0,1:T(4,128)}, u32[]{:S(2)}) copy-start(f32[16,4]{0,1:T(4,128)} %param.12) | copy-start | bytes 772
  14.5 27.2 %copy-start.8 = (bf16[64,4]{0,1:T(4,128)(2,1)S(1)}, bf16[64,4]{0,1:T(4,128)(2,1)}, u32[]{:S(2)}) copy-start(bf16[64,4]{0,1:T(4,128)(2,1)} %param.18) | copy-start | bytes 1540
  14.5 27.2 %copy-start.9 = (s32[32]{0:T(128)S(1)}, s32[32]{0:T(128)}, u32[]{:S(2)}) copy-start(s32[32]{0:T(128)} %counts.1) | copy-start | bytes 388
  17.0 1.2 %copy-start.13 = (bf16[400,2048]{1,0:T(8,128)(2,1)}, bf16[400,2048]{1,0:T(8,128)(2,1)S(1)}, u32[]{:S(2)}) copy-start(bf16[400,2048]{1,0:T(8,128)(2,1)S(1)} %get-tuple-element.39.near) | copy-start | bytes 4915204
  18.2 1.0 %copy-start.15 = (bf16[2048,128]{1,0:T(8,128)(2,1)}, bf16[2048,128]{1,0:T(8,128)(2,1)S(1)}, u32[]{:S(2)}) copy-start(bf16[2048,128]{1,0:T(8,128)(2,1)S(1)} %get-tuple-element.31.wd1) | copy-start | bytes 1572868
  19.3 22.5 %all-to-all-start = ((bf16[32,8,128]{2,1,0:T(8,128)(2,1)}), bf16[32,8,128]{2,1,0:T(8,128)(2,1)S(1)}, u32[]{:S(2)}, u32[]{:S(2)}) async-start(bf16[32,8,128]{2,1,0:T(8,128)(2,1)} %get-tuple-element.30), calls=%async_computation | async-start | bytes 131072 | tf_op jit(solution)/shard_map/all_to_all | solution.py:504
  32.2 12.4 %collective-permute-start.2 = (bf16[64,2048]{1,0:T(8,128)(2,1)S(1)}, bf16[64,2048]{1,0:T(8,128)(2,1)S(1)}, u32[]{:S(2)}, u32[]{:S(2)}) collective-permute-start(bf16[64,2048]{1,0:T(8,128)(2,1)S(1)} %get-tuple-element.38.slope2), channel_id=1, source_target_pairs={{1,0},{2,1},{3,2},{4,3},{5,4},{6,5},{7,6},{8,7},{9,8},{10,9},{11,1... | collective-permute-start | bytes 786440 | tf_op jit(solution)/shard_map/ppermute | solution.py:505
  41.8 1.0 %copy-start.16 = (bf16[2048,128]{1,0:T(8,128)(2,1)S(1)}, bf16[2048,128]{1,0:T(8,128)(2,1)}, u32[]{:S(2)}) copy-start(bf16[2048,128]{1,0:T(8,128)(2,1)} %copy-done.15) | copy-start | bytes 1572868
  42.8 1.7 %copy-start.14 = (bf16[400,2048]{1,0:T(8,128)(2,1)S(1)}, bf16[400,2048]{1,0:T(8,128)(2,1)}, u32[]{:S(2)}) copy-start(bf16[400,2048]{1,0:T(8,128)(2,1)} %copy-done.13) | copy-start | bytes 4915204
  81.2 4.4 %collective-permute-start.3 = (bf16[8,160,128]{2,1,0:T(8,128)(2,1)S(1)}, bf16[8,160,128]{2,1,0:T(8,128)(2,1)S(1)}, u32[]{:S(2)}, u32[]{:S(2)}) collective-permute-start(bf16[8,160,128]{2,1,0:T(8,128)(2,1)S(1)} %all_to_all.22.mine), channel_id=1, source_target_pairs={{0,1},{1,0},{2,3},{3,2},{4,5},{5,4},{6,7},{7,6},{8,9},{9,8},{10,11... | collective-permute-start | bytes 983048 | tf_op jit(solution)/shard_map/ppermute | solution.py:536

commit v4 on v3

--- a/solution.py
+++ b/solution.py
@@ -42,37 +42,6 @@
 
 def slope(v, t):
     return 0.65 + 0.35 * t + 0.35 * v * (1.0 - t * t)
-
-
-@functools.cache
-def split_matrix():
-    m = np.zeros((512, 640), np.float32)
-    for k, offset in enumerate((-1, 0, 1, 2, 3)):
-        for i in range(128):
-            if 4 * i + offset >= 0:
-                m[4 * i + offset, k * 128 + i] = 1.0
-    return m
-
-
-@functools.cache
-def band_matrices():
-    own = np.zeros((2, 2, 108, 192), np.float32)
-    rim = np.zeros((2, 108, 48), np.float32)
-    for i in range(2):
-        for j in range(2):
-            for a in range(3):
-                for b in range(3):
-                    x, y = 2 * i + a - 1, 2 * j + b - 1
-                    if y < 0:
-                        continue
-                    for e in range(3):
-                        for c in range(4):
-                            src = ((a * 3 + b) * 3 + e) * 4 + c
-                            if x >= 0:
-                                own[i, j, src, ((e * 4 + c) * 4 + x) * 4 + y] = 1.0
-                            else:
-                                rim[j, src, (e * 4 + c) * 4 + y] = 1.0
-    return own, rim
 
 
 def lane_ids(shape):
@@ -121,25 +90,20 @@
     return jnp.concatenate([mm(taps, ref[(*index, j)], TN).astype(BF) for j in range(2)], axis=0)
 
 
-def split_here():
-    z = lax.broadcasted_iota(jnp.int32, (512, LANES), 0)
-    m = lax.broadcasted_iota(jnp.int32, (512, LANES), 1)
-    return jnp.concatenate(
-        [jnp.where(z - 4 * m == k - 1, 1.0, 0.0).astype(BF) for k in range(5)], axis=1
-    )
-
-
-def band_here(i, j):
+def band_here(i, j, planes):
     row = lax.broadcasted_iota(jnp.int32, (108, 1), 0)
     tap = lax.shift_right_logical(row, 2)
     third = lax.shift_right_logical(tap * 43, 7)
     a = lax.shift_right_logical(third * 43, 7)
     e, b = tap - 3 * third, third - 3 * a
     row_key = (e * 4 + jnp.bitwise_and(row, 3)) * 64 + a * 8 + b
-    col = lax.broadcasted_iota(jnp.int32, (1, 192), 1)
-    x = jnp.bitwise_and(lax.shift_right_logical(col, 2), 3) - 2 * i + 1
+    col = lax.broadcasted_iota(jnp.int32, (1, 48 * planes), 1)
     y = jnp.bitwise_and(col, 3) - 2 * j + 1
-    col_key = lax.shift_right_logical(col, 4) * 64 + x * 8 + y
+    if planes == 4:
+        x = jnp.bitwise_and(lax.shift_right_logical(col, 2), 3) - 2 * i + 1
+        col_key = lax.shift_right_logical(col, 4) * 64 + x * 8 + y
+    else:
+        col_key = lax.shift_right_logical(col, 2) * 64 + y
     return jnp.where(row_key == col_key, 1.0, 0.0).astype(BF)
 
 
@@ -163,7 +127,7 @@
 
 
 OWN = (320, 192)
-NEAR = (80, 192, 128)
+NEAR = (80, 192, 128, 128)
 
 
 def separate(rows, split, out_ref, height, first, many):
@@ -176,10 +140,20 @@
             ].astype(BF)
 
 
-def first_kernel(v, w1, w2, out_ref, slope_ref, away_ref):
+def matrices_kernel(split_ref, own_ref, rim_ref):
+    z = lax.broadcasted_iota(jnp.int32, (512, LANES), 0)
+    m = lax.broadcasted_iota(jnp.int32, (512, LANES), 1)
+    for k in range(5):
+        split_ref[:, k * LANES : (k + 1) * LANES] = jnp.where(z - 4 * m == k - 1, 1.0, 0.0).astype(BF)
+    for j in range(2):
+        for i in range(2):
+            own_ref[i, j] = band_here(i, j, 4)
+        rim_ref[j] = band_here(0, j, 1)
+
+
+def first_kernel(v, w1, w2, split, own, out_ref, slope_ref, away_ref):
     x4_ref, a1_ref = parts(out_ref, *OWN)
-    split = split_here()
-    w = bands(w1[...].reshape(108, 32), {(j,): band_here(1, j) for j in range(2)})
+    w = bands(w1[...].reshape(108, 32), own, 1)
     w2a = taps_of(w2, 0)
     for q in range(4):
         rows = jnp.concatenate([v[4 * q + n].reshape(64, 512) for n in range(4)], axis=0)
@@ -192,10 +166,11 @@
 
 
 def second_kernel(
-    halo, split, w1, own, rim, w2, first_ref, wd1, out_ref, part_ref, wd1_ref, block_ref, wide_ref
+    halo, split, w1, own, rim, w2, first_ref, s1c, out_ref, part_ref, back_ref
 ):
     x4, a1c = parts(first_ref, *OWN)
-    xh_ref, a1_ref, slope_ref = parts(out_ref, *NEAR)
+    xh_ref, a1_ref, slope_ref, slope_c_ref = parts(out_ref, *NEAR)
+    slope_c_ref[...] = s1c[...]
     taps = w1[...].reshape(108, 32)
     w, wh = bands(taps, own, 0), bands(taps, rim)
     rows = jnp.concatenate([halo[n].reshape(16, 512) for n in range(S)], axis=0)
@@ -208,7 +183,16 @@
                 wh, xh_ref[s * 32 : s * 32 + 48, cols]
             )
             store_plane(h, s, cols, a1_ref, slope_ref)
-        part_ref[:, cols] = mm(taps_b, a1_ref[:, cols], TN) + mm(taps_c, a1c[:, cols], TN)
+        part = mm(taps_b, a1_ref[:, cols], TN) + mm(taps_c, a1c[:, cols], TN)
+        part_ref[:, cols] = part
+        back_ref[:, cols] = part.astype(BF)
+
+
+def between_kernel(part, away, wd1, w2, next2_ref, wd1_ref, block_ref, wide_ref):
+    for q in range(4):
+        cols = slice(q * CHUNK, (q + 1) * CHUNK)
+        h2 = part[:, cols].astype(F32) + away[:, cols].astype(F32)
+        next2_ref[:, cols] = slope(h2, jnp.tanh(h2)).astype(BF)
 
     def tap(a, e):
         return jnp.concatenate([w2[a, 1, e], w2[a, 2, e]], axis=0)
@@ -304,6 +288,7 @@
     for k, slab in enumerate((here, after)):
         rows = wd1[pl.ds(pl.multiple_of(slab * 64, 64), 64), :]
         gf_ref[k * 64 : (k + 1) * 64] = mm(rows, gdense1, NT)
+    gf_ref[64:128] = jnp.where(here < 31, gf_ref[64:128], 0.0)
 
     d1 = mm(fown[...], gdense1, TN)
     d2 = mm(gdense2, out1, TN)
@@ -342,7 +327,7 @@
 
 
 def back_kernel(
-    gf_ref, mix, small, first_ref, s1c, block, slope2, next2, near, out_ref,
+    gf_ref, mix, small, first_ref, block, slope2, next2, near, out_ref,
     g_ref, h_ref, w_ref, r_ref, rh_ref,
 ):
     x4, a1c = parts(first_ref, *OWN)
@@ -360,14 +345,14 @@
         g_ref[128:192, cols] = shift_down(go).astype(BF)
         g_ref[192:256, cols] = shift_down(gn).astype(BF)
         gact = mm(block[...], g_ref[:, cols])
-        s1b = parts(near, *NEAR)[2]
+        s1b, s1c = parts(near, *NEAR)[2:]
         for s in range(2):
             for i, s1 in enumerate((s1b, s1c)):
                 r = (2 * s + i) * 64
                 h_ref[s, i * 64 : (i + 1) * 64, cols] = (
                     gact[r : r + 64] * s1[s * 64 : (s + 1) * 64, cols].astype(F32)
                 ).astype(BF)
-    xh, a1b, _ = parts(near, *NEAR)
+    xh, a1b = parts(near, *NEAR)[:2]
     w_ref[0:192] = mm(a1c[...], g_ref[0:128, :], NT)
     a1 = mm(a1b[...], g_ref[0:64, :], NT)
     w_ref[192:288] = jnp.concatenate([a1[0:96], a1[96:192]], axis=1)
@@ -470,8 +455,12 @@
     forward = [(i, i + 1) for i in range(31)]
     backward = [(i + 1, i) for i in range(31)]
     swap = [(0, 1), (1, 0)]
-    split = jnp.asarray(split_matrix(), BF)
-    own, rim = (jnp.asarray(m, BF) for m in band_matrices())
+    split, own, rim = call(
+        matrices_kernel,
+        [((512, 640), BF), ((2, 2, 108, 192), BF), ((2, 108, 48), BF)],
+        (),
+        flops=2 * 10**9,
+    )
     w1 = jnp.swapaxes(w_conv1, 3, 4).reshape(27, 4, 32)
     w2 = jnp.swapaxes(w_conv2, 3, 4)
 
@@ -479,30 +468,31 @@
     held_own, held_slope, away = call(
         first_kernel,
         [((sum(OWN), WIDE), BF), ((128, WIDE), BF), ((64, WIDE), BF)],
-        (volumes, w1, w2),
+        (volumes, w1, w2, split, own),
         flops=10**9,
     )
     got = lax.ppermute(away, SLABS, forward)
-    held_near, part, wd1, block = call(
+    held_near, part, part_back = call(
         second_kernel,
-        [
-            ((sum(NEAR), WIDE), BF), ((64, WIDE), F32), ((2048, LANES), BF),
-            ((256, 256), BF),
-        ],
-        (
-            halo, split, w1, own, rim, w2, held_own, w_dense1,
-        ),
-        scratch=[pltpu.VMEM((2048, LANES), F32)],
+        [((sum(NEAR), WIDE), BF), ((64, WIDE), F32), ((64, WIDE), BF)],
+        (halo, split, w1, own, rim, w2, held_own, held_slope),
         flops=2 * 10**9,
     )
+    part_next = lax.ppermute(part_back, SLABS, backward)
     slope2, pay, fown = call(
         third_kernel,
         [((64, WIDE), BF), ((32, 8, LANES), BF), ((S, LANES), BF)],
         (part, got),
+        flops=3 * 10**9,
+    )
+    gathered = lax.all_to_all(pay, SLABS, 0, 0, tiled=True)
+    next2, wd1, block = call(
+        between_kernel,
+        [((64, WIDE), BF), ((2048, LANES), BF), ((256, 256), BF)],
+        (part_next, away, w_dense1, w2),
+        scratch=[pltpu.VMEM((2048, LANES), F32)],
         flops=10**8,
     )
-    gathered = lax.all_to_all(pay, SLABS, 0, 0, tiled=True)
-    next2 = lax.ppermute(slope2, SLABS, backward)
     gf, mix, small = call(
         tail_kernel,
         [((LANES, S), F32), ((LANES, LANES), F32), ((8, LANES), F32)],
@@ -514,7 +504,7 @@
     (scattered,) = call(
         back_kernel,
         [((16, 48, LANES), BF)],
-        (gf, mix, small, held_own, held_slope, block, slope2, next2, held_near),
+        (gf, mix, small, held_own, block, slope2, next2, held_near),
         scratch=[
             pltpu.VMEM((256, WIDE), BF), pltpu.VMEM((2, 128, WIDE), BF),
             pltpu.VMEM((16 * PART, LANES), F32), pltpu.VMEM((192, LANES), F32),

time: 87.8 us -> 83.2 us (0.948)
  local copies, waits for them, and re-layouts: 6.31 us -> 1.61 us
  waiting for transfers between devices: 8.68 us -> 9.93 us
  blocking collectives: 33.8 us -> 32.8 us
    unnamed x34 -> x24, local copies, waits for them, and re-layouts: 5.2 us -> 0.56 us
    all_to_all x1, waiting for transfers between devices: 7.42 us -> 8.67 us  [local(): gathered = lax.all_to_all(pay, SLABS, 0, 0, tiled=True)]
    all_to_all x1, blocking collectives: 12.6 us -> 11.6 us  [local(): over_column = lax.all_to_all(to_column, COLUMN, 0, 0, tiled=True)]
    pallas_call x8 -> x10, Pallas kernels: 12.6 us -> 13.2 us  [call(): pl.pallas_call(kernel, out_shape=[jax.ShapeDtypeStruct(s, d) for s, d in...]
where the time goes in v4:
time: 83.2 us; the launch traced here: 82.8 us
  blocking collectives  32.8 us (39%)
  starting transfers between devices  24.3 us (29%)
  Pallas kernels  13.2 us (16%)
  waiting for transfers between devices  9.93 us (12%)
  local copies, waits for them, and re-layouts  1.61 us (2%)
  between operations  0.9 us (1%)
    pallas_call x10, Pallas kernels, call(): pl.pallas_call(kernel, out_shape=[jax.ShapeDtypeStruct(s, d) for s, d in...  13.2 us
    all_to_all x1, blocking collectives, local(): over_group = lax.all_to_all(scattered, (*DP, 'core'), 0, 0, tiled=True)  12.3 us
    all_to_all x1, starting transfers between devices, local(): gathered = lax.all_to_all(pay, SLABS, 0, 0, tiled=True)  12.2 us
    all_to_all x1, blocking collectives, local(): over_column = lax.all_to_all(to_column, COLUMN, 0, 0, tiled=True)  11.6 us
    all_to_all x1, blocking collectives, local(): summed = lax.all_to_all(back, DP, 0, 0, tiled=True)  8.98 us
    all_to_all x1, waiting for transfers between devices, local(): gathered = lax.all_to_all(pay, SLABS, 0, 0, tiled=True)  8.67 us
    ppermute x1, starting transfers between devices, local(): halo = lax.ppermute(volumes[:, :, 3], SLABS, forward)  5.07 us
    ppermute x1, starting transfers between devices, local(): other = lax.ppermute(summed, 'core', swap)  2.66 us
  transfers between devices with their start and end apart: 5, of which 2 were waited for; matrix products, arithmetic and copies ran while one was open for 0% of the time, Pallas kernels for 8%

profile of v4, /device:TPU:1, one launch (start us, length us, event | category | flops | bytes accessed | tf_op | source)
XLA Modules:
  0.0 82.8 jit_solution(11407990654500766020)
XLA Ops:
  0.6 1.1 %slice_bitcast_fusion = bf16[16,4,4,512]{3,2,1,0:T(4,128)(2,1)S(1)} fusion(bf16[16,4,4,4,512]{4,3,2,1,0:T(4,128)(2,1)} %v.1), kind=kLoop, calls=%fused_computation | loop fusion | bytes 524288 | tf_op jit(solution)/shard_map/squeeze | solution.py:467
  1.7 0.0 copy-start.1
  1.7 0.0 copy-start.2
  1.7 0.0 copy-start.3
  1.7 5.1 %collective-permute-start = (bf16[16,4,4,512]{3,2,1,0:T(4,128)(2,1)S(1)}, bf16[16,4,4,512]{3,2,1,0:T(4,128)(2,1)S(1)}, u32[]{:S(2)}, u32[]{:S(2)}) collective-permute-start(bf16[16,4,4,512]{3,2,1,0:T(4,128)(2,1)S(1)} %slice_bitcast_fusion), channel_id=1, source_target_pairs={{0,1},{1,2},{2,3},{3,4},{4,5},{5,6},{6,7},{7,8},{8,9},{9,10},{10,1... | collective-permute-start | bytes 786440 | tf_op jit(solution)/shard_map/ppermute | solution.py:467
  6.8 0.2 shard_map.127
  7.1 0.0 copy-done.1
  7.1 0.0 copy-done.2
  7.1 0.0 copy-done.3
  7.1 2.8 %shard_map.128 = (bf16[512,2048]{1,0:T(8,128)(2,1)S(1)}, bf16[128,2048]{1,0:T(8,128)(2,1)S(1)}, bf16[64,2048]{1,0:T(8,128)(2,1)S(1)}) custom-call(bf16[16,4,4,4,512]{4,3,2,1,0:T(4,128)(2,1)S(1)} %copy-done.2, bf16[27,4,32]{2,1,0:T(4,128)(2,1)S(1)} %bitcast.21, bf16[3,3,3,32,64]{4,3,2,1,0:T(8,128)(2,1)S(1)} %bitcast.18, ...), custom_call_target="tpu_custom_call" | custom-call | flops 1000000000 | bytes 2883584 | tf_op jit(solution)/shard_map/pallas_call | solution.py:69
  9.9 0.0 copy-start.8
  9.9 1.9 %collective-permute-start.1 = (bf16[64,2048]{1,0:T(8,128)(2,1)S(1)}, bf16[64,2048]{1,0:T(8,128)(2,1)S(1)}, u32[]{:S(2)}, u32[]{:S(2)}) collective-permute-start(bf16[64,2048]{1,0:T(8,128)(2,1)S(1)} %get-tuple-element.38.away), channel_id=1, source_target_pairs={{0,1},{1,2},{2,3},{3,4},{4,5},{5,6},{6,7},{7,8},{8,9},{9,10},{10,1... | collective-permute-start | bytes 786440 | tf_op jit(solution)/shard_map/ppermute | solution.py:474
  11.9 0.0 collective-permute-done.halo
  11.9 2.0 %shard_map.129 = (bf16[528,2048]{1,0:T(8,128)(2,1)S(1)}, f32[64,2048]{1,0:T(8,128)S(1)}, bf16[64,2048]{1,0:T(8,128)(2,1)S(1)}) custom-call(bf16[16,4,4,512]{3,2,1,0:T(4,128)(2,1)S(1)} %collective-permute-done.halo, bf16[512,640]{1,0:T(8,128)(2,1)S(1)} %get-tuple-element.32.split, bf16[27,4,32]{2,1,0:T(4,128)(2,1)S(1)} %bitcast.22, ...), custom_call_target="tpu_custom_call" | custom-call | flops 2000000000 | bytes 2949120 | tf_op jit(solution)/shard_map/pallas_call | solution.py:69
  13.8 0.0 copy-done.8
  13.8 0.0 copy-start.10
  13.9 2.4 %collective-permute-start.2 = (bf16[64,2048]{1,0:T(8,128)(2,1)S(1)}, bf16[64,2048]{1,0:T(8,128)(2,1)S(1)}, u32[]{:S(2)}, u32[]{:S(2)}) collective-permute-start(bf16[64,2048]{1,0:T(8,128)(2,1)S(1)} %get-tuple-element.40), channel_id=1, source_target_pairs={{1,0},{2,1},{3,2},{4,3},{5,4},{6,5},{7,6},{8,7},{9,8},{10,9},{11,1... | collective-permute-start | bytes 786440 | tf_op jit(solution)/shard_map/ppermute | solution.py:481
  16.3 0.0 collective-permute-done.1.got
  16.3 0.0 copy-start
  16.3 0.0 copy-start.4
  16.3 0.0 copy-start.5
  16.3 0.0 copy-start.6
  16.3 0.0 copy-start.7
  16.4 1.0 %shard_map.130 = (bf16[64,2048]{1,0:T(8,128)(2,1)S(1)}, bf16[32,8,128]{2,1,0:T(8,128)(2,1)}, bf16[16,128]{1,0:T(8,128)(2,1)S(1)}) custom-call(f32[64,2048]{1,0:T(8,128)S(1)} %get-tuple-element.37.part, bf16[64,2048]{1,0:T(8,128)(2,1)S(1)} %collective-permute-done.1.got), custom_call_target="tpu_custom_call" | custom-call | flops 3000000000 | bytes 331776 | tf_op jit(solution)/shard_map/pallas_call | solution.py:69
  17.4 0.0 copy-done.10
  17.4 12.2 %all-to-all-start = ((bf16[32,8,128]{2,1,0:T(8,128)(2,1)}), bf16[32,8,128]{2,1,0:T(8,128)(2,1)S(1)}, u32[]{:S(2)}, u32[]{:S(2)}) async-start(bf16[32,8,128]{2,1,0:T(8,128)(2,1)} %get-tuple-element.39), calls=%async_computation | async-start | bytes 131072 | tf_op jit(solution)/shard_map/all_to_all | solution.py:488
  29.7 0.0 collective-permute-done.2.part
  29.7 0.0 copy-done
  29.7 0.9 %shard_map.131 = (bf16[64,2048]{1,0:T(8,128)(2,1)S(1)}, bf16[2048,128]{1,0:T(8,128)(2,1)S(1)}, bf16[256,256]{1,0:T(8,128)(2,1)S(1)}) custom-call(bf16[64,2048]{1,0:T(8,128)(2,1)S(1)} %collective-permute-done.2.part, bf16[64,2048]{1,0:T(8,128)(2,1)S(1)} %get-tuple-element.38.away, bf16[2048,128]{1,0:T(8,128)(2,1)S(1)} %copy-done, ...), custom_call_target="tpu_custom_call" | custom-call | flops 100000000 | bytes 917504 | tf_op jit(solution)/shard_map/pallas_call | solution.py:69
  30.6 8.7 %all-to-all-done.g = bf16[32,8,128]{2,1,0:T(8,128)(2,1)S(1)} async-done(((bf16[32,8,128]{2,1,0:T(8,128)(2,1)}), bf16[32,8,128]{2,1,0:T(8,128)(2,1)S(1)}, u32[]{:S(2)}, u32[]{:S(2)}) %all-to-all-start) | async-done | bytes 65568 | tf_op jit(solution)/shard_map/all_to_all | solution.py:488
  39.2 0.0 copy-done.4
  39.2 0.0 copy-done.5
  39.2 0.0 copy-done.6
  39.2 0.0 copy-done.7
  39.2 0.0 copy-start.9
  39.3 0.0 copy-start.11
  39.3 1.7 %shard_map.132 = (f32[128,16]{1,0:T(8,128)S(1)}, f32[128,128]{1,0:T(8,128)S(1)}, f32[8,128]{1,0:T(8,128)S(1)}) custom-call(s32[32]{0:T(128)S(1)} %copy-done.7, s32[1]{0:T(128)} %bitcast.position, bf16[32,8,128]{2,1,0:T(8,128)(2,1)S(1)} %all-to-all-done.g, bf16[2048,128]{1,0:T(8,128)(2,1)S(1)} %get-tuple-element.41.wd1, bf16[64,128]{1,0:T(8,128)(2,1)S(1)} %bitcast.23, ...), custom_call_target="tpu_custom_call" | custom-call | flops 2000000000 | bytes 77824 | tf_op jit(solution)/shard_map/pallas_call | solution.py:69
  41.0 0.0 copy-done.9
  41.0 0.5 copy-done.11
  41.5 2.2 %shard_map.133 = bf16[16,48,128]{2,1,0:T(8,128)(2,1)S(1)} custom-call(f32[128,16]{1,0:T(8,128)S(1)} %get-tuple-element.43.gf_ref, f32[128,128]{1,0:T(8,128)S(1)} %get-tuple-element.44.mix, f32[8,128]{1,0:T(8,128)S(1)} %get-tuple-element.45.small, bf16[512,2048]{1,0:T(8,128)(2,1)S(1)} %copy-done.9, bf16[256,256]{1,0:T(8,128)(2,1)S(1)} %get-tuple-element.46.block, ...), custom_call_target="tpu_custom_call" | custom-call | flops 2000000000 | bytes 196608 | tf_op jit(solution)/shard_map/pallas_call | solution.py:69
  43.7 12.3 %all_to_all.20.got = bf16[16,48,128]{2,1,0:T(8,128)(2,1)S(1)} all-to-all(bf16[16,48,128]{2,1,0:T(8,128)(2,1)S(1)} %shard_map.133), channel_id=1, replica_groups=mesh['x'=4,'yl'=2,'yh'=2,'z'=8,'core'=2] {'x','yl','core'}, dimensions={0} | all-to-all | bytes 393216 | tf_op jit(solution)/shard_map/all_to_all | solution.py:515
  56.0 0.6 shard_map.134
  56.6 11.6 %all_to_all.21.got = bf16[16,32,128]{2,1,0:T(8,128)(2,1)S(1)} all-to-all(bf16[16,32,128]{2,1,0:T(8,128)(2,1)S(1)} %get-tuple-element.51), channel_id=1, replica_groups=mesh['x'=4,'yl'=2,'yh'=2,'z'=8,'core'=2] {'yh','z'}, dimensions={0} | all-to-all | bytes 262144 | tf_op jit(solution)/shard_map/all_to_all | solution.py:521
  68.2 9.0 %all_to_all.22.mine = bf16[8,160,128]{2,1,0:T(8,128)(2,1)S(1)} all-to-all(bf16[8,160,128]{2,1,0:T(8,128)(2,1)S(1)} %shard_map.135), channel_id=1, replica_groups=mesh['x'=4,'yl'=2,'yh'=2,'z'=8,'core'=2] {'x','yl'}, dimensions={0} | all-to-all | bytes 655360 | tf_op jit(solution)/shard_map/all_to_all | solution.py:525
  77.2 2.7 %collective-permute-start.3 = (bf16[8,160,128]{2,1,0:T(8,128)(2,1)S(1)}, bf16[8,160,128]{2,1,0:T(8,128)(2,1)S(1)}, u32[]{:S(2)}, u32[]{:S(2)}) collective-permute-start(bf16[8,160,128]{2,1,0:T(8,128)(2,1)S(1)} %all_to_all.22.mine), channel_id=1, source_target_pairs={{0,1},{1,0},{2,3},{3,2},{4,5},{5,4},{6,7},{7,6},{8,9},{9,8},{10,11... | collective-permute-start | bytes 983048 | tf_op jit(solution)/shard_map/ppermute | solution.py:526
  79.9 1.3 %collective-permute-done.3.other = bf16[8,160,128]{2,1,0:T(8,128)(2,1)S(1)} collective-permute-done((bf16[8,160,128]{2,1,0:T(8,128)(2,1)S(1)}, bf16[8,160,128]{2,1,0:T(8,128)(2,1)S(1)}, u32[]{:S(2)}, u32[]{:S(2)}) %collective-permute-start.3) | collective-permute-done | bytes 327712 | tf_op jit(solution)/shard_map/ppermute | solution.py:526
  81.1 1.7 %shard_map.136 = (f32[3,3,3,4,32]{4,3,2,1,0:T(4,128)}, f32[3,3,3,32,64]{4,3,2,1,0:T(8,128)}, f32[2048,128]{1,0:T(8,128)}, f32[64,128]{1,0:T(8,128)}) custom-call(s32[1]{0:T(128)} %bitcast.10.core, bf16[8,160,128]{2,1,0:T(8,128)(2,1)S(1)} %all_to_all.22.mine, bf16[8,160,128]{2,1,0:T(8,128)(2,1)S(1)} %collective-permute-done.3.other), custom_call_target="tpu_custom_call" | custom-call | flops 100000000 | bytes 1316352 | tf_op jit(solution)/shard_map/pallas_call | solution.py:69
  (1 shorter events, 0.0 us)
Async XLA Ops:
  1.7 5.4 %copy-start.1 = (bf16[3,3,3,64,32]{3,4,2,1,0:T(8,128)(2,1)S(1)}, bf16[3,3,3,64,32]{3,4,2,1,0:T(8,128)(2,1)}, u32[]{:S(2)}) copy-start(bf16[3,3,3,64,32]{3,4,2,1,0:T(8,128)(2,1)} %param.12) | copy-start | bytes 331780
  1.7 5.4 %copy-start.2 = (bf16[16,4,4,4,512]{4,3,2,1,0:T(4,128)(2,1)S(1)}, bf16[16,4,4,4,512]{4,3,2,1,0:T(4,128)(2,1)}, u32[]{:S(2)}) copy-start(bf16[16,4,4,4,512]{4,3,2,1,0:T(4,128)(2,1)} %v.1) | copy-start | bytes 3145732
  1.7 5.4 %copy-start.3 = (bf16[3,3,3,32,4]{3,4,2,1,0:T(4,128)(2,1)S(1)}, bf16[3,3,3,32,4]{3,4,2,1,0:T(4,128)(2,1)}, u32[]{:S(2)}) copy-start(bf16[3,3,3,32,4]{3,4,2,1,0:T(4,128)(2,1)} %param.11) | copy-start | bytes 20740
  1.7 10.1 %collective-permute-start = (bf16[16,4,4,512]{3,2,1,0:T(4,128)(2,1)S(1)}, bf16[16,4,4,512]{3,2,1,0:T(4,128)(2,1)S(1)}, u32[]{:S(2)}, u32[]{:S(2)}) collective-permute-start(bf16[16,4,4,512]{3,2,1,0:T(4,128)(2,1)S(1)} %slice_bitcast_fusion), channel_id=1, source_target_pairs={{0,1},{1,2},{2,3},{3,4},{4,5},{5,6},{6,7},{7,8},{8,9},{9,10},{10,1... | collective-permute-start | bytes 786440 | tf_op jit(solution)/shard_map/ppermute | solution.py:467
  9.9 3.9 %copy-start.8 = (bf16[512,2048]{1,0:T(8,128)(2,1)}, bf16[512,2048]{1,0:T(8,128)(2,1)S(1)}, u32[]{:S(2)}) copy-start(bf16[512,2048]{1,0:T(8,128)(2,1)S(1)} %get-tuple-element.35.first_ref) | copy-start | bytes 6291460
  9.9 6.4 %collective-permute-start.1 = (bf16[64,2048]{1,0:T(8,128)(2,1)S(1)}, bf16[64,2048]{1,0:T(8,128)(2,1)S(1)}, u32[]{:S(2)}, u32[]{:S(2)}) collective-permute-start(bf16[64,2048]{1,0:T(8,128)(2,1)S(1)} %get-tuple-element.38.away), channel_id=1, source_target_pairs={{0,1},{1,2},{2,3},{3,4},{4,5},{5,6},{6,7},{7,8},{8,9},{9,10},{10,1... | collective-permute-start | bytes 786440 | tf_op jit(solution)/shard_map/ppermute | solution.py:474
  13.8 3.5 %copy-start.10 = (bf16[528,2048]{1,0:T(8,128)(2,1)}, bf16[528,2048]{1,0:T(8,128)(2,1)S(1)}, u32[]{:S(2)}) copy-start(bf16[528,2048]{1,0:T(8,128)(2,1)S(1)} %get-tuple-element.49.near) | copy-start | bytes 6488068
  13.9 15.8 %collective-permute-start.2 = (bf16[64,2048]{1,0:T(8,128)(2,1)S(1)}, bf16[64,2048]{1,0:T(8,128)(2,1)S(1)}, u32[]{:S(2)}, u32[]{:S(2)}) collective-permute-start(bf16[64,2048]{1,0:T(8,128)(2,1)S(1)} %get-tuple-element.40), channel_id=1, source_target_pairs={{1,0},{2,1},{3,2},{4,3},{5,4},{6,5},{7,6},{8,7},{9,8},{10,9},{11,1... | collective-permute-start | bytes 786440 | tf_op jit(solution)/shard_map/ppermute | solution.py:481
  16.3 13.4 %copy-start = (bf16[2048,128]{1,0:T(8,128)(2,1)S(1)}, bf16[2048,128]{1,0:T(8,128)(2,1)}, u32[]{:S(2)}) copy-start(bf16[2048,128]{1,0:T(8,128)(2,1)} %wd1.1) | copy-start | bytes 1572868
  16.3 22.9 %copy-start.4 = (bf16[128,64]{0,1:T(8,128)(2,1)S(1)}, bf16[128,64]{0,1:T(8,128)(2,1)}, u32[]{:S(2)}) copy-start(bf16[128,64]{0,1:T(8,128)(2,1)} %param.14) | copy-start | bytes 49156
  16.3 22.9 %copy-start.5 = (f32[16,4]{0,1:T(4,128)S(1)}, f32[16,4]{0,1:T(4,128)}, u32[]{:S(2)}) copy-start(f32[16,4]{0,1:T(4,128)} %param.9) | copy-start | bytes 772
  16.3 22.9 %copy-start.6 = (bf16[64,4]{0,1:T(4,128)(2,1)S(1)}, bf16[64,4]{0,1:T(4,128)(2,1)}, u32[]{:S(2)}) copy-start(bf16[64,4]{0,1:T(4,128)(2,1)} %param.15) | copy-start | bytes 1540
  16.3 22.9 %copy-start.7 = (s32[32]{0:T(128)S(1)}, s32[32]{0:T(128)}, u32[]{:S(2)}) copy-start(s32[32]{0:T(128)} %counts.1) | copy-start | bytes 388
  17.4 21.8 %all-to-all-start = ((bf16[32,8,128]{2,1,0:T(8,128)(2,1)}), bf16[32,8,128]{2,1,0:T(8,128)(2,1)S(1)}, u32[]{:S(2)}, u32[]{:S(2)}) async-start(bf16[32,8,128]{2,1,0:T(8,128)(2,1)} %get-tuple-element.39), calls=%async_computation | async-start | bytes 131072 | tf_op jit(solution)/shard_map/all_to_all | solution.py:488
  39.2 1.7 %copy-start.9 = (bf16[512,2048]{1,0:T(8,128)(2,1)S(1)}, bf16[512,2048]{1,0:T(8,128)(2,1)}, u32[]{:S(2)}) copy-start(bf16[512,2048]{1,0:T(8,128)(2,1)} %copy-done.8) | copy-start | bytes 6291460
  39.3 2.2 %copy-start.11 = (bf16[528,2048]{1,0:T(8,128)(2,1)S(1)}, bf16[528,2048]{1,0:T(8,128)(2,1)}, u32[]{:S(2)}) copy-start(bf16[528,2048]{1,0:T(8,128)(2,1)} %copy-done.10) | copy-start | bytes 6488068
  77.2 3.9 %collective-permute-start.3 = (bf16[8,160,128]{2,1,0:T(8,128)(2,1)S(1)}, bf16[8,160,128]{2,1,0:T(8,128)(2,1)S(1)}, u32[]{:S(2)}, u32[]{:S(2)}) collective-permute-start(bf16[8,160,128]{2,1,0:T(8,128)(2,1)S(1)} %all_to_all.22.mine), channel_id=1, source_target_pairs={{0,1},{1,0},{2,3},{3,2},{4,5},{5,4},{6,7},{7,6},{8,9},{9,8},{10,11... | collective-permute-start | bytes 983048 | tf_op jit(solution)/shard_map/ppermute | solution.py:526

commit v5 on v4

--- a/solution.py
+++ b/solution.py
@@ -30,10 +30,11 @@
     return lax.dot_general(a, b, dims, preferred_element_type=F32)
 
 
-def mm_exact(a, b):
-    return lax.dot_general(
-        a, b, NN, preferred_element_type=F32, precision=lax.Precision.HIGHEST
-    )
+def three(x):
+    high = x.astype(BF)
+    rest = x - high.astype(F32)
+    mid = rest.astype(BF)
+    return high, mid, (rest - mid.astype(F32)).astype(BF)
 
 
 def leaky(v, t):
@@ -231,12 +232,6 @@
     fown_ref[...] = jnp.concatenate([feats, jnp.zeros((S, 64), F32)], axis=1).astype(BF)
 
 
-def split_loss(loss):
-    high = loss.astype(BF).astype(F32)
-    mid = (loss - high).astype(BF).astype(F32)
-    return high, mid, loss - high - mid
-
-
 def tail_kernel(
     counts, position, g, wd1, wd2, wd3, targets, fown, gf_ref, mix_ref, small_ref, padded_ref
 ):
@@ -251,7 +246,8 @@
         row_owner = row_owner + jnp.where(by_row >= end, 1, 0)
         col_owner = col_owner + jnp.where(by_col >= end, 1, 0)
     alike = jnp.where(row_owner == col_owner, 1.0, 0.0)
-    same = alike / jnp.sum(alike, axis=1, keepdims=True)
+    same = (alike / jnp.sum(alike, axis=1, keepdims=True)).astype(BF)
+    same = jnp.concatenate([same] * 3, axis=1)
 
     low = lane_ids((8, LANES)) < 64
     pairs = []
@@ -262,7 +258,7 @@
         pairs.append(jnp.concatenate([lo, hi], axis=0).astype(BF))
     feats = jnp.concatenate(pairs, axis=1)
     dense1 = mm(feats, wd1[...])
-    centred = dense1 - 0.5 * mm_exact(same, dense1)
+    centred = dense1 - 0.5 * mm(same, jnp.concatenate(three(dense1), axis=0))
     t1 = jnp.tanh(centred)
     out1 = leaky(centred, t1).astype(BF)
 
@@ -282,7 +278,7 @@
     gpred = (diff / 16.0).astype(BF)
     gdense2 = (mm(gpred, w3) * slope(dense2, t2)).astype(BF)
     gcentred = mm(gdense2, w2) * slope(centred, t1)
-    gdense1 = (gcentred - 0.5 * mm_exact(same, gcentred)).astype(BF)
+    gdense1 = (gcentred - 0.5 * mm(same, jnp.concatenate(three(gcentred), axis=0))).astype(BF)
     here = position[0]
     after = jnp.minimum(here + 1, 31)
     for k, slab in enumerate((here, after)):
@@ -295,12 +291,13 @@
     d3 = mm(gpred, out2, TN)[64:72]
     lanes = lane_ids((8, LANES))
     top = lax.broadcasted_iota(jnp.int32, (8, LANES), 0) == 0
-    for k, piece in enumerate(split_loss(loss)):
-        d3 = jnp.where(jnp.logical_and(top, lanes == 64 + k), piece, d3)
+    for k, piece in enumerate(three(loss)):
+        d3 = jnp.where(jnp.logical_and(top, lanes == 64 + k), piece.astype(F32), d3)
     small_ref[...] = d3
-    for p in range(16):
-        mix_ref[p * 8 : p * 8 + 4] = d1[p * 4 : p * 4 + 4]
-        mix_ref[p * 8 + 4 : p * 8 + 8] = d2[p * 4 : p * 4 + 4]
+    for k in range(8):
+        pair = d1[k * 8 : (k + 1) * 8], d2[k * 8 : (k + 1) * 8]
+        mix_ref[k * 16 : k * 16 + 8] = low_half(*pair)
+        mix_ref[k * 16 + 8 : k * 16 + 16] = high_half(*pair)
 
 
 def tap_sums(r_ref, rh_ref):
@@ -413,19 +410,20 @@
         out_ref[k] = pay
 
 
-def last_kernel(core, mine, other, gw1_ref, gw2_ref, gd1_ref, gd2_ref, w_ref):
+def last_kernel(core, mine, other, gw1_ref, gw2_ref, gd1_ref, gd2_ref, w_ref, t_ref):
     first = core[0] == 0
     for k in range(8):
-        a, b = mine[k].astype(F32), other[k].astype(F32)
+        for n, chunk in enumerate((mine, other)):
+            t_ref[2 * k + n] = chunk[k, 32:160].astype(F32)
+            base = k * 256 + jnp.bitwise_xor(core[0], n) * 128
+            for r in range(4):
+                at = pl.multiple_of(base + r * 32, 32)
+                gd1_ref[pl.ds(at, 32), :] = t_ref[2 * k + n, pl.ds(r, 32, stride=4), :]
+        a, b = mine[k, 0:32].astype(F32), other[k, 0:32].astype(F32)
         low, high = jnp.where(first, a, b), jnp.where(first, b, a)
         w_ref[2 * k * PART : (2 * k + 1) * PART] = low[0:PART]
         w_ref[(2 * k + 1) * PART : (2 * k + 2) * PART] = high[0:PART]
         gd2_ref[k * 8 : (k + 1) * 8] = low_half(low[PART:32], high[PART:32])
-        for q in range(16):
-            at = 32 + 8 * q
-            lo, hi = low[at : at + 8], high[at : at + 8]
-            gd1_ref[pl.ds(k * 256 + 2 * q, 8, stride=32), :] = low_half(lo, hi)
-            gd1_ref[pl.ds(k * 256 + 2 * q + 1, 8, stride=32), :] = high_half(lo, hi)
     for a in range(3):
         for e in range(3):
             gw2_ref[a, 0, e] = jnp.zeros((32, 64), F32)
@@ -532,7 +530,7 @@
         ],
         (summed, other),
         scalars=(core,),
-        scratch=[pltpu.VMEM((16 * PART, LANES), F32)],
+        scratch=[pltpu.VMEM((16 * PART, LANES), F32), pltpu.VMEM((16, LANES, LANES), F32)],
     )
     return (
         loss.reshape(()), jnp.swapaxes(gw1, 3, 4), jnp.swapaxes(gw2, 3, 4), gd1, gd2.T, d3.T,

time: 83.2 us -> 82.8 us (level)
  no operation moved by 1% of the time
where the time goes in v5:
time: 82.8 us; the launch traced here: 82.5 us
  blocking collectives  32.8 us (40%)
  starting transfers between devices  24.3 us (29%)
  Pallas kernels  12.9 us (16%)
  waiting for transfers between devices  9.93 us (12%)
  local copies, waits for them, and re-layouts  1.64 us (2%)
  between operations  0.9 us (1%)
    pallas_call x10, Pallas kernels, call(): pl.pallas_call(kernel, out_shape=[jax.ShapeDtypeStruct(s, d) for s, d in...  12.9 us
    all_to_all x1, blocking collectives, local(): over_group = lax.all_to_all(scattered, (*DP, 'core'), 0, 0, tiled=True)  12.3 us
    all_to_all x1, starting transfers between devices, local(): gathered = lax.all_to_all(pay, SLABS, 0, 0, tiled=True)  12.2 us
    all_to_all x1, blocking collectives, local(): over_column = lax.all_to_all(to_column, COLUMN, 0, 0, tiled=True)  11.6 us
    all_to_all x1, blocking collectives, local(): summed = lax.all_to_all(back, DP, 0, 0, tiled=True)  8.98 us
    all_to_all x1, waiting for transfers between devices, local(): gathered = lax.all_to_all(pay, SLABS, 0, 0, tiled=True)  8.67 us
    ppermute x1, starting transfers between devices, local(): halo = lax.ppermute(volumes[:, :, 3], SLABS, forward)  5.07 us
    ppermute x1, starting transfers between devices, local(): other = lax.ppermute(summed, 'core', swap)  2.66 us
  transfers between devices with their start and end apart: 5, of which 2 were waited for; matrix products, arithmetic and copies ran while one was open for 0% of the time, Pallas kernels for 8%

profile of v5, /device:TPU:1, one launch (start us, length us, event | category | flops | bytes accessed | tf_op | source)
XLA Modules:
  0.0 82.5 jit_solution(10163442626211069163)
XLA Ops:
  0.6 1.1 %slice_bitcast_fusion = bf16[16,4,4,512]{3,2,1,0:T(4,128)(2,1)S(1)} fusion(bf16[16,4,4,4,512]{4,3,2,1,0:T(4,128)(2,1)} %v.1), kind=kLoop, calls=%fused_computation | loop fusion | bytes 524288 | tf_op jit(solution)/shard_map/squeeze | solution.py:465
  1.7 0.0 copy-start.1
  1.7 0.0 copy-start.2
  1.7 0.0 copy-start.3
  1.7 5.1 %collective-permute-start = (bf16[16,4,4,512]{3,2,1,0:T(4,128)(2,1)S(1)}, bf16[16,4,4,512]{3,2,1,0:T(4,128)(2,1)S(1)}, u32[]{:S(2)}, u32[]{:S(2)}) collective-permute-start(bf16[16,4,4,512]{3,2,1,0:T(4,128)(2,1)S(1)} %slice_bitcast_fusion), channel_id=1, source_target_pairs={{0,1},{1,2},{2,3},{3,4},{4,5},{5,6},{6,7},{7,8},{8,9},{9,10},{10,1... | collective-permute-start | bytes 786440 | tf_op jit(solution)/shard_map/ppermute | solution.py:465
  6.8 0.2 shard_map.127
  7.1 0.0 copy-done.1
  7.1 0.0 copy-done.2
  7.1 0.0 copy-done.3
  7.1 2.8 %shard_map.128 = (bf16[512,2048]{1,0:T(8,128)(2,1)S(1)}, bf16[128,2048]{1,0:T(8,128)(2,1)S(1)}, bf16[64,2048]{1,0:T(8,128)(2,1)S(1)}) custom-call(bf16[16,4,4,4,512]{4,3,2,1,0:T(4,128)(2,1)S(1)} %copy-done.2, bf16[27,4,32]{2,1,0:T(4,128)(2,1)S(1)} %bitcast.21, bf16[3,3,3,32,64]{4,3,2,1,0:T(8,128)(2,1)S(1)} %bitcast.18, ...), custom_call_target="tpu_custom_call" | custom-call | flops 1000000000 | bytes 2883584 | tf_op jit(solution)/shard_map/pallas_call | solution.py:70
  9.9 0.0 copy-start.8
  9.9 1.9 %collective-permute-start.1 = (bf16[64,2048]{1,0:T(8,128)(2,1)S(1)}, bf16[64,2048]{1,0:T(8,128)(2,1)S(1)}, u32[]{:S(2)}, u32[]{:S(2)}) collective-permute-start(bf16[64,2048]{1,0:T(8,128)(2,1)S(1)} %get-tuple-element.38.away), channel_id=1, source_target_pairs={{0,1},{1,2},{2,3},{3,4},{4,5},{5,6},{6,7},{7,8},{8,9},{9,10},{10,1... | collective-permute-start | bytes 786440 | tf_op jit(solution)/shard_map/ppermute | solution.py:472
  11.9 0.0 collective-permute-done.halo
  11.9 2.0 %shard_map.129 = (bf16[528,2048]{1,0:T(8,128)(2,1)S(1)}, f32[64,2048]{1,0:T(8,128)S(1)}, bf16[64,2048]{1,0:T(8,128)(2,1)S(1)}) custom-call(bf16[16,4,4,512]{3,2,1,0:T(4,128)(2,1)S(1)} %collective-permute-done.halo, bf16[512,640]{1,0:T(8,128)(2,1)S(1)} %get-tuple-element.32.split, bf16[27,4,32]{2,1,0:T(4,128)(2,1)S(1)} %bitcast.22, ...), custom_call_target="tpu_custom_call" | custom-call | flops 2000000000 | bytes 2949120 | tf_op jit(solution)/shard_map/pallas_call | solution.py:70
  13.8 0.0 copy-done.8
  13.8 0.0 copy-start.10
  13.9 2.4 %collective-permute-start.2 = (bf16[64,2048]{1,0:T(8,128)(2,1)S(1)}, bf16[64,2048]{1,0:T(8,128)(2,1)S(1)}, u32[]{:S(2)}, u32[]{:S(2)}) collective-permute-start(bf16[64,2048]{1,0:T(8,128)(2,1)S(1)} %get-tuple-element.40), channel_id=1, source_target_pairs={{1,0},{2,1},{3,2},{4,3},{5,4},{6,5},{7,6},{8,7},{9,8},{10,9},{11,1... | collective-permute-start | bytes 786440 | tf_op jit(solution)/shard_map/ppermute | solution.py:479
  16.3 0.0 collective-permute-done.1.got
  16.3 0.0 copy-start
  16.3 0.0 copy-start.4
  16.3 0.0 copy-start.5
  16.3 0.0 copy-start.6
  16.3 0.0 copy-start.7
  16.4 1.0 %shard_map.130 = (bf16[64,2048]{1,0:T(8,128)(2,1)S(1)}, bf16[32,8,128]{2,1,0:T(8,128)(2,1)}, bf16[16,128]{1,0:T(8,128)(2,1)S(1)}) custom-call(f32[64,2048]{1,0:T(8,128)S(1)} %get-tuple-element.37.part, bf16[64,2048]{1,0:T(8,128)(2,1)S(1)} %collective-permute-done.1.got), custom_call_target="tpu_custom_call" | custom-call | flops 3000000000 | bytes 331776 | tf_op jit(solution)/shard_map/pallas_call | solution.py:70
  17.4 0.0 copy-done.10
  17.4 12.2 %all-to-all-start = ((bf16[32,8,128]{2,1,0:T(8,128)(2,1)}), bf16[32,8,128]{2,1,0:T(8,128)(2,1)S(1)}, u32[]{:S(2)}, u32[]{:S(2)}) async-start(bf16[32,8,128]{2,1,0:T(8,128)(2,1)} %get-tuple-element.39), calls=%async_computation | async-start | bytes 131072 | tf_op jit(solution)/shard_map/all_to_all | solution.py:486
  29.7 0.0 collective-permute-done.2.part
  29.7 0.0 copy-done
  29.7 0.9 %shard_map.131 = (bf16[64,2048]{1,0:T(8,128)(2,1)S(1)}, bf16[2048,128]{1,0:T(8,128)(2,1)S(1)}, bf16[256,256]{1,0:T(8,128)(2,1)S(1)}) custom-call(bf16[64,2048]{1,0:T(8,128)(2,1)S(1)} %collective-permute-done.2.part, bf16[64,2048]{1,0:T(8,128)(2,1)S(1)} %get-tuple-element.38.away, bf16[2048,128]{1,0:T(8,128)(2,1)S(1)} %copy-done, ...), custom_call_target="tpu_custom_call" | custom-call | flops 100000000 | bytes 917504 | tf_op jit(solution)/shard_map/pallas_call | solution.py:70
  30.6 8.7 %all-to-all-done.g = bf16[32,8,128]{2,1,0:T(8,128)(2,1)S(1)} async-done(((bf16[32,8,128]{2,1,0:T(8,128)(2,1)}), bf16[32,8,128]{2,1,0:T(8,128)(2,1)S(1)}, u32[]{:S(2)}, u32[]{:S(2)}) %all-to-all-start) | async-done | bytes 65568 | tf_op jit(solution)/shard_map/all_to_all | solution.py:486
  39.2 0.0 copy-done.4
  39.2 0.0 copy-done.5
  39.2 0.0 copy-done.6
  39.2 0.0 copy-done.7
  39.2 0.0 copy-start.9
  39.3 0.0 copy-start.11
  39.3 1.7 %shard_map.132 = (f32[128,16]{1,0:T(8,128)S(1)}, f32[128,128]{1,0:T(8,128)S(1)}, f32[8,128]{1,0:T(8,128)S(1)}) custom-call(s32[32]{0:T(128)S(1)} %copy-done.7, s32[1]{0:T(128)} %bitcast.position, bf16[32,8,128]{2,1,0:T(8,128)(2,1)S(1)} %all-to-all-done.g, bf16[2048,128]{1,0:T(8,128)(2,1)S(1)} %get-tuple-element.41.wd1, bf16[64,128]{1,0:T(8,128)(2,1)S(1)} %bitcast.23, ...), custom_call_target="tpu_custom_call" | custom-call | flops 2000000000 | bytes 77824 | tf_op jit(solution)/shard_map/pallas_call | solution.py:70
  41.0 0.0 copy-done.9
  41.0 0.5 copy-done.11
  41.5 2.2 %shard_map.133 = bf16[16,48,128]{2,1,0:T(8,128)(2,1)S(1)} custom-call(f32[128,16]{1,0:T(8,128)S(1)} %get-tuple-element.43.gf_ref, f32[128,128]{1,0:T(8,128)S(1)} %get-tuple-element.44.mix, f32[8,128]{1,0:T(8,128)S(1)} %get-tuple-element.45.small, bf16[512,2048]{1,0:T(8,128)(2,1)S(1)} %copy-done.9, bf16[256,256]{1,0:T(8,128)(2,1)S(1)} %get-tuple-element.46.block, ...), custom_call_target="tpu_custom_call" | custom-call | flops 2000000000 | bytes 196608 | tf_op jit(solution)/shard_map/pallas_call | solution.py:70
  43.7 12.3 %all_to_all.20.got = bf16[16,48,128]{2,1,0:T(8,128)(2,1)S(1)} all-to-all(bf16[16,48,128]{2,1,0:T(8,128)(2,1)S(1)} %shard_map.133), channel_id=1, replica_groups=mesh['x'=4,'yl'=2,'yh'=2,'z'=8,'core'=2] {'x','yl','core'}, dimensions={0} | all-to-all | bytes 393216 | tf_op jit(solution)/shard_map/all_to_all | solution.py:513
  56.0 0.6 shard_map.134
  56.6 11.6 %all_to_all.21.got = bf16[16,32,128]{2,1,0:T(8,128)(2,1)S(1)} all-to-all(bf16[16,32,128]{2,1,0:T(8,128)(2,1)S(1)} %get-tuple-element.51), channel_id=1, replica_groups=mesh['x'=4,'yl'=2,'yh'=2,'z'=8,'core'=2] {'yh','z'}, dimensions={0} | all-to-all | bytes 262144 | tf_op jit(solution)/shard_map/all_to_all | solution.py:519
  68.2 9.0 %all_to_all.22.mine = bf16[8,160,128]{2,1,0:T(8,128)(2,1)S(1)} all-to-all(bf16[8,160,128]{2,1,0:T(8,128)(2,1)S(1)} %shard_map.135), channel_id=1, replica_groups=mesh['x'=4,'yl'=2,'yh'=2,'z'=8,'core'=2] {'x','yl'}, dimensions={0} | all-to-all | bytes 655360 | tf_op jit(solution)/shard_map/all_to_all | solution.py:523
  77.2 2.7 %collective-permute-start.3 = (bf16[8,160,128]{2,1,0:T(8,128)(2,1)S(1)}, bf16[8,160,128]{2,1,0:T(8,128)(2,1)S(1)}, u32[]{:S(2)}, u32[]{:S(2)}) collective-permute-start(bf16[8,160,128]{2,1,0:T(8,128)(2,1)S(1)} %all_to_all.22.mine), channel_id=1, source_target_pairs={{0,1},{1,0},{2,3},{3,2},{4,5},{5,4},{6,7},{7,6},{8,9},{9,8},{10,11... | collective-permute-start | bytes 983048 | tf_op jit(solution)/shard_map/ppermute | solution.py:524
  79.9 1.3 %collective-permute-done.3.other = bf16[8,160,128]{2,1,0:T(8,128)(2,1)S(1)} collective-permute-done((bf16[8,160,128]{2,1,0:T(8,128)(2,1)S(1)}, bf16[8,160,128]{2,1,0:T(8,128)(2,1)S(1)}, u32[]{:S(2)}, u32[]{:S(2)}) %collective-permute-start.3) | collective-permute-done | bytes 327712 | tf_op jit(solution)/shard_map/ppermute | solution.py:524
  81.1 1.3 %shard_map.136 = (f32[3,3,3,4,32]{4,3,2,1,0:T(4,128)}, f32[3,3,3,32,64]{4,3,2,1,0:T(8,128)}, f32[2048,128]{1,0:T(8,128)}, f32[64,128]{1,0:T(8,128)}) custom-call(s32[1]{0:T(128)} %bitcast.10.core, bf16[8,160,128]{2,1,0:T(8,128)(2,1)S(1)} %all_to_all.22.mine, bf16[8,160,128]{2,1,0:T(8,128)(2,1)S(1)} %collective-permute-done.3.other), custom_call_target="tpu_custom_call" | custom-call | flops 100000000 | bytes 1316352 | tf_op jit(solution)/shard_map/pallas_call | solution.py:70
  (1 shorter events, 0.0 us)
Async XLA Ops:
  1.7 5.4 %copy-start.1 = (bf16[3,3,3,64,32]{3,4,2,1,0:T(8,128)(2,1)S(1)}, bf16[3,3,3,64,32]{3,4,2,1,0:T(8,128)(2,1)}, u32[]{:S(2)}) copy-start(bf16[3,3,3,64,32]{3,4,2,1,0:T(8,128)(2,1)} %param.12) | copy-start | bytes 331780
  1.7 5.4 %copy-start.2 = (bf16[16,4,4,4,512]{4,3,2,1,0:T(4,128)(2,1)S(1)}, bf16[16,4,4,4,512]{4,3,2,1,0:T(4,128)(2,1)}, u32[]{:S(2)}) copy-start(bf16[16,4,4,4,512]{4,3,2,1,0:T(4,128)(2,1)} %v.1) | copy-start | bytes 3145732
  1.7 5.4 %copy-start.3 = (bf16[3,3,3,32,4]{3,4,2,1,0:T(4,128)(2,1)S(1)}, bf16[3,3,3,32,4]{3,4,2,1,0:T(4,128)(2,1)}, u32[]{:S(2)}) copy-start(bf16[3,3,3,32,4]{3,4,2,1,0:T(4,128)(2,1)} %param.11) | copy-start | bytes 20740
  1.7 10.1 %collective-permute-start = (bf16[16,4,4,512]{3,2,1,0:T(4,128)(2,1)S(1)}, bf16[16,4,4,512]{3,2,1,0:T(4,128)(2,1)S(1)}, u32[]{:S(2)}, u32[]{:S(2)}) collective-permute-start(bf16[16,4,4,512]{3,2,1,0:T(4,128)(2,1)S(1)} %slice_bitcast_fusion), channel_id=1, source_target_pairs={{0,1},{1,2},{2,3},{3,4},{4,5},{5,6},{6,7},{7,8},{8,9},{9,10},{10,1... | collective-permute-start | bytes 786440 | tf_op jit(solution)/shard_map/ppermute | solution.py:465
  9.9 3.9 %copy-start.8 = (bf16[512,2048]{1,0:T(8,128)(2,1)}, bf16[512,2048]{1,0:T(8,128)(2,1)S(1)}, u32[]{:S(2)}) copy-start(bf16[512,2048]{1,0:T(8,128)(2,1)S(1)} %get-tuple-element.35.first_ref) | copy-start | bytes 6291460
  9.9 6.4 %collective-permute-start.1 = (bf16[64,2048]{1,0:T(8,128)(2,1)S(1)}, bf16[64,2048]{1,0:T(8,128)(2,1)S(1)}, u32[]{:S(2)}, u32[]{:S(2)}) collective-permute-start(bf16[64,2048]{1,0:T(8,128)(2,1)S(1)} %get-tuple-element.38.away), channel_id=1, source_target_pairs={{0,1},{1,2},{2,3},{3,4},{4,5},{5,6},{6,7},{7,8},{8,9},{9,10},{10,1... | collective-permute-start | bytes 786440 | tf_op jit(solution)/shard_map/ppermute | solution.py:472
  13.8 3.5 %copy-start.10 = (bf16[528,2048]{1,0:T(8,128)(2,1)}, bf16[528,2048]{1,0:T(8,128)(2,1)S(1)}, u32[]{:S(2)}) copy-start(bf16[528,2048]{1,0:T(8,128)(2,1)S(1)} %get-tuple-element.49.near) | copy-start | bytes 6488068
  13.9 15.8 %collective-permute-start.2 = (bf16[64,2048]{1,0:T(8,128)(2,1)S(1)}, bf16[64,2048]{1,0:T(8,128)(2,1)S(1)}, u32[]{:S(2)}, u32[]{:S(2)}) collective-permute-start(bf16[64,2048]{1,0:T(8,128)(2,1)S(1)} %get-tuple-element.40), channel_id=1, source_target_pairs={{1,0},{2,1},{3,2},{4,3},{5,4},{6,5},{7,6},{8,7},{9,8},{10,9},{11,1... | collective-permute-start | bytes 786440 | tf_op jit(solution)/shard_map/ppermute | solution.py:479
  16.3 13.4 %copy-start = (bf16[2048,128]{1,0:T(8,128)(2,1)S(1)}, bf16[2048,128]{1,0:T(8,128)(2,1)}, u32[]{:S(2)}) copy-start(bf16[2048,128]{1,0:T(8,128)(2,1)} %wd1.1) | copy-start | bytes 1572868
  16.3 22.9 %copy-start.4 = (bf16[128,64]{0,1:T(8,128)(2,1)S(1)}, bf16[128,64]{0,1:T(8,128)(2,1)}, u32[]{:S(2)}) copy-start(bf16[128,64]{0,1:T(8,128)(2,1)} %param.14) | copy-start | bytes 49156
  16.3 22.9 %copy-start.5 = (f32[16,4]{0,1:T(4,128)S(1)}, f32[16,4]{0,1:T(4,128)}, u32[]{:S(2)}) copy-start(f32[16,4]{0,1:T(4,128)} %param.9) | copy-start | bytes 772
  16.3 22.9 %copy-start.6 = (bf16[64,4]{0,1:T(4,128)(2,1)S(1)}, bf16[64,4]{0,1:T(4,128)(2,1)}, u32[]{:S(2)}) copy-start(bf16[64,4]{0,1:T(4,128)(2,1)} %param.15) | copy-start | bytes 1540
  16.3 22.9 %copy-start.7 = (s32[32]{0:T(128)S(1)}, s32[32]{0:T(128)}, u32[]{:S(2)}) copy-start(s32[32]{0:T(128)} %counts.1) | copy-start | bytes 388
  17.4 21.8 %all-to-all-start = ((bf16[32,8,128]{2,1,0:T(8,128)(2,1)}), bf16[32,8,128]{2,1,0:T(8,128)(2,1)S(1)}, u32[]{:S(2)}, u32[]{:S(2)}) async-start(bf16[32,8,128]{2,1,0:T(8,128)(2,1)} %get-tuple-element.39), calls=%async_computation | async-start | bytes 131072 | tf_op jit(solution)/shard_map/all_to_all | solution.py:486
  39.2 1.7 %copy-start.9 = (bf16[512,2048]{1,0:T(8,128)(2,1)S(1)}, bf16[512,2048]{1,0:T(8,128)(2,1)}, u32[]{:S(2)}) copy-start(bf16[512,2048]{1,0:T(8,128)(2,1)} %copy-done.8) | copy-start | bytes 6291460
  39.3 2.2 %copy-start.11 = (bf16[528,2048]{1,0:T(8,128)(2,1)S(1)}, bf16[528,2048]{1,0:T(8,128)(2,1)}, u32[]{:S(2)}) copy-start(bf16[528,2048]{1,0:T(8,128)(2,1)} %copy-done.10) | copy-start | bytes 6488068
  77.2 3.9 %collective-permute-start.3 = (bf16[8,160,128]{2,1,0:T(8,128)(2,1)S(1)}, bf16[8,160,128]{2,1,0:T(8,128)(2,1)S(1)}, u32[]{:S(2)}, u32[]{:S(2)}) collective-permute-start(bf16[8,160,128]{2,1,0:T(8,128)(2,1)S(1)} %all_to_all.22.mine), channel_id=1, source_target_pairs={{0,1},{1,0},{2,3},{3,2},{4,5},{5,4},{6,7},{7,6},{8,9},{9,8},{10,11... | collective-permute-start | bytes 983048 | tf_op jit(solution)/shard_map/ppermute | solution.py:524

commit v6 on v5

--- a/solution.py
+++ b/solution.py
@@ -17,7 +17,9 @@
 S = 16
 LANES = 128
 WIDE = S * LANES
-CHUNK = 512
+CHUNK = 2048
+MANY = WIDE // CHUNK
+PER = CHUNK // LANES
 PART = 24
 SMALL = 16 * 1024 * 1024
 
@@ -156,13 +158,16 @@
     x4_ref, a1_ref = parts(out_ref, *OWN)
     w = bands(w1[...].reshape(108, 32), own, 1)
     w2a = taps_of(w2, 0)
-    for q in range(4):
-        rows = jnp.concatenate([v[4 * q + n].reshape(64, 512) for n in range(4)], axis=0)
-        separate(rows, split, x4_ref, 64, 4 * q, 4)
+    for q in range(MANY):
+        rows = jnp.concatenate([v[PER * q + n].reshape(64, 512) for n in range(PER)], axis=0)
+        separate(rows, split, x4_ref, 64, PER * q, PER)
+    for q in range(MANY):
         cols = slice(q * CHUNK, (q + 1) * CHUNK)
         for s in range(2):
             h = mm(w, x4_ref[s * 128 : s * 128 + 192, cols])
             store_plane(h, s, cols, a1_ref, slope_ref)
+    for q in range(MANY):
+        cols = slice(q * CHUNK, (q + 1) * CHUNK)
         away_ref[:, cols] = mm(w2a, a1_ref[:, cols], TN).astype(BF)
 
 
@@ -177,20 +182,22 @@
     rows = jnp.concatenate([halo[n].reshape(16, 512) for n in range(S)], axis=0)
     separate(rows, split, xh_ref, 16, 0, S)
     taps_b, taps_c = taps_of(w2, 1), taps_of(w2, 2)
-    for q in range(4):
+    for q in range(MANY):
         cols = slice(q * CHUNK, (q + 1) * CHUNK)
         for s in range(2):
             h = mm(w, x4[s * 128 : s * 128 + 192, cols]) + mm(
                 wh, xh_ref[s * 32 : s * 32 + 48, cols]
             )
             store_plane(h, s, cols, a1_ref, slope_ref)
+    for q in range(MANY):
+        cols = slice(q * CHUNK, (q + 1) * CHUNK)
         part = mm(taps_b, a1_ref[:, cols], TN) + mm(taps_c, a1c[:, cols], TN)
         part_ref[:, cols] = part
         back_ref[:, cols] = part.astype(BF)
 
 
 def between_kernel(part, away, wd1, w2, next2_ref, wd1_ref, block_ref, wide_ref):
-    for q in range(4):
+    for q in range(MANY):
         cols = slice(q * CHUNK, (q + 1) * CHUNK)
         h2 = part[:, cols].astype(F32) + away[:, cols].astype(F32)
         next2_ref[:, cols] = slope(h2, jnp.tanh(h2)).astype(BF)
@@ -215,14 +222,14 @@
 
 def third_kernel(part, got, slope2_ref, pay_ref, fown_ref):
     total = jnp.zeros((S, 64), F32)
-    for q in range(4):
+    for q in range(MANY):
         cols = slice(q * CHUNK, (q + 1) * CHUNK)
         h2 = part[:, cols] + got[:, cols].astype(F32)
         t = jnp.tanh(h2)
         act2 = leaky(h2, t).astype(BF)
         slope2_ref[:, cols] = slope(h2, t).astype(BF)
         rows = lax.broadcasted_iota(jnp.int32, (S, CHUNK), 0)
-        owner = lax.shift_right_logical(lane_ids((S, CHUNK)), 7) + 4 * q
+        owner = lax.shift_right_logical(lane_ids((S, CHUNK)), 7) + PER * q
         pick = jnp.where(rows == owner, 1.0, 0.0).astype(BF)
         total = total + mm(pick, act2, NT)
     feats = total * (1.0 / 128.0)
@@ -329,10 +336,10 @@
 ):
     x4, a1c = parts(first_ref, *OWN)
     gf = gf_ref[...].astype(BF).astype(F32) * (1.0 / 128.0)
-    for q in range(4):
+    for q in range(MANY):
         cols = slice(q * CHUNK, (q + 1) * CHUNK)
         spread = jnp.concatenate(
-            [jnp.broadcast_to(gf[:, 4 * q + n : 4 * q + n + 1], (128, LANES)) for n in range(4)],
+            [jnp.broadcast_to(gf[:, PER * q + n : PER * q + n + 1], (128, LANES)) for n in range(PER)],
             axis=1,
         )
         go = spread[0:64] * slope2[:, cols].astype(F32)
@@ -350,11 +357,19 @@
                     gact[r : r + 64] * s1[s * 64 : (s + 1) * 64, cols].astype(F32)
                 ).astype(BF)
     xh, a1b = parts(near, *NEAR)[:2]
-    w_ref[0:192] = mm(a1c[...], g_ref[0:128, :], NT)
-    a1 = mm(a1b[...], g_ref[0:64, :], NT)
-    w_ref[192:288] = jnp.concatenate([a1[0:96], a1[96:192]], axis=1)
-    r_ref[...] = mm(x4[0:192, :], h_ref[0], NT) + mm(x4[128:320, :], h_ref[1], NT)
-    rh_ref[...] = mm(xh[0:48, :], h_ref[0], NT) + mm(xh[32:80, :], h_ref[1], NT)
+    both = mm(jnp.concatenate([a1c[...], a1b[...]], axis=0), g_ref[0:128, :], NT)
+    w_ref[0:192] = both[0:192]
+    w_ref[192:288] = jnp.concatenate([both[192:288, 0:64], both[288:384, 0:64]], axis=1)
+    bands_of = [
+        mm(
+            jnp.concatenate([x4[128 * s : 128 * s + 192, :], xh[32 * s : 32 * s + 48, :]], axis=0),
+            h_ref[s],
+            NT,
+        )
+        for s in range(2)
+    ]
+    r_ref[...] = bands_of[0][0:192] + bands_of[1][0:192]
+    rh_ref[...] = bands_of[0][192:240] + bands_of[1][192:240]
     sums = tap_sums(r_ref, rh_ref)
     group = lax.shift_right_logical(lane_ids((12, LANES)), 5)
     w_ref[288:384] = jnp.zeros((96, LANES), F32)

time: 82.8 us -> 81.6 us (0.986)
  Pallas kernels: 12.9 us -> 11.2 us
    pallas_call x10, Pallas kernels: 12.9 us -> 11.2 us  [call(): pl.pallas_call(kernel, out_shape=[jax.ShapeDtypeStruct(s, d) for s, d in...]
  transfers between devices with their start and end apart: 5 -> 5, of which waited for: 2 -> 2; matrix products, arithmetic and copies ran while one was open for 0% -> 0% of each run, Pallas kernels for 8% -> 7%
where the time goes in v6:
time: 81.6 us; the launch traced here: 81.2 us
  blocking collectives  32.8 us (40%)
  starting transfers between devices  24.8 us (30%)
  Pallas kernels  11.2 us (14%)
  waiting for transfers between devices  9.83 us (12%)
  local copies, waits for them, and re-layouts  1.64 us (2%)
  between operations  0.9 us (1%)
    all_to_all x1, starting transfers between devices, local(): gathered = lax.all_to_all(pay, SLABS, 0, 0, tiled=True)  12.8 us
    all_to_all x1, blocking collectives, local(): over_group = lax.all_to_all(scattered, (*DP, 'core'), 0, 0, tiled=True)  12.2 us
    all_to_all x1, blocking collectives, local(): over_column = lax.all_to_all(to_column, COLUMN, 0, 0, tiled=True)  11.6 us
    pallas_call x10, Pallas kernels, call(): pl.pallas_call(kernel, out_shape=[jax.ShapeDtypeStruct(s, d) for s, d in...  11.2 us
    all_to_all x1, blocking collectives, local(): summed = lax.all_to_all(back, DP, 0, 0, tiled=True)  8.98 us
    all_to_all x1, waiting for transfers between devices, local(): gathered = lax.all_to_all(pay, SLABS, 0, 0, tiled=True)  8.57 us
    ppermute x1, starting transfers between devices, local(): halo = lax.ppermute(volumes[:, :, 3], SLABS, forward)  5.07 us
    ppermute x1, starting transfers between devices, local(): other = lax.ppermute(summed, 'core', swap)  2.66 us
  transfers between devices with their start and end apart: 5, of which 2 were waited for; matrix products, arithmetic and copies ran while one was open for 0% of the time, Pallas kernels for 7%

profile of v6, /device:TPU:1, one launch (start us, length us, event | category | flops | bytes accessed | tf_op | source)
XLA Modules:
  0.0 81.2 jit_solution(12054908324250414155)
XLA Ops:
  0.6 1.1 %slice_bitcast_fusion = bf16[16,4,4,512]{3,2,1,0:T(4,128)(2,1)S(1)} fusion(bf16[16,4,4,4,512]{4,3,2,1,0:T(4,128)(2,1)} %v.1), kind=kLoop, calls=%fused_computation | loop fusion | bytes 524288 | tf_op jit(solution)/shard_map/squeeze | solution.py:480
  1.7 0.0 copy-start.1
  1.7 0.0 copy-start.2
  1.7 0.0 copy-start.3
  1.7 5.1 %collective-permute-start = (bf16[16,4,4,512]{3,2,1,0:T(4,128)(2,1)S(1)}, bf16[16,4,4,512]{3,2,1,0:T(4,128)(2,1)S(1)}, u32[]{:S(2)}, u32[]{:S(2)}) collective-permute-start(bf16[16,4,4,512]{3,2,1,0:T(4,128)(2,1)S(1)} %slice_bitcast_fusion), channel_id=1, source_target_pairs={{0,1},{1,2},{2,3},{3,4},{4,5},{5,6},{6,7},{7,8},{8,9},{9,10},{10,1... | collective-permute-start | bytes 786440 | tf_op jit(solution)/shard_map/ppermute | solution.py:480
  6.8 0.2 shard_map.127
  7.1 0.0 copy-done.1
  7.1 0.0 copy-done.2
  7.1 0.0 copy-done.3
  7.1 1.9 %shard_map.128 = (bf16[512,2048]{1,0:T(8,128)(2,1)S(1)}, bf16[128,2048]{1,0:T(8,128)(2,1)S(1)}, bf16[64,2048]{1,0:T(8,128)(2,1)S(1)}) custom-call(bf16[16,4,4,4,512]{4,3,2,1,0:T(4,128)(2,1)S(1)} %copy-done.2, bf16[27,4,32]{2,1,0:T(4,128)(2,1)S(1)} %bitcast.21, bf16[3,3,3,32,64]{4,3,2,1,0:T(8,128)(2,1)S(1)} %bitcast.18, ...), custom_call_target="tpu_custom_call" | custom-call | flops 1000000000 | bytes 2883584 | tf_op jit(solution)/shard_map/pallas_call | solution.py:72
  9.0 0.0 copy-start.8
  9.0 1.9 %collective-permute-start.1 = (bf16[64,2048]{1,0:T(8,128)(2,1)S(1)}, bf16[64,2048]{1,0:T(8,128)(2,1)S(1)}, u32[]{:S(2)}, u32[]{:S(2)}) collective-permute-start(bf16[64,2048]{1,0:T(8,128)(2,1)S(1)} %get-tuple-element.38.away), channel_id=1, source_target_pairs={{0,1},{1,2},{2,3},{3,4},{4,5},{5,6},{6,7},{7,8},{8,9},{9,10},{10,1... | collective-permute-start | bytes 786440 | tf_op jit(solution)/shard_map/ppermute | solution.py:487
  10.9 0.0 collective-permute-done.halo
  10.9 1.4 %shard_map.129 = (bf16[528,2048]{1,0:T(8,128)(2,1)S(1)}, f32[64,2048]{1,0:T(8,128)S(1)}, bf16[64,2048]{1,0:T(8,128)(2,1)S(1)}) custom-call(bf16[16,4,4,512]{3,2,1,0:T(4,128)(2,1)S(1)} %collective-permute-done.halo, bf16[512,640]{1,0:T(8,128)(2,1)S(1)} %get-tuple-element.32.split, bf16[27,4,32]{2,1,0:T(4,128)(2,1)S(1)} %bitcast.22, ...), custom_call_target="tpu_custom_call" | custom-call | flops 2000000000 | bytes 2949120 | tf_op jit(solution)/shard_map/pallas_call | solution.py:72
  12.4 0.0 copy-done.8
  12.4 0.0 copy-start.10
  12.4 2.4 %collective-permute-start.2 = (bf16[64,2048]{1,0:T(8,128)(2,1)S(1)}, bf16[64,2048]{1,0:T(8,128)(2,1)S(1)}, u32[]{:S(2)}, u32[]{:S(2)}) collective-permute-start(bf16[64,2048]{1,0:T(8,128)(2,1)S(1)} %get-tuple-element.40), channel_id=1, source_target_pairs={{1,0},{2,1},{3,2},{4,3},{5,4},{6,5},{7,6},{8,7},{9,8},{10,9},{11,1... | collective-permute-start | bytes 786440 | tf_op jit(solution)/shard_map/ppermute | solution.py:494
  14.8 0.0 collective-permute-done.1.got
  14.8 0.0 copy-start
  14.8 0.0 copy-start.4
  14.8 0.0 copy-start.5
  14.8 0.0 copy-start.6
  14.8 0.0 copy-start.7
  14.9 1.0 %shard_map.130 = (bf16[64,2048]{1,0:T(8,128)(2,1)S(1)}, bf16[32,8,128]{2,1,0:T(8,128)(2,1)}, bf16[16,128]{1,0:T(8,128)(2,1)S(1)}) custom-call(f32[64,2048]{1,0:T(8,128)S(1)} %get-tuple-element.37.part, bf16[64,2048]{1,0:T(8,128)(2,1)S(1)} %collective-permute-done.1.got), custom_call_target="tpu_custom_call" | custom-call | flops 3000000000 | bytes 331776 | tf_op jit(solution)/shard_map/pallas_call | solution.py:72
  15.9 0.0 copy-done.10
  15.9 12.8 %all-to-all-start = ((bf16[32,8,128]{2,1,0:T(8,128)(2,1)}), bf16[32,8,128]{2,1,0:T(8,128)(2,1)S(1)}, u32[]{:S(2)}, u32[]{:S(2)}) async-start(bf16[32,8,128]{2,1,0:T(8,128)(2,1)} %get-tuple-element.39), calls=%async_computation | async-start | bytes 131072 | tf_op jit(solution)/shard_map/all_to_all | solution.py:501
  28.7 0.0 collective-permute-done.2.part
  28.7 0.0 copy-done
  28.7 1.0 %shard_map.131 = (bf16[64,2048]{1,0:T(8,128)(2,1)S(1)}, bf16[2048,128]{1,0:T(8,128)(2,1)S(1)}, bf16[256,256]{1,0:T(8,128)(2,1)S(1)}) custom-call(bf16[64,2048]{1,0:T(8,128)(2,1)S(1)} %collective-permute-done.2.part, bf16[64,2048]{1,0:T(8,128)(2,1)S(1)} %get-tuple-element.38.away, bf16[2048,128]{1,0:T(8,128)(2,1)S(1)} %copy-done, ...), custom_call_target="tpu_custom_call" | custom-call | flops 100000000 | bytes 917504 | tf_op jit(solution)/shard_map/pallas_call | solution.py:72
  29.7 8.6 %all-to-all-done.g = bf16[32,8,128]{2,1,0:T(8,128)(2,1)S(1)} async-done(((bf16[32,8,128]{2,1,0:T(8,128)(2,1)}), bf16[32,8,128]{2,1,0:T(8,128)(2,1)S(1)}, u32[]{:S(2)}, u32[]{:S(2)}) %all-to-all-start) | async-done | bytes 65568 | tf_op jit(solution)/shard_map/all_to_all | solution.py:501
  38.3 0.0 copy-done.4
  38.3 0.0 copy-done.5
  38.3 0.0 copy-done.6
  38.3 0.0 copy-done.7
  38.3 0.0 copy-start.9
  38.3 0.0 copy-start.11
  38.3 1.7 %shard_map.132 = (f32[128,16]{1,0:T(8,128)S(1)}, f32[128,128]{1,0:T(8,128)S(1)}, f32[8,128]{1,0:T(8,128)S(1)}) custom-call(s32[32]{0:T(128)S(1)} %copy-done.7, s32[1]{0:T(128)} %bitcast.position, bf16[32,8,128]{2,1,0:T(8,128)(2,1)S(1)} %all-to-all-done.g, bf16[2048,128]{1,0:T(8,128)(2,1)S(1)} %get-tuple-element.41.wd1, bf16[64,128]{1,0:T(8,128)(2,1)S(1)} %bitcast.23, ...), custom_call_target="tpu_custom_call" | custom-call | flops 2000000000 | bytes 77824 | tf_op jit(solution)/shard_map/pallas_call | solution.py:72
  40.0 0.0 copy-done.9
  40.0 0.5 copy-done.11
  40.5 2.0 %shard_map.133 = bf16[16,48,128]{2,1,0:T(8,128)(2,1)S(1)} custom-call(f32[128,16]{1,0:T(8,128)S(1)} %get-tuple-element.43.gf_ref, f32[128,128]{1,0:T(8,128)S(1)} %get-tuple-element.44.mix, f32[8,128]{1,0:T(8,128)S(1)} %get-tuple-element.45.small, bf16[512,2048]{1,0:T(8,128)(2,1)S(1)} %copy-done.9, bf16[256,256]{1,0:T(8,128)(2,1)S(1)} %get-tuple-element.46.block, ...), custom_call_target="tpu_custom_call" | custom-call | flops 2000000000 | bytes 196608 | tf_op jit(solution)/shard_map/pallas_call | solution.py:72
  42.5 12.2 %all_to_all.20.got = bf16[16,48,128]{2,1,0:T(8,128)(2,1)S(1)} all-to-all(bf16[16,48,128]{2,1,0:T(8,128)(2,1)S(1)} %shard_map.133), channel_id=1, replica_groups=mesh['x'=4,'yl'=2,'yh'=2,'z'=8,'core'=2] {'x','yl','core'}, dimensions={0} | all-to-all | bytes 393216 | tf_op jit(solution)/shard_map/all_to_all | solution.py:528
  54.8 0.6 shard_map.134
  55.4 11.6 %all_to_all.21.got = bf16[16,32,128]{2,1,0:T(8,128)(2,1)S(1)} all-to-all(bf16[16,32,128]{2,1,0:T(8,128)(2,1)S(1)} %get-tuple-element.51), channel_id=1, replica_groups=mesh['x'=4,'yl'=2,'yh'=2,'z'=8,'core'=2] {'yh','z'}, dimensions={0} | all-to-all | bytes 262144 | tf_op jit(solution)/shard_map/all_to_all | solution.py:534
  67.0 9.0 %all_to_all.22.mine = bf16[8,160,128]{2,1,0:T(8,128)(2,1)S(1)} all-to-all(bf16[8,160,128]{2,1,0:T(8,128)(2,1)S(1)} %shard_map.135), channel_id=1, replica_groups=mesh['x'=4,'yl'=2,'yh'=2,'z'=8,'core'=2] {'x','yl'}, dimensions={0} | all-to-all | bytes 655360 | tf_op jit(solution)/shard_map/all_to_all | solution.py:538
  76.0 2.7 %collective-permute-start.3 = (bf16[8,160,128]{2,1,0:T(8,128)(2,1)S(1)}, bf16[8,160,128]{2,1,0:T(8,128)(2,1)S(1)}, u32[]{:S(2)}, u32[]{:S(2)}) collective-permute-start(bf16[8,160,128]{2,1,0:T(8,128)(2,1)S(1)} %all_to_all.22.mine), channel_id=1, source_target_pairs={{0,1},{1,0},{2,3},{3,2},{4,5},{5,4},{6,7},{7,6},{8,9},{9,8},{10,11... | collective-permute-start | bytes 983048 | tf_op jit(solution)/shard_map/ppermute | solution.py:539
  78.7 1.3 %collective-permute-done.3.other = bf16[8,160,128]{2,1,0:T(8,128)(2,1)S(1)} collective-permute-done((bf16[8,160,128]{2,1,0:T(8,128)(2,1)S(1)}, bf16[8,160,128]{2,1,0:T(8,128)(2,1)S(1)}, u32[]{:S(2)}, u32[]{:S(2)}) %collective-permute-start.3) | collective-permute-done | bytes 327712 | tf_op jit(solution)/shard_map/ppermute | solution.py:539
  79.9 1.3 %shard_map.136 = (f32[3,3,3,4,32]{4,3,2,1,0:T(4,128)}, f32[3,3,3,32,64]{4,3,2,1,0:T(8,128)}, f32[2048,128]{1,0:T(8,128)}, f32[64,128]{1,0:T(8,128)}) custom-call(s32[1]{0:T(128)} %bitcast.10.core, bf16[8,160,128]{2,1,0:T(8,128)(2,1)S(1)} %all_to_all.22.mine, bf16[8,160,128]{2,1,0:T(8,128)(2,1)S(1)} %collective-permute-done.3.other), custom_call_target="tpu_custom_call" | custom-call | flops 100000000 | bytes 1316352 | tf_op jit(solution)/shard_map/pallas_call | solution.py:72
  (1 shorter events, 0.0 us)
Async XLA Ops:
  1.7 5.4 %copy-start.1 = (bf16[3,3,3,64,32]{3,4,2,1,0:T(8,128)(2,1)S(1)}, bf16[3,3,3,64,32]{3,4,2,1,0:T(8,128)(2,1)}, u32[]{:S(2)}) copy-start(bf16[3,3,3,64,32]{3,4,2,1,0:T(8,128)(2,1)} %param.12) | copy-start | bytes 331780
  1.7 5.4 %copy-start.2 = (bf16[16,4,4,4,512]{4,3,2,1,0:T(4,128)(2,1)S(1)}, bf16[16,4,4,4,512]{4,3,2,1,0:T(4,128)(2,1)}, u32[]{:S(2)}) copy-start(bf16[16,4,4,4,512]{4,3,2,1,0:T(4,128)(2,1)} %v.1) | copy-start | bytes 3145732
  1.7 5.4 %copy-start.3 = (bf16[3,3,3,32,4]{3,4,2,1,0:T(4,128)(2,1)S(1)}, bf16[3,3,3,32,4]{3,4,2,1,0:T(4,128)(2,1)}, u32[]{:S(2)}) copy-start(bf16[3,3,3,32,4]{3,4,2,1,0:T(4,128)(2,1)} %param.11) | copy-start | bytes 20740
  1.7 9.2 %collective-permute-start = (bf16[16,4,4,512]{3,2,1,0:T(4,128)(2,1)S(1)}, bf16[16,4,4,512]{3,2,1,0:T(4,128)(2,1)S(1)}, u32[]{:S(2)}, u32[]{:S(2)}) collective-permute-start(bf16[16,4,4,512]{3,2,1,0:T(4,128)(2,1)S(1)} %slice_bitcast_fusion), channel_id=1, source_target_pairs={{0,1},{1,2},{2,3},{3,4},{4,5},{5,6},{6,7},{7,8},{8,9},{9,10},{10,1... | collective-permute-start | bytes 786440 | tf_op jit(solution)/shard_map/ppermute | solution.py:480
  9.0 3.4 %copy-start.8 = (bf16[512,2048]{1,0:T(8,128)(2,1)}, bf16[512,2048]{1,0:T(8,128)(2,1)S(1)}, u32[]{:S(2)}) copy-start(bf16[512,2048]{1,0:T(8,128)(2,1)S(1)} %get-tuple-element.35.first_ref) | copy-start | bytes 6291460
  9.0 5.8 %collective-permute-start.1 = (bf16[64,2048]{1,0:T(8,128)(2,1)S(1)}, bf16[64,2048]{1,0:T(8,128)(2,1)S(1)}, u32[]{:S(2)}, u32[]{:S(2)}) collective-permute-start(bf16[64,2048]{1,0:T(8,128)(2,1)S(1)} %get-tuple-element.38.away), channel_id=1, source_target_pairs={{0,1},{1,2},{2,3},{3,4},{4,5},{5,6},{6,7},{7,8},{8,9},{9,10},{10,1... | collective-permute-start | bytes 786440 | tf_op jit(solution)/shard_map/ppermute | solution.py:487
  12.4 3.5 %copy-start.10 = (bf16[528,2048]{1,0:T(8,128)(2,1)}, bf16[528,2048]{1,0:T(8,128)(2,1)S(1)}, u32[]{:S(2)}) copy-start(bf16[528,2048]{1,0:T(8,128)(2,1)S(1)} %get-tuple-element.49.near) | copy-start | bytes 6488068
  12.4 16.3 %collective-permute-start.2 = (bf16[64,2048]{1,0:T(8,128)(2,1)S(1)}, bf16[64,2048]{1,0:T(8,128)(2,1)S(1)}, u32[]{:S(2)}, u32[]{:S(2)}) collective-permute-start(bf16[64,2048]{1,0:T(8,128)(2,1)S(1)} %get-tuple-element.40), channel_id=1, source_target_pairs={{1,0},{2,1},{3,2},{4,3},{5,4},{6,5},{7,6},{8,7},{9,8},{10,9},{11,1... | collective-permute-start | bytes 786440 | tf_op jit(solution)/shard_map/ppermute | solution.py:494
  14.8 13.9 %copy-start = (bf16[2048,128]{1,0:T(8,128)(2,1)S(1)}, bf16[2048,128]{1,0:T(8,128)(2,1)}, u32[]{:S(2)}) copy-start(bf16[2048,128]{1,0:T(8,128)(2,1)} %wd1.1) | copy-start | bytes 1572868
  14.8 23.5 %copy-start.4 = (bf16[128,64]{0,1:T(8,128)(2,1)S(1)}, bf16[128,64]{0,1:T(8,128)(2,1)}, u32[]{:S(2)}) copy-start(bf16[128,64]{0,1:T(8,128)(2,1)} %param.14) | copy-start | bytes 49156
  14.8 23.4 %copy-start.5 = (f32[16,4]{0,1:T(4,128)S(1)}, f32[16,4]{0,1:T(4,128)}, u32[]{:S(2)}) copy-start(f32[16,4]{0,1:T(4,128)} %param.9) | copy-start | bytes 772
  14.8 23.4 %copy-start.6 = (bf16[64,4]{0,1:T(4,128)(2,1)S(1)}, bf16[64,4]{0,1:T(4,128)(2,1)}, u32[]{:S(2)}) copy-start(bf16[64,4]{0,1:T(4,128)(2,1)} %param.15) | copy-start | bytes 1540
  14.8 23.4 %copy-start.7 = (s32[32]{0:T(128)S(1)}, s32[32]{0:T(128)}, u32[]{:S(2)}) copy-start(s32[32]{0:T(128)} %counts.1) | copy-start | bytes 388
  15.9 22.4 %all-to-all-start = ((bf16[32,8,128]{2,1,0:T(8,128)(2,1)}), bf16[32,8,128]{2,1,0:T(8,128)(2,1)S(1)}, u32[]{:S(2)}, u32[]{:S(2)}) async-start(bf16[32,8,128]{2,1,0:T(8,128)(2,1)} %get-tuple-element.39), calls=%async_computation | async-start | bytes 131072 | tf_op jit(solution)/shard_map/all_to_all | solution.py:501
  38.3 1.7 %copy-start.9 = (bf16[512,2048]{1,0:T(8,128)(2,1)S(1)}, bf16[512,2048]{1,0:T(8,128)(2,1)}, u32[]{:S(2)}) copy-start(bf16[512,2048]{1,0:T(8,128)(2,1)} %copy-done.8) | copy-start | bytes 6291460
  38.3 2.2 %copy-start.11 = (bf16[528,2048]{1,0:T(8,128)(2,1)S(1)}, bf16[528,2048]{1,0:T(8,128)(2,1)}, u32[]{:S(2)}) copy-start(bf16[528,2048]{1,0:T(8,128)(2,1)} %copy-done.10) | copy-start | bytes 6488068
  76.0 3.9 %collective-permute-start.3 = (bf16[8,160,128]{2,1,0:T(8,128)(2,1)S(1)}, bf16[8,160,128]{2,1,0:T(8,128)(2,1)S(1)}, u32[]{:S(2)}, u32[]{:S(2)}) collective-permute-start(bf16[8,160,128]{2,1,0:T(8,128)(2,1)S(1)} %all_to_all.22.mine), channel_id=1, source_target_pairs={{0,1},{1,0},{2,3},{3,2},{4,5},{5,4},{6,7},{7,6},{8,9},{9,8},{10,11... | collective-permute-start | bytes 983048 | tf_op jit(solution)/shard_map/ppermute | solution.py:539

commit v7 on v6

--- a/solution.py
+++ b/solution.py
@@ -425,15 +425,23 @@
         out_ref[k] = pay
 
 
-def last_kernel(core, mine, other, gw1_ref, gw2_ref, gd1_ref, gd2_ref, w_ref, t_ref):
+def order_kernel(mine, out_ref, t_ref):
+    for k in range(8):
+        t_ref[k] = mine[k, 32:160].astype(F32)
+        for r in range(4):
+            out_ref[k, r * 32 : (r + 1) * 32] = t_ref[k, pl.ds(r, 32, stride=4), :]
+
+
+def last_kernel(core, ordered, mine, other, gw1_ref, gw2_ref, gd1_ref, gd2_ref, w_ref, t_ref):
     first = core[0] == 0
     for k in range(8):
-        for n, chunk in enumerate((mine, other)):
-            t_ref[2 * k + n] = chunk[k, 32:160].astype(F32)
-            base = k * 256 + jnp.bitwise_xor(core[0], n) * 128
-            for r in range(4):
-                at = pl.multiple_of(base + r * 32, 32)
-                gd1_ref[pl.ds(at, 32), :] = t_ref[2 * k + n, pl.ds(r, 32, stride=4), :]
+        at = pl.multiple_of(k * 256 + core[0] * 128, 128)
+        gd1_ref[pl.ds(at, 128), :] = ordered[k]
+        t_ref[k] = other[k, 32:160].astype(F32)
+        base = k * 256 + (1 - core[0]) * 128
+        for r in range(4):
+            at = pl.multiple_of(base + r * 32, 32)
+            gd1_ref[pl.ds(at, 32), :] = t_ref[k, pl.ds(r, 32, stride=4), :]
         a, b = mine[k, 0:32].astype(F32), other[k, 0:32].astype(F32)
         low, high = jnp.where(first, a, b), jnp.where(first, b, a)
         w_ref[2 * k * PART : (2 * k + 1) * PART] = low[0:PART]
@@ -537,15 +545,21 @@
     )
     summed = lax.all_to_all(back, DP, 0, 0, tiled=True)
     other = lax.ppermute(summed, "core", swap)
+    (ordered,) = call(
+        order_kernel,
+        [((8, LANES, LANES), F32)],
+        (summed,),
+        scratch=[pltpu.VMEM((8, LANES, LANES), F32)],
+    )
     gw1, gw2, gd1, gd2 = call(
         last_kernel,
         [
             ((3, 3, 3, 4, 32), F32), ((3, 3, 3, 32, 64), F32),
             ((2048, LANES), F32), ((64, LANES), F32),
         ],
-        (summed, other),
+        (ordered, summed, other),
         scalars=(core,),
-        scratch=[pltpu.VMEM((16 * PART, LANES), F32), pltpu.VMEM((16, LANES, LANES), F32)],
+        scratch=[pltpu.VMEM((16 * PART, LANES), F32), pltpu.VMEM((8, LANES, LANES), F32)],
     )
     return (
         loss.reshape(()), jnp.swapaxes(gw1, 3, 4), jnp.swapaxes(gw2, 3, 4), gd1, gd2.T, d3.T,

time: 81.6 us -> 81.6 us (level)
    pallas_call x10 -> x11, Pallas kernels: 11.2 us -> 11.3 us  [call(): pl.pallas_call(kernel, out_shape=[jax.ShapeDtypeStruct(s, d) for s, d in...]
where the time goes in v7:
time: 81.6 us; the launch traced here: 81.2 us
  blocking collectives  32.8 us (40%)
  starting transfers between devices  24.8 us (30%)
  Pallas kernels  11.3 us (14%)
  waiting for transfers between devices  9.74 us (12%)
  local copies, waits for them, and re-layouts  1.64 us (2%)
  between operations  0.9 us (1%)
    all_to_all x1, starting transfers between devices, local(): gathered = lax.all_to_all(pay, SLABS, 0, 0, tiled=True)  12.8 us
    all_to_all x1, blocking collectives, local(): over_group = lax.all_to_all(scattered, (*DP, 'core'), 0, 0, tiled=True)  12.2 us
    all_to_all x1, blocking collectives, local(): over_column = lax.all_to_all(to_column, COLUMN, 0, 0, tiled=True)  11.6 us
    pallas_call x11, Pallas kernels, call(): pl.pallas_call(kernel, out_shape=[jax.ShapeDtypeStruct(s, d) for s, d in...  11.3 us
    all_to_all x1, blocking collectives, local(): summed = lax.all_to_all(back, DP, 0, 0, tiled=True)  8.98 us
    all_to_all x1, waiting for transfers between devices, local(): gathered = lax.all_to_all(pay, SLABS, 0, 0, tiled=True)  8.57 us
    ppermute x1, starting transfers between devices, local(): halo = lax.ppermute(volumes[:, :, 3], SLABS, forward)  5.07 us
    ppermute x1, starting transfers between devices, local(): other = lax.ppermute(summed, 'core', swap)  2.66 us
  transfers between devices with their start and end apart: 5, of which 2 were waited for; matrix products, arithmetic and copies ran while one was open for 0% of the time, Pallas kernels for 7%

profile of v7, /device:TPU:1, one launch (start us, length us, event | category | flops | bytes accessed | tf_op | source)
XLA Modules:
  0.0 81.2 jit_solution(3150439995710951573)
XLA Ops:
  0.6 1.1 %slice_bitcast_fusion = bf16[16,4,4,512]{3,2,1,0:T(4,128)(2,1)S(1)} fusion(bf16[16,4,4,4,512]{4,3,2,1,0:T(4,128)(2,1)} %v.1), kind=kLoop, calls=%fused_computation | loop fusion | bytes 524288 | tf_op jit(solution)/shard_map/squeeze | solution.py:488
  1.7 0.0 copy-start.1
  1.7 0.0 copy-start.2
  1.7 0.0 copy-start.3
  1.7 5.1 %collective-permute-start = (bf16[16,4,4,512]{3,2,1,0:T(4,128)(2,1)S(1)}, bf16[16,4,4,512]{3,2,1,0:T(4,128)(2,1)S(1)}, u32[]{:S(2)}, u32[]{:S(2)}) collective-permute-start(bf16[16,4,4,512]{3,2,1,0:T(4,128)(2,1)S(1)} %slice_bitcast_fusion), channel_id=1, source_target_pairs={{0,1},{1,2},{2,3},{3,4},{4,5},{5,6},{6,7},{7,8},{8,9},{9,10},{10,1... | collective-permute-start | bytes 786440 | tf_op jit(solution)/shard_map/ppermute | solution.py:488
  6.8 0.2 shard_map.127
  7.1 0.0 copy-done.1
  7.1 0.0 copy-done.2
  7.1 0.0 copy-done.3
  7.1 1.9 %shard_map.128 = (bf16[512,2048]{1,0:T(8,128)(2,1)S(1)}, bf16[128,2048]{1,0:T(8,128)(2,1)S(1)}, bf16[64,2048]{1,0:T(8,128)(2,1)S(1)}) custom-call(bf16[16,4,4,4,512]{4,3,2,1,0:T(4,128)(2,1)S(1)} %copy-done.2, bf16[27,4,32]{2,1,0:T(4,128)(2,1)S(1)} %bitcast.21, bf16[3,3,3,32,64]{4,3,2,1,0:T(8,128)(2,1)S(1)} %bitcast.18, ...), custom_call_target="tpu_custom_call" | custom-call | flops 1000000000 | bytes 2883584 | tf_op jit(solution)/shard_map/pallas_call | solution.py:72
  9.0 0.0 copy-start.8
  9.0 1.9 %collective-permute-start.1 = (bf16[64,2048]{1,0:T(8,128)(2,1)S(1)}, bf16[64,2048]{1,0:T(8,128)(2,1)S(1)}, u32[]{:S(2)}, u32[]{:S(2)}) collective-permute-start(bf16[64,2048]{1,0:T(8,128)(2,1)S(1)} %get-tuple-element.38.away), channel_id=1, source_target_pairs={{0,1},{1,2},{2,3},{3,4},{4,5},{5,6},{6,7},{7,8},{8,9},{9,10},{10,1... | collective-permute-start | bytes 786440 | tf_op jit(solution)/shard_map/ppermute | solution.py:495
  10.9 0.0 collective-permute-done.halo
  10.9 1.4 %shard_map.129 = (bf16[528,2048]{1,0:T(8,128)(2,1)S(1)}, f32[64,2048]{1,0:T(8,128)S(1)}, bf16[64,2048]{1,0:T(8,128)(2,1)S(1)}) custom-call(bf16[16,4,4,512]{3,2,1,0:T(4,128)(2,1)S(1)} %collective-permute-done.halo, bf16[512,640]{1,0:T(8,128)(2,1)S(1)} %get-tuple-element.32.split, bf16[27,4,32]{2,1,0:T(4,128)(2,1)S(1)} %bitcast.22, ...), custom_call_target="tpu_custom_call" | custom-call | flops 2000000000 | bytes 2949120 | tf_op jit(solution)/shard_map/pallas_call | solution.py:72
  12.4 0.0 copy-done.8
  12.4 0.0 copy-start.10
  12.4 2.4 %collective-permute-start.2 = (bf16[64,2048]{1,0:T(8,128)(2,1)S(1)}, bf16[64,2048]{1,0:T(8,128)(2,1)S(1)}, u32[]{:S(2)}, u32[]{:S(2)}) collective-permute-start(bf16[64,2048]{1,0:T(8,128)(2,1)S(1)} %get-tuple-element.40), channel_id=1, source_target_pairs={{1,0},{2,1},{3,2},{4,3},{5,4},{6,5},{7,6},{8,7},{9,8},{10,9},{11,1... | collective-permute-start | bytes 786440 | tf_op jit(solution)/shard_map/ppermute | solution.py:502
  14.8 0.0 collective-permute-done.1.got
  14.8 0.0 copy-start
  14.8 0.0 copy-start.4
  14.8 0.0 copy-start.5
  14.8 0.0 copy-start.6
  14.8 0.0 copy-start.7
  14.9 1.0 %shard_map.130 = (bf16[64,2048]{1,0:T(8,128)(2,1)S(1)}, bf16[32,8,128]{2,1,0:T(8,128)(2,1)}, bf16[16,128]{1,0:T(8,128)(2,1)S(1)}) custom-call(f32[64,2048]{1,0:T(8,128)S(1)} %get-tuple-element.37.part, bf16[64,2048]{1,0:T(8,128)(2,1)S(1)} %collective-permute-done.1.got), custom_call_target="tpu_custom_call" | custom-call | flops 3000000000 | bytes 331776 | tf_op jit(solution)/shard_map/pallas_call | solution.py:72
  15.9 0.0 copy-done.10
  15.9 12.8 %all-to-all-start = ((bf16[32,8,128]{2,1,0:T(8,128)(2,1)}), bf16[32,8,128]{2,1,0:T(8,128)(2,1)S(1)}, u32[]{:S(2)}, u32[]{:S(2)}) async-start(bf16[32,8,128]{2,1,0:T(8,128)(2,1)} %get-tuple-element.39), calls=%async_computation | async-start | bytes 131072 | tf_op jit(solution)/shard_map/all_to_all | solution.py:509
  28.7 0.0 collective-permute-done.2.part
  28.7 0.0 copy-done
  28.7 1.0 %shard_map.131 = (bf16[64,2048]{1,0:T(8,128)(2,1)S(1)}, bf16[2048,128]{1,0:T(8,128)(2,1)S(1)}, bf16[256,256]{1,0:T(8,128)(2,1)S(1)}) custom-call(bf16[64,2048]{1,0:T(8,128)(2,1)S(1)} %collective-permute-done.2.part, bf16[64,2048]{1,0:T(8,128)(2,1)S(1)} %get-tuple-element.38.away, bf16[2048,128]{1,0:T(8,128)(2,1)S(1)} %copy-done, ...), custom_call_target="tpu_custom_call" | custom-call | flops 100000000 | bytes 917504 | tf_op jit(solution)/shard_map/pallas_call | solution.py:72
  29.7 8.6 %all-to-all-done.g = bf16[32,8,128]{2,1,0:T(8,128)(2,1)S(1)} async-done(((bf16[32,8,128]{2,1,0:T(8,128)(2,1)}), bf16[32,8,128]{2,1,0:T(8,128)(2,1)S(1)}, u32[]{:S(2)}, u32[]{:S(2)}) %all-to-all-start) | async-done | bytes 65568 | tf_op jit(solution)/shard_map/all_to_all | solution.py:509
  38.3 0.0 copy-done.4
  38.3 0.0 copy-done.5
  38.3 0.0 copy-done.6
  38.3 0.0 copy-done.7
  38.3 0.0 copy-start.9
  38.3 0.0 copy-start.11
  38.3 1.7 %shard_map.132 = (f32[128,16]{1,0:T(8,128)S(1)}, f32[128,128]{1,0:T(8,128)S(1)}, f32[8,128]{1,0:T(8,128)S(1)}) custom-call(s32[32]{0:T(128)S(1)} %copy-done.7, s32[1]{0:T(128)} %bitcast.position, bf16[32,8,128]{2,1,0:T(8,128)(2,1)S(1)} %all-to-all-done.g, bf16[2048,128]{1,0:T(8,128)(2,1)S(1)} %get-tuple-element.41.wd1, bf16[64,128]{1,0:T(8,128)(2,1)S(1)} %bitcast.23, ...), custom_call_target="tpu_custom_call" | custom-call | flops 2000000000 | bytes 77824 | tf_op jit(solution)/shard_map/pallas_call | solution.py:72
  40.0 0.0 copy-done.9
  40.0 0.5 copy-done.11
  40.5 2.0 %shard_map.133 = bf16[16,48,128]{2,1,0:T(8,128)(2,1)S(1)} custom-call(f32[128,16]{1,0:T(8,128)S(1)} %get-tuple-element.43.gf_ref, f32[128,128]{1,0:T(8,128)S(1)} %get-tuple-element.44.mix, f32[8,128]{1,0:T(8,128)S(1)} %get-tuple-element.45.small, bf16[512,2048]{1,0:T(8,128)(2,1)S(1)} %copy-done.9, bf16[256,256]{1,0:T(8,128)(2,1)S(1)} %get-tuple-element.46.block, ...), custom_call_target="tpu_custom_call" | custom-call | flops 2000000000 | bytes 196608 | tf_op jit(solution)/shard_map/pallas_call | solution.py:72
  42.5 12.2 %all_to_all.20.got = bf16[16,48,128]{2,1,0:T(8,128)(2,1)S(1)} all-to-all(bf16[16,48,128]{2,1,0:T(8,128)(2,1)S(1)} %shard_map.133), channel_id=1, replica_groups=mesh['x'=4,'yl'=2,'yh'=2,'z'=8,'core'=2] {'x','yl','core'}, dimensions={0} | all-to-all | bytes 393216 | tf_op jit(solution)/shard_map/all_to_all | solution.py:536
  54.8 0.6 shard_map.134
  55.4 11.6 %all_to_all.21.got = bf16[16,32,128]{2,1,0:T(8,128)(2,1)S(1)} all-to-all(bf16[16,32,128]{2,1,0:T(8,128)(2,1)S(1)} %get-tuple-element.51), channel_id=1, replica_groups=mesh['x'=4,'yl'=2,'yh'=2,'z'=8,'core'=2] {'yh','z'}, dimensions={0} | all-to-all | bytes 262144 | tf_op jit(solution)/shard_map/all_to_all | solution.py:542
  67.0 9.0 %all_to_all.22.mine = bf16[8,160,128]{2,1,0:T(8,128)(2,1)S(1)} all-to-all(bf16[8,160,128]{2,1,0:T(8,128)(2,1)S(1)} %shard_map.135), channel_id=1, replica_groups=mesh['x'=4,'yl'=2,'yh'=2,'z'=8,'core'=2] {'x','yl'}, dimensions={0} | all-to-all | bytes 655360 | tf_op jit(solution)/shard_map/all_to_all | solution.py:546
  76.0 2.7 %collective-permute-start.3 = (bf16[8,160,128]{2,1,0:T(8,128)(2,1)S(1)}, bf16[8,160,128]{2,1,0:T(8,128)(2,1)S(1)}, u32[]{:S(2)}, u32[]{:S(2)}) collective-permute-start(bf16[8,160,128]{2,1,0:T(8,128)(2,1)S(1)} %all_to_all.22.mine), channel_id=1, source_target_pairs={{0,1},{1,0},{2,3},{3,2},{4,5},{5,4},{6,7},{7,6},{8,9},{9,8},{10,11... | collective-permute-start | bytes 983048 | tf_op jit(solution)/shard_map/ppermute | solution.py:547
  78.7 0.1 shard_map.136.ordered
  78.7 1.2 %collective-permute-done.3.other = bf16[8,160,128]{2,1,0:T(8,128)(2,1)S(1)} collective-permute-done((bf16[8,160,128]{2,1,0:T(8,128)(2,1)S(1)}, bf16[8,160,128]{2,1,0:T(8,128)(2,1)S(1)}, u32[]{:S(2)}, u32[]{:S(2)}) %collective-permute-start.3) | collective-permute-done | bytes 327712 | tf_op jit(solution)/shard_map/ppermute | solution.py:547
  79.9 1.3 %shard_map.137 = (f32[3,3,3,4,32]{4,3,2,1,0:T(4,128)}, f32[3,3,3,32,64]{4,3,2,1,0:T(8,128)}, f32[2048,128]{1,0:T(8,128)}, f32[64,128]{1,0:T(8,128)}) custom-call(s32[1]{0:T(128)} %bitcast.10.core, f32[8,128,128]{2,1,0:T(8,128)S(1)} %shard_map.136.ordered, bf16[8,160,128]{2,1,0:T(8,128)(2,1)S(1)} %all_to_all.22.mine, ...), custom_call_target="tpu_custom_call" | custom-call | flops 100000000 | bytes 1316352 | tf_op jit(solution)/shard_map/pallas_call | solution.py:72
  (1 shorter events, 0.0 us)
Async XLA Ops:
  1.7 5.4 %copy-start.1 = (bf16[3,3,3,64,32]{3,4,2,1,0:T(8,128)(2,1)S(1)}, bf16[3,3,3,64,32]{3,4,2,1,0:T(8,128)(2,1)}, u32[]{:S(2)}) copy-start(bf16[3,3,3,64,32]{3,4,2,1,0:T(8,128)(2,1)} %param.12) | copy-start | bytes 331780
  1.7 5.4 %copy-start.2 = (bf16[16,4,4,4,512]{4,3,2,1,0:T(4,128)(2,1)S(1)}, bf16[16,4,4,4,512]{4,3,2,1,0:T(4,128)(2,1)}, u32[]{:S(2)}) copy-start(bf16[16,4,4,4,512]{4,3,2,1,0:T(4,128)(2,1)} %v.1) | copy-start | bytes 3145732
  1.7 5.4 %copy-start.3 = (bf16[3,3,3,32,4]{3,4,2,1,0:T(4,128)(2,1)S(1)}, bf16[3,3,3,32,4]{3,4,2,1,0:T(4,128)(2,1)}, u32[]{:S(2)}) copy-start(bf16[3,3,3,32,4]{3,4,2,1,0:T(4,128)(2,1)} %param.11) | copy-start | bytes 20740
  1.7 9.2 %collective-permute-start = (bf16[16,4,4,512]{3,2,1,0:T(4,128)(2,1)S(1)}, bf16[16,4,4,512]{3,2,1,0:T(4,128)(2,1)S(1)}, u32[]{:S(2)}, u32[]{:S(2)}) collective-permute-start(bf16[16,4,4,512]{3,2,1,0:T(4,128)(2,1)S(1)} %slice_bitcast_fusion), channel_id=1, source_target_pairs={{0,1},{1,2},{2,3},{3,4},{4,5},{5,6},{6,7},{7,8},{8,9},{9,10},{10,1... | collective-permute-start | bytes 786440 | tf_op jit(solution)/shard_map/ppermute | solution.py:488
  9.0 3.4 %copy-start.8 = (bf16[512,2048]{1,0:T(8,128)(2,1)}, bf16[512,2048]{1,0:T(8,128)(2,1)S(1)}, u32[]{:S(2)}) copy-start(bf16[512,2048]{1,0:T(8,128)(2,1)S(1)} %get-tuple-element.35.first_ref) | copy-start | bytes 6291460
  9.0 5.8 %collective-permute-start.1 = (bf16[64,2048]{1,0:T(8,128)(2,1)S(1)}, bf16[64,2048]{1,0:T(8,128)(2,1)S(1)}, u32[]{:S(2)}, u32[]{:S(2)}) collective-permute-start(bf16[64,2048]{1,0:T(8,128)(2,1)S(1)} %get-tuple-element.38.away), channel_id=1, source_target_pairs={{0,1},{1,2},{2,3},{3,4},{4,5},{5,6},{6,7},{7,8},{8,9},{9,10},{10,1... | collective-permute-start | bytes 786440 | tf_op jit(solution)/shard_map/ppermute | solution.py:495
  12.4 3.5 %copy-start.10 = (bf16[528,2048]{1,0:T(8,128)(2,1)}, bf16[528,2048]{1,0:T(8,128)(2,1)S(1)}, u32[]{:S(2)}) copy-start(bf16[528,2048]{1,0:T(8,128)(2,1)S(1)} %get-tuple-element.49.near) | copy-start | bytes 6488068
  12.4 16.3 %collective-permute-start.2 = (bf16[64,2048]{1,0:T(8,128)(2,1)S(1)}, bf16[64,2048]{1,0:T(8,128)(2,1)S(1)}, u32[]{:S(2)}, u32[]{:S(2)}) collective-permute-start(bf16[64,2048]{1,0:T(8,128)(2,1)S(1)} %get-tuple-element.40), channel_id=1, source_target_pairs={{1,0},{2,1},{3,2},{4,3},{5,4},{6,5},{7,6},{8,7},{9,8},{10,9},{11,1... | collective-permute-start | bytes 786440 | tf_op jit(solution)/shard_map/ppermute | solution.py:502
  14.8 13.9 %copy-start = (bf16[2048,128]{1,0:T(8,128)(2,1)S(1)}, bf16[2048,128]{1,0:T(8,128)(2,1)}, u32[]{:S(2)}) copy-start(bf16[2048,128]{1,0:T(8,128)(2,1)} %wd1.1) | copy-start | bytes 1572868
  14.8 23.5 %copy-start.4 = (bf16[128,64]{0,1:T(8,128)(2,1)S(1)}, bf16[128,64]{0,1:T(8,128)(2,1)}, u32[]{:S(2)}) copy-start(bf16[128,64]{0,1:T(8,128)(2,1)} %param.14) | copy-start | bytes 49156
  14.8 23.4 %copy-start.5 = (f32[16,4]{0,1:T(4,128)S(1)}, f32[16,4]{0,1:T(4,128)}, u32[]{:S(2)}) copy-start(f32[16,4]{0,1:T(4,128)} %param.9) | copy-start | bytes 772
  14.8 23.4 %copy-start.6 = (bf16[64,4]{0,1:T(4,128)(2,1)S(1)}, bf16[64,4]{0,1:T(4,128)(2,1)}, u32[]{:S(2)}) copy-start(bf16[64,4]{0,1:T(4,128)(2,1)} %param.15) | copy-start | bytes 1540
  14.8 23.4 %copy-start.7 = (s32[32]{0:T(128)S(1)}, s32[32]{0:T(128)}, u32[]{:S(2)}) copy-start(s32[32]{0:T(128)} %counts.1) | copy-start | bytes 388
  15.9 22.4 %all-to-all-start = ((bf16[32,8,128]{2,1,0:T(8,128)(2,1)}), bf16[32,8,128]{2,1,0:T(8,128)(2,1)S(1)}, u32[]{:S(2)}, u32[]{:S(2)}) async-start(bf16[32,8,128]{2,1,0:T(8,128)(2,1)} %get-tuple-element.39), calls=%async_computation | async-start | bytes 131072 | tf_op jit(solution)/shard_map/all_to_all | solution.py:509
  38.3 1.7 %copy-start.9 = (bf16[512,2048]{1,0:T(8,128)(2,1)S(1)}, bf16[512,2048]{1,0:T(8,128)(2,1)}, u32[]{:S(2)}) copy-start(bf16[512,2048]{1,0:T(8,128)(2,1)} %copy-done.8) | copy-start | bytes 6291460
  38.3 2.2 %copy-start.11 = (bf16[528,2048]{1,0:T(8,128)(2,1)S(1)}, bf16[528,2048]{1,0:T(8,128)(2,1)}, u32[]{:S(2)}) copy-start(bf16[528,2048]{1,0:T(8,128)(2,1)} %copy-done.10) | copy-start | bytes 6488068
  76.0 3.9 %collective-permute-start.3 = (bf16[8,160,128]{2,1,0:T(8,128)(2,1)S(1)}, bf16[8,160,128]{2,1,0:T(8,128)(2,1)S(1)}, u32[]{:S(2)}, u32[]{:S(2)}) collective-permute-start(bf16[8,160,128]{2,1,0:T(8,128)(2,1)S(1)} %all_to_all.22.mine), channel_id=1, source_target_pairs={{0,1},{1,0},{2,3},{3,2},{4,5},{5,4},{6,7},{7,6},{8,9},{9,8},{10,11... | collective-permute-start | bytes 983048 | tf_op jit(solution)/shard_map/ppermute | solution.py:547
